TPU v7x, 1024 devices: a whole 4x8x16 slice. The times are simulated.
1024 devices in a mesh: wide: 64 (over z, x), narrow: 16 (over y, core).
Axes of the slice: x: 4, y: 8, z: 16, core: 2. Of those that a mesh axis runs over, the one named last changes fastest.
Arguments:
- amplitudes: float32 [960, 72000], P('narrow', 'wide'), may hold values from -6 to 6
- integrals: float32 [72000, 7680], P('wide', 'narrow'), may hold values from -0.0234375 to 0.0234375
- occupied_energy: float32 [60], replicated, may hold values from -3 to -1
- virtual_energy_rows: float32 [16], replicated, may hold values from 0.2 to 1.2
- virtual_energy_cols: float32 [128], replicated, may hold values from 0.2 to 1.2
Outputs:
- amplitude_step: float32 [960, 7680], P('wide', 'narrow')
All inputs are finite; a program needn't handle non-finite values.
Results may differ from a plain program's by a relative error of at most 0.00012.
Values sent between devices are 32-bit elements; how exact they have to be, the bound alone decides.
No kernel may reach another device: no remote copies, remote signals or barrier semaphores. Data moves between devices by JAX's collectives and lax.ppermute only.
A program may use at most 32 MiB of HBM per device.

v0:
```python
import jax
import jax.numpy as jnp
from jax import lax
from jax.sharding import PartitionSpec as P


def per_device(amplitudes, integrals, occupied_energy, virtual_energy_rows, virtual_energy_cols):
    partial_term = jnp.dot(
        lax.all_gather(amplitudes, "narrow", axis=0, tiled=True),
        integrals,
        precision=lax.Precision.HIGHEST,
        preferred_element_type=jnp.float32,
    )
    cycle_term = lax.psum_scatter(partial_term, "wide", scatter_dimension=0, tiled=True)
    row_count = cycle_term.shape[0]
    col_count = cycle_term.shape[1]
    row_first = lax.axis_index("wide") * row_count
    col_first = lax.axis_index("narrow") * col_count
    row_energy = (occupied_energy[None, :] - virtual_energy_rows[:, None]).reshape(-1)
    col_energy = (occupied_energy[None, :] - virtual_energy_cols[:, None]).reshape(-1)
    row_part = lax.dynamic_slice_in_dim(row_energy, row_first, row_count)
    col_part = lax.dynamic_slice_in_dim(col_energy, col_first, col_count)
    denominator = row_part[:, None] + col_part[None, :]
    return cycle_term / denominator


def solution(mesh):
    in_specs = (P("narrow", "wide"), P("wide", "narrow"), P(), P(), P())
    out_specs = P("wide", "narrow")
    return jax.shard_map(
        per_device, mesh=mesh, in_specs=in_specs, out_specs=out_specs, check_vma=False
    )
```

profile of v0, /device:TPU:68, one launch (start us, length us, event | category | flops | bytes accessed | tf_op | source)
XLA Modules:
  0.0 264.1 jit_solution(4652361662137021628)
XLA Ops:
  6.5 0.0 copy-start
  6.5 0.0 all-gather.3.cloned.1.call-start
  6.5 0.7 all-gather.3.cloned.1.call-update
  7.3 0.7 broadcast_subtract_fusion
  8.0 59.8 %all-gather.3.cloned.1.call-done = f32[16,60,1125]{2,1,0:T(8,128)} async-done(((f32[1,60,1125]{2,1,0:T(8,128)}), f32[16,60,1125]{2,1,0:T(8,128)}) %all-gather.3.cloned.1.call-update) | async-done | bytes 4320016 | tf_op jit(solution)/shard_map/all_gather | solution.py:9
  67.8 5.1 %reshape.14 = f32[960,1125]{1,0:T(8,128)} reshape(f32[16,60,1125]{2,1,0:T(8,128)} %all-gather.3.cloned.1.call-done) | data formatting | bytes 8640000
  72.9 0.0 copy-done
  72.9 0.0 copy-start.1
  72.9 0.0 copy-start.2
  72.9 10.8 %fusion.1 = f32[960,480]{1,0:T(8,128)} fusion(f32[960,1125]{1,0:T(8,128)} %reshape.14, f32[1125,480]{0,1:T(8,128)S(1)} %copy-done), kind=kOutput, calls=%fused_computation.3 | convolution fusion | flops 6220800000 | bytes 8323200 | tf_op jit(solution)/shard_map/dot_general | solution.py:8
  83.6 146.8 %fusion = f32[16,480]{1,0:T(8,128)S(1)} fusion(f32[960,480]{1,0:T(8,128)} %fusion.1), kind=kCustom, calls=%all-reduce-scatter | all-reduce-scatter fusion | flops 491521 | bytes 1878016
  230.5 1.9 collective-permute-start
  232.4 2.3 collective-permute-start.1
  234.7 9.2 %collective-permute-start.2 = (f32[16,480]{1,0:T(8,128)S(1)}, f32[16,480]{1,0:T(8,128)S(1)}, u32[]{:S(2)}, u32[]{:S(2)}) collective-permute-start(f32[16,480]{1,0:T(8,128)S(1)} %fusion), channel_id=1, source_target_pairs={{0,48},{16,64},{32,80},{48,96},{64,112},{80,128},{96,144},{112,160... | collective-permute-start | bytes 92168
  243.9 9.7 %collective-permute-start.3 = (f32[15,480]{1,0:T(8,128)S(1)}, f32[15,480]{1,0:T(8,128)S(1)}, u32[]{:S(2)}, u32[]{:S(2)}) collective-permute-start(f32[15,480]{1,0:T(8,128)S(1)} %slice), channel_id=1, source_target_pairs={{0,64},{16,80},{32,96},{48,112},{64,128},{80,144},{96,160},{112,17... | collective-permute-start | bytes 86408
  253.6 0.0 copy-done.1
  253.6 0.0 copy-done.2
  253.6 0.1 broadcast_subtract_fusion.1
  253.7 0.1 sub.41
  253.8 0.1 sub.37
  253.9 0.1 dynamic_slice.7
  254.0 0.1 dynamic_slice.6
  254.1 1.3 dynamic-slice.4
  256.0 0.0 collective-permute-done.3
  256.0 0.0 collective-permute-done
  256.0 0.0 collective-permute-done.1
  256.0 0.0 collective-permute-done.2
  256.0 0.5 concatenate
  256.5 0.7 dynamic-slice_divide_fusion
  (1 shorter events, 0.0 us)
Async XLA Ops:
  6.5 66.3 %copy-start = (f32[1125,480]{0,1:T(8,128)S(1)}, f32[1125,480]{0,1:T(8,128)}, u32[]{:S(2)}) copy-start(f32[1125,480]{0,1:T(8,128)} %param.6) | copy-start | bytes 6480004
  6.5 61.3 %all-gather.3.cloned.1.call-start = ((), (), s32[]{:S(2)}) async-start(), calls=%async_computation | async-start | bytes 5013504 | tf_op jit(solution)/shard_map/all_gather | solution.py:9
  72.9 180.8 %copy-start.1 = (f32[60]{0:T(128)S(1)}, f32[60]{0:T(128)}, u32[]{:S(2)}) copy-start(f32[60]{0:T(128)} %param.7) | copy-start | bytes 724
  72.9 180.8 %copy-start.2 = (f32[16]{0:T(128)S(1)}, f32[16]{0:T(128)}, u32[]{:S(2)}) copy-start(f32[16]{0:T(128)} %param.8) | copy-start | bytes 196
  230.5 25.5 %collective-permute-start = (f32[16,480]{1,0:T(8,128)S(1)}, f32[16,480]{1,0:T(8,128)S(1)}, u32[]{:S(2)}, u32[]{:S(2)}) collective-permute-start(f32[16,480]{1,0:T(8,128)S(1)} %fusion), channel_id=1, source_target_pairs={{0,16},{16,32},{32,48},{48,64},{64,80},{80,96},{96,112},{112,128},... | collective-permute-start | bytes 92168
  232.4 23.6 %collective-permute-start.1 = (f32[16,480]{1,0:T(8,128)S(1)}, f32[16,480]{1,0:T(8,128)S(1)}, u32[]{:S(2)}, u32[]{:S(2)}) collective-permute-start(f32[16,480]{1,0:T(8,128)S(1)} %fusion), channel_id=1, source_target_pairs={{0,32},{16,48},{32,64},{48,80},{64,96},{80,112},{96,128},{112,144}... | collective-permute-start | bytes 92168
  234.7 21.3 %collective-permute-start.2 = (f32[16,480]{1,0:T(8,128)S(1)}, f32[16,480]{1,0:T(8,128)S(1)}, u32[]{:S(2)}, u32[]{:S(2)}) collective-permute-start(f32[16,480]{1,0:T(8,128)S(1)} %fusion), channel_id=1, source_target_pairs={{0,48},{16,64},{32,80},{48,96},{64,112},{80,128},{96,144},{112,160... | collective-permute-start | bytes 92168
  243.9 12.1 %collective-permute-start.3 = (f32[15,480]{1,0:T(8,128)S(1)}, f32[15,480]{1,0:T(8,128)S(1)}, u32[]{:S(2)}, u32[]{:S(2)}) collective-permute-start(f32[15,480]{1,0:T(8,128)S(1)} %slice), channel_id=1, source_target_pairs={{0,64},{16,80},{32,96},{48,112},{64,128},{80,144},{96,160},{112,17... | collective-permute-start | bytes 86408
Sparse Core Ops, SparseCore 0:
  10.1 57.6 all-gather.2
where the time goes:
time: 264 us
  blocking collectives  147 us (56%)
  waiting for transfers between devices  60.5 us (23%)
  starting transfers between devices  23.1 us (9%)
  between operations  14.2 us (5%)
  matrix products  10.8 us (4%)
  local copies, waits for them, and re-layouts  7.18 us (3%)
    unnamed x1, blocking collectives  147 us
    all_gather x1, waiting for transfers between devices, per_device(): lax.all_gather(amplitudes, 'narrow', axis=0, tiled=True)  59.8 us
    unnamed x4, starting transfers between devices  23.1 us
    dot_general x1, matrix products, per_device(): jnp.dot(lax.all_gather(amplitudes, 'narrow', axis=0, tiled=True), integra...  10.8 us
    unnamed x10, local copies, waits for them, and re-layouts  6.85 us
  transfers between devices with their start and end apart: 5, of which 1 were waited for; matrix products, arithmetic and copies ran while one was open for 1% of the time, Pallas kernels for 0%

commit v1 on v0

v1 whole, which is shorter than its diff:
```python
import jax
import jax.numpy as jnp
from jax import lax
from jax.sharding import PartitionSpec as P

Z, X, Y, CORES = 16, 4, 8, 2
AXES = ("wide", "narrow")
OFFSETS = (0, 2, 1, 4, 3, 6, 5, 8)


def table(move):
    def index(z, x, y, c):
        return (z % Z * X + x % X) * (Y * CORES) + y % Y * CORES + c

    return [
        (index(z, x, y, c), index(*move(z, x, y, c)))
        for z in range(Z)
        for x in range(X)
        for y in range(Y)
        for c in range(CORES)
    ]


def send(array, move):
    return lax.ppermute(array, AXES, table(move))


def other_core(z, x, y, c):
    return z, x, y, 1 - c


def along_y(z, x, y, c):
    return z, x, y + (1 if c == 0 else -1), c


def along_x(step):
    return lambda z, x, y, c: (z, x + step, y, c)


def to_z(u, y, c):
    return 2 * y - u if c == 0 else 2 * y + 1 + u


def from_z(z, y, c):
    return (2 * y - z) % Z if c == 0 else (z - 2 * y - 1) % Z


def along_u(step):
    return lambda z, x, y, c: (to_z(from_z(z, y, c) + step, y, c), x, y, c)


def final(turn):
    def move(z, x, y, c):
        u = from_z(z, y, c)
        piece = (u // 4 + turn) % 4
        number = u % 4 * 4 + piece
        offset, half = OFFSETS[number // 2], number % 2
        return to_z(offset, y, c), x, y, c if half == 0 else 1 - c

    return move


def per_device(amplitudes, integrals, occupied_energy, virtual_energy_rows, virtual_energy_cols):
    wide, narrow = lax.axis_index("wide"), lax.axis_index("narrow")
    z, x, y, c = wide // X, wide % X, narrow // CORES, narrow % CORES
    u = jnp.where(c == 0, 2 * y - z, z - 2 * y - 1) % Z
    rows, depth = amplitudes.shape
    cols = integrals.shape[1]
    share = rows // X

    block = jnp.pad(amplitudes.reshape(X, share, depth), ((0, 0), (0, 16 - share), (0, 0)))
    block = jnp.roll(block, -x, axis=0).reshape(X * 16, depth)
    swapped = send(block, other_core)
    others = send(integrals, other_core)
    a1 = send(block, along_y)
    b1 = send(swapped, along_y)
    a2 = send(a1, along_y)
    b2 = send(b1, along_y)
    a3 = send(a2, along_y)
    b3 = send(b2, along_y)
    a4 = send(a3, along_y)

    def partial_sums(blocks):
        tall = jnp.concatenate(blocks, 0)
        halves = [
            jnp.dot(tall, part, precision=lax.Precision.HIGH, preferred_element_type=jnp.float32)
            for part in (integrals, others)
        ]
        return [half.reshape(len(blocks), X, 16, cols) for half in halves]

    def sum_over_x(blocks):
        halves = jnp.stack(partial_sums(blocks), 1)
        total = halves[:, :, 0]
        for place, step in ((1, 1), (3, -1), (2, 2)):
            total = total + send(halves[:, :, place], along_x(step))
        return total

    groups = ((block, a1, b1, a2, b2), (a3, b3, a4))
    pieces = jnp.concatenate([sum_over_x(blocks) for blocks in groups], 0).reshape(4, 4, 16, cols)

    mine = u % 4
    total = lax.dynamic_index_in_dim(pieces, mine, 0, keepdims=False)
    for step in (1, -1, 2):
        total = total + send(lax.dynamic_index_in_dim(pieces, (mine + step) % 4, 0, keepdims=False), along_u(step))
    cycle_term = None
    for turn in range(4):
        part = send(lax.dynamic_index_in_dim(total, (u // 4 + turn) % 4, 0, keepdims=False), final(turn))
        cycle_term = part if cycle_term is None else cycle_term + part
    cycle_term = cycle_term[:share]

    row_energy = (occupied_energy[None, :] - virtual_energy_rows[:, None]).reshape(-1)
    col_energy = (occupied_energy[None, :] - virtual_energy_cols[:, None]).reshape(-1)
    row_part = lax.dynamic_slice_in_dim(row_energy, wide * share, share)
    col_part = lax.dynamic_slice_in_dim(col_energy, narrow * cols, cols)
    return cycle_term / (row_part[:, None] + col_part[None, :])


def solution(mesh):
    in_specs = (P("narrow", "wide"), P("wide", "narrow"), P(), P(), P())
    out_specs = P("wide", "narrow")
    return jax.shard_map(
        per_device, mesh=mesh, in_specs=in_specs, out_specs=out_specs, check_vma=False
    )
```

time: 264 us -> 136 us (0.52)
  the two profiles are of different devices: /device:TPU:68 before, /device:TPU:38 now
where the time goes in v1:
time: 136 us; the launch traced here: 135 us
  starting transfers between devices  81.3 us (60%)
  waiting for transfers between devices  44.4 us (33%)
  matrix products  5.54 us (4%)
  local copies, waits for them, and re-layouts  1.72 us (1%)
  other arithmetic  1.37 us (1%)
    ppermute x22, starting transfers between devices, send(): return lax.ppermute(array, AXES, table(move))  81.3 us
    ppermute x22, waiting for transfers between devices, send(): return lax.ppermute(array, AXES, table(move))  44.4 us
    dot_general x4, matrix products, partial_sums(): jnp.dot(tall, part, precision=lax.Precision.HIGH, preferred_element_type=...  5.54 us
  transfers between devices with their start and end apart: 22, of which 13 were waited for; matrix products, arithmetic and copies ran while one was open for 4% of the time, Pallas kernels for 0%

profile of v1, /device:TPU:38, one launch (start us, length us, event | category | flops | bytes accessed | tf_op | source)
XLA Modules:
  0.0 135.1 jit_solution(5900231191481469595)
XLA Ops:
  0.0 1.0 reshape.22
  1.0 0.1 fusion.6
  1.1 0.0 copy-start
  1.1 2.1 %collective-permute-start.1 = (f32[64,1125]{1,0:T(8,128)S(1)}, f32[64,1125]{1,0:T(8,128)S(1)}, u32[]{:S(2)}, u32[]{:S(2)}) collective-permute-start(f32[64,1125]{1,0:T(8,128)S(1)} %bitcast.74), channel_id=1, source_target_pairs={{0,1},{1,0},{2,3},{3,2},{4,5},{5,4},{6,7},{7,6},{8,9},{9,8},{10,11... | collective-permute-start | bytes 864008 | tf_op jit(solution)/shard_map/ppermute | solution.py:25
  3.2 2.6 %collective-permute-start = (f32[64,1125]{1,0:T(8,128)S(1)}, f32[64,1125]{1,0:T(8,128)S(1)}, u32[]{:S(2)}, u32[]{:S(2)}) collective-permute-start(f32[64,1125]{1,0:T(8,128)S(1)} %bitcast.75), channel_id=1, source_target_pairs={{0,2},{1,15},{2,4},{3,1},{4,6},{5,3},{6,8},{7,5},{8,10},{9,7},{10,... | collective-permute-start | bytes 864008 | tf_op jit(solution)/shard_map/ppermute | solution.py:25
  5.8 1.9 %collective-permute-start.5 = (f32[1125,480]{0,1:T(8,128)}, f32[1125,480]{0,1:T(8,128)S(1)}, u32[]{:S(2)}, u32[]{:S(2)}) collective-permute-start(f32[1125,480]{0,1:T(8,128)} %param.6), channel_id=1, source_target_pairs={{0,1},{1,0},{2,3},{3,2},{4,5},{5,4},{6,7},{7,6},{8,9},{9,8},{10,11... | collective-permute-start | bytes 6480008 | tf_op jit(solution)/shard_map/ppermute | solution.py:25
  7.7 0.0 collective-permute-done.1
  7.7 3.5 %collective-permute-start.2 = (f32[64,1125]{1,0:T(8,128)S(1)}, f32[64,1125]{1,0:T(8,128)S(1)}, u32[]{:S(2)}, u32[]{:S(2)}) collective-permute-start(f32[64,1125]{1,0:T(8,128)S(1)} %collective-permute-done.1), channel_id=1, source_target_pairs={{0,2},{1,15},{2,4},{3,1},{4,6},{5,3},{6,8},{7,5},{8,10},{9,7},{10,... | collective-permute-start | bytes 864008 | tf_op jit(solution)/shard_map/ppermute | solution.py:25
  11.2 1.8 %collective-permute-done = f32[64,1125]{1,0:T(8,128)S(1)} collective-permute-done((f32[64,1125]{1,0:T(8,128)S(1)}, f32[64,1125]{1,0:T(8,128)S(1)}, u32[]{:S(2)}, u32[]{:S(2)}) %collective-permute-start) | collective-permute-done | bytes 288032 | tf_op jit(solution)/shard_map/ppermute | solution.py:25
  13.0 1.9 %collective-permute-start.3 = (f32[64,1125]{1,0:T(8,128)S(1)}, f32[64,1125]{1,0:T(8,128)S(1)}, u32[]{:S(2)}, u32[]{:S(2)}) collective-permute-start(f32[64,1125]{1,0:T(8,128)S(1)} %collective-permute-done), channel_id=1, source_target_pairs={{0,2},{1,15},{2,4},{3,1},{4,6},{5,3},{6,8},{7,5},{8,10},{9,7},{10,... | collective-permute-start | bytes 864008 | tf_op jit(solution)/shard_map/ppermute | solution.py:25
  15.0 2.6 %collective-permute-done.2 = f32[64,1125]{1,0:T(8,128)S(1)} collective-permute-done((f32[64,1125]{1,0:T(8,128)S(1)}, f32[64,1125]{1,0:T(8,128)S(1)}, u32[]{:S(2)}, u32[]{:S(2)}) %collective-permute-start.2) | collective-permute-done | bytes 288032 | tf_op jit(solution)/shard_map/ppermute | solution.py:25
  17.5 2.2 %collective-permute-start.4 = (f32[64,1125]{1,0:T(8,128)S(1)}, f32[64,1125]{1,0:T(8,128)S(1)}, u32[]{:S(2)}, u32[]{:S(2)}) collective-permute-start(f32[64,1125]{1,0:T(8,128)S(1)} %collective-permute-done.2), channel_id=1, source_target_pairs={{0,2},{1,15},{2,4},{3,1},{4,6},{5,3},{6,8},{7,5},{8,10},{9,7},{10,... | collective-permute-start | bytes 864008 | tf_op jit(solution)/shard_map/ppermute | solution.py:25
  19.8 3.0 %collective-permute-done.3 = f32[64,1125]{1,0:T(8,128)S(1)} collective-permute-done((f32[64,1125]{1,0:T(8,128)S(1)}, f32[64,1125]{1,0:T(8,128)S(1)}, u32[]{:S(2)}, u32[]{:S(2)}) %collective-permute-start.3) | collective-permute-done | bytes 288032 | tf_op jit(solution)/shard_map/ppermute | solution.py:25
  22.8 1.9 %collective-permute-start.9 = (f32[64,1125]{1,0:T(8,128)S(1)}, f32[64,1125]{1,0:T(8,128)S(1)}, u32[]{:S(2)}, u32[]{:S(2)}) collective-permute-start(f32[64,1125]{1,0:T(8,128)S(1)} %collective-permute-done.3), channel_id=1, source_target_pairs={{0,2},{1,15},{2,4},{3,1},{4,6},{5,3},{6,8},{7,5},{8,10},{9,7},{10,... | collective-permute-start | bytes 864008 | tf_op jit(solution)/shard_map/ppermute | solution.py:25
  24.8 2.6 %collective-permute-done.4 = f32[64,1125]{1,0:T(8,128)S(1)} collective-permute-done((f32[64,1125]{1,0:T(8,128)S(1)}, f32[64,1125]{1,0:T(8,128)S(1)}, u32[]{:S(2)}, u32[]{:S(2)}) %collective-permute-start.4) | collective-permute-done | bytes 288032 | tf_op jit(solution)/shard_map/ppermute | solution.py:25
  27.4 1.9 %collective-permute-start.10 = (f32[64,1125]{1,0:T(8,128)S(1)}, f32[64,1125]{1,0:T(8,128)S(1)}, u32[]{:S(2)}, u32[]{:S(2)}) collective-permute-start(f32[64,1125]{1,0:T(8,128)S(1)} %collective-permute-done.4), channel_id=1, source_target_pairs={{0,2},{1,15},{2,4},{3,1},{4,6},{5,3},{6,8},{7,5},{8,10},{9,7},{10,... | collective-permute-start | bytes 864008 | tf_op jit(solution)/shard_map/ppermute | solution.py:25
  29.3 0.0 copy-done
  29.3 1.6 %fusion.16 = f32[320,480]{1,0:T(8,128)S(1)} fusion(f32[320,1125]{1,0:T(8,128)S(1)} %constant_dynamic-update-slice_fusion, f32[1125,480]{0,1:T(8,128)S(1)} %copy-done), kind=kOutput, calls=%fused_computation.62 | convolution fusion | flops 1036800000 | bytes 4214400 | tf_op jit(solution)/shard_map/dot_general | solution.py:86
  30.9 1.8 %collective-permute-done.9 = f32[64,1125]{1,0:T(8,128)S(1)} collective-permute-done((f32[64,1125]{1,0:T(8,128)S(1)}, f32[64,1125]{1,0:T(8,128)S(1)}, u32[]{:S(2)}, u32[]{:S(2)}) %collective-permute-start.9) | collective-permute-done | bytes 288032 | tf_op jit(solution)/shard_map/ppermute | solution.py:25
  32.6 1.9 %collective-permute-start.11 = (f32[64,1125]{1,0:T(8,128)S(1)}, f32[64,1125]{1,0:T(8,128)S(1)}, u32[]{:S(2)}, u32[]{:S(2)}) collective-permute-start(f32[64,1125]{1,0:T(8,128)S(1)} %collective-permute-done.9), channel_id=1, source_target_pairs={{0,2},{1,15},{2,4},{3,1},{4,6},{5,3},{6,8},{7,5},{8,10},{9,7},{10,... | collective-permute-start | bytes 864008 | tf_op jit(solution)/shard_map/ppermute | solution.py:25
  34.6 2.6 %collective-permute-done.10 = f32[64,1125]{1,0:T(8,128)S(1)} collective-permute-done((f32[64,1125]{1,0:T(8,128)S(1)}, f32[64,1125]{1,0:T(8,128)S(1)}, u32[]{:S(2)}, u32[]{:S(2)}) %collective-permute-start.10) | collective-permute-done | bytes 288032 | tf_op jit(solution)/shard_map/ppermute | solution.py:25
  37.2 5.3 %collective-permute-done.11 = f32[64,1125]{1,0:T(8,128)S(1)} collective-permute-done((f32[64,1125]{1,0:T(8,128)S(1)}, f32[64,1125]{1,0:T(8,128)S(1)}, u32[]{:S(2)}, u32[]{:S(2)}) %collective-permute-start.11) | collective-permute-done | bytes 288032 | tf_op jit(solution)/shard_map/ppermute | solution.py:25
  42.5 1.2 fusion.18
  43.7 0.0 collective-permute-done.5
  43.7 1.2 fusion.19
  44.9 0.1 fusion.8
  45.0 7.3 %collective-permute-start.12 = (f32[3,2,16,480]{3,2,1,0:T(8,128)S(1)}, f32[3,2,16,480]{3,2,1,0:T(8,128)S(1)}, u32[]{:S(2)}, u32[]{:S(2)}) collective-permute-start(f32[3,2,16,480]{3,2,1,0:T(8,128)S(1)} %bitcast.82), channel_id=1, source_target_pairs={{0,16},{1,17},{2,18},{3,19},{4,20},{5,21},{6,22},{7,23},{8,24},{9,... | collective-permute-start | bytes 552968 | tf_op jit(solution)/shard_map/ppermute | solution.py:25
  52.4 1.9 %collective-permute-start.13 = (f32[3,2,16,480]{3,2,1,0:T(8,128)S(1)}, f32[3,2,16,480]{3,2,1,0:T(8,128)S(1)}, u32[]{:S(2)}, u32[]{:S(2)}) collective-permute-start(f32[3,2,16,480]{3,2,1,0:T(8,128)S(1)} %bitcast.80), channel_id=1, source_target_pairs={{0,48},{1,49},{2,50},{3,51},{4,52},{5,53},{6,54},{7,55},{8,56},{9,... | collective-permute-start | bytes 552968 | tf_op jit(solution)/shard_map/ppermute | solution.py:25
  54.3 3.4 %collective-permute-start.14 = (f32[3,2,16,480]{3,2,1,0:T(8,128)S(1)}, f32[3,2,16,480]{3,2,1,0:T(8,128)S(1)}, u32[]{:S(2)}, u32[]{:S(2)}) collective-permute-start(f32[3,2,16,480]{3,2,1,0:T(8,128)S(1)} %bitcast.81), channel_id=1, source_target_pairs={{0,32},{1,33},{2,34},{3,35},{4,36},{5,37},{6,38},{7,39},{8,40},{9,... | collective-permute-start | bytes 552968 | tf_op jit(solution)/shard_map/ppermute | solution.py:25
  57.7 1.6 %fusion.17 = f32[320,480]{1,0:T(8,128)S(1)} fusion(f32[320,1125]{1,0:T(8,128)S(1)} %constant_dynamic-update-slice_fusion, f32[1125,480]{0,1:T(8,128)S(1)} %collective-permute-done.5), kind=kOutput, calls=%fused_computation.63 | convolution fusion | flops 1036800000 | bytes 4214400 | tf_op jit(solution)/shard_map/dot_general | solution.py:86
  59.2 0.1 fusion.1
  59.4 3.7 %collective-permute-start.6 = (f32[5,2,16,480]{3,2,1,0:T(8,128)S(1)}, f32[5,2,16,480]{3,2,1,0:T(8,128)S(1)}, u32[]{:S(2)}, u32[]{:S(2)}) collective-permute-start(f32[5,2,16,480]{3,2,1,0:T(8,128)S(1)} %bitcast.77), channel_id=1, source_target_pairs={{0,16},{1,17},{2,18},{3,19},{4,20},{5,21},{6,22},{7,23},{8,24},{9,... | collective-permute-start | bytes 921608 | tf_op jit(solution)/shard_map/ppermute | solution.py:25
  63.2 2.8 %collective-permute-start.7 = (f32[5,2,16,480]{3,2,1,0:T(8,128)S(1)}, f32[5,2,16,480]{3,2,1,0:T(8,128)S(1)}, u32[]{:S(2)}, u32[]{:S(2)}) collective-permute-start(f32[5,2,16,480]{3,2,1,0:T(8,128)S(1)} %bitcast.78), channel_id=1, source_target_pairs={{0,48},{1,49},{2,50},{3,51},{4,52},{5,53},{6,54},{7,55},{8,56},{9,... | collective-permute-start | bytes 921608 | tf_op jit(solution)/shard_map/ppermute | solution.py:25
  66.0 0.0 collective-permute-done.12
  66.0 4.0 %collective-permute-start.8 = (f32[5,2,16,480]{3,2,1,0:T(8,128)S(1)}, f32[5,2,16,480]{3,2,1,0:T(8,128)S(1)}, u32[]{:S(2)}, u32[]{:S(2)}) collective-permute-start(f32[5,2,16,480]{3,2,1,0:T(8,128)S(1)} %bitcast.79), channel_id=1, source_target_pairs={{0,32},{1,33},{2,34},{3,35},{4,36},{5,37},{6,38},{7,39},{8,40},{9,... | collective-permute-start | bytes 921608 | tf_op jit(solution)/shard_map/ppermute | solution.py:25
  70.2 0.0 collective-permute-done.13
  70.2 0.0 collective-permute-done.14
  70.2 0.1 fusion.12
  70.3 2.7 %collective-permute-done.6 = f32[5,2,16,480]{3,2,1,0:T(8,128)S(1)} collective-permute-done((f32[5,2,16,480]{3,2,1,0:T(8,128)S(1)}, f32[5,2,16,480]{3,2,1,0:T(8,128)S(1)}, u32[]{:S(2)}, u32[]{:S(2)}) %collective-permute-start.6) | collective-permute-done | bytes 307232 | tf_op jit(solution)/shard_map/ppermute | solution.py:25
  73.0 6.5 %collective-permute-done.7 = f32[5,2,16,480]{3,2,1,0:T(8,128)S(1)} collective-permute-done((f32[5,2,16,480]{3,2,1,0:T(8,128)S(1)}, f32[5,2,16,480]{3,2,1,0:T(8,128)S(1)}, u32[]{:S(2)}, u32[]{:S(2)}) %collective-permute-start.7) | collective-permute-done | bytes 307232 | tf_op jit(solution)/shard_map/ppermute | solution.py:25
  79.4 0.0 collective-permute-done.8
  79.4 0.1 fusion.5
  79.6 0.0 copy-start.3
  79.7 13.8 %collective-permute-start.15 = (f32[4,16,480]{2,1,0:T(8,128)S(1)}, f32[4,16,480]{2,1,0:T(8,128)S(1)}, u32[]{:S(2)}, u32[]{:S(2)}) collective-permute-start(f32[4,16,480]{2,1,0:T(8,128)S(1)} %get-tuple-element.13), channel_id=1, source_target_pairs={{0,960},{1,65},{2,962},{3,67},{4,964},{5,69},{6,966},{7,71},{8,968... | collective-permute-start | bytes 368648 | tf_op jit(solution)/shard_map/ppermute | solution.py:25
  93.5 1.9 %collective-permute-start.16 = (f32[4,16,480]{2,1,0:T(8,128)S(1)}, f32[4,16,480]{2,1,0:T(8,128)S(1)}, u32[]{:S(2)}, u32[]{:S(2)}) collective-permute-start(f32[4,16,480]{2,1,0:T(8,128)S(1)} %get-tuple-element.15), channel_id=1, source_target_pairs={{0,64},{1,961},{2,66},{3,963},{4,68},{5,965},{6,70},{7,967},{8,72}... | collective-permute-start | bytes 368648 | tf_op jit(solution)/shard_map/ppermute | solution.py:25
  95.4 3.9 %collective-permute-start.17 = (f32[4,16,480]{2,1,0:T(8,128)S(1)}, f32[4,16,480]{2,1,0:T(8,128)S(1)}, u32[]{:S(2)}, u32[]{:S(2)}) collective-permute-start(f32[4,16,480]{2,1,0:T(8,128)S(1)} %get-tuple-element.14), channel_id=1, source_target_pairs={{0,896},{1,129},{2,898},{3,131},{4,900},{5,133},{6,902},{7,135},{8... | collective-permute-start | bytes 368648 | tf_op jit(solution)/shard_map/ppermute | solution.py:25
  99.4 0.1 broadcast_subtract_fusion
  99.5 0.0 collective-permute-done.15
  99.5 2.1 %collective-permute-done.16 = f32[4,16,480]{2,1,0:T(8,128)S(1)} collective-permute-done((f32[4,16,480]{2,1,0:T(8,128)S(1)}, f32[4,16,480]{2,1,0:T(8,128)S(1)}, u32[]{:S(2)}, u32[]{:S(2)}) %collective-permute-start.16) | collective-permute-done | bytes 122912 | tf_op jit(solution)/shard_map/ppermute | solution.py:25
  101.6 2.3 %collective-permute-done.17 = f32[4,16,480]{2,1,0:T(8,128)S(1)} collective-permute-done((f32[4,16,480]{2,1,0:T(8,128)S(1)}, f32[4,16,480]{2,1,0:T(8,128)S(1)}, u32[]{:S(2)}, u32[]{:S(2)}) %collective-permute-start.17) | collective-permute-done | bytes 122912 | tf_op jit(solution)/shard_map/ppermute | solution.py:25
  103.9 2.0 %collective-permute-start.18 = (f32[16,480]{1,0:T(8,128)S(1)}, f32[16,480]{1,0:T(8,128)S(1)}, u32[]{:S(2)}, u32[]{:S(2)}) collective-permute-start(f32[16,480]{1,0:T(8,128)S(1)} %get-tuple-element.16), channel_id=1, source_target_pairs={{0,0},{1,576},{2,962},{3,450},{4,261},{5,837},{6,199},{7,711},{8,3... | collective-permute-start | bytes 92168 | tf_op jit(solution)/shard_map/ppermute | solution.py:25
  106.0 9.8 %collective-permute-start.19 = (f32[16,480]{1,0:T(8,128)S(1)}, f32[16,480]{1,0:T(8,128)S(1)}, u32[]{:S(2)}, u32[]{:S(2)}) collective-permute-start(f32[16,480]{1,0:T(8,128)S(1)} %get-tuple-element.19), channel_id=1, source_target_pairs={{0,1},{1,385},{2,963},{3,259},{4,132},{5,836},{6,6},{7,710},{8,393... | collective-permute-start | bytes 92168 | tf_op jit(solution)/shard_map/ppermute | solution.py:25
  115.8 5.0 %collective-permute-start.20 = (f32[16,480]{1,0:T(8,128)S(1)}, f32[16,480]{1,0:T(8,128)S(1)}, u32[]{:S(2)}, u32[]{:S(2)}) collective-permute-start(f32[16,480]{1,0:T(8,128)S(1)} %get-tuple-element.18), channel_id=1, source_target_pairs={{0,896},{1,384},{2,770},{3,258},{4,133},{5,645},{6,7},{7,519},{8,5... | collective-permute-start | bytes 92168 | tf_op jit(solution)/shard_map/ppermute | solution.py:25
  120.8 1.9 %collective-permute-start.21 = (f32[16,480]{1,0:T(8,128)S(1)}, f32[16,480]{1,0:T(8,128)S(1)}, u32[]{:S(2)}, u32[]{:S(2)}) collective-permute-start(f32[16,480]{1,0:T(8,128)S(1)} %get-tuple-element.17), channel_id=1, source_target_pairs={{0,897},{1,577},{2,771},{3,451},{4,260},{5,644},{6,198},{7,518},{8... | collective-permute-start | bytes 92168 | tf_op jit(solution)/shard_map/ppermute | solution.py:25
  122.7 0.1 broadcast_subtract_fusion.1
  122.8 0.1 sub.74
  122.9 0.1 sub.70
  123.0 0.1 dynamic_slice.46
  123.0 0.1 dynamic_slice.45
  123.1 0.0 collective-permute-done.18
  123.1 0.0 collective-permute-done.19
  123.1 4.0 %collective-permute-done.20 = f32[16,480]{1,0:T(8,128)S(1)} collective-permute-done((f32[16,480]{1,0:T(8,128)S(1)}, f32[16,480]{1,0:T(8,128)S(1)}, u32[]{:S(2)}, u32[]{:S(2)}) %collective-permute-start.20) | collective-permute-done | bytes 30752 | tf_op jit(solution)/shard_map/ppermute | solution.py:25
  127.1 7.2 %collective-permute-done.21 = f32[16,480]{1,0:T(8,128)S(1)} collective-permute-done((f32[16,480]{1,0:T(8,128)S(1)}, f32[16,480]{1,0:T(8,128)S(1)}, u32[]{:S(2)}, u32[]{:S(2)}) %collective-permute-start.21) | collective-permute-done | bytes 30752 | tf_op jit(solution)/shard_map/ppermute | solution.py:25
  134.4 0.7 fusion.15
  (24 shorter events, 0.4 us)
Async XLA Ops:
  1.1 28.2 %copy-start = (f32[1125,480]{0,1:T(8,128)S(1)}, f32[1125,480]{0,1:T(8,128)}, u32[]{:S(2)}) copy-start(f32[1125,480]{0,1:T(8,128)} %param.6) | copy-start | bytes 6480004
  1.1 6.6 %collective-permute-start.1 = (f32[64,1125]{1,0:T(8,128)S(1)}, f32[64,1125]{1,0:T(8,128)S(1)}, u32[]{:S(2)}, u32[]{:S(2)}) collective-permute-start(f32[64,1125]{1,0:T(8,128)S(1)} %bitcast.74), channel_id=1, source_target_pairs={{0,1},{1,0},{2,3},{3,2},{4,5},{5,4},{6,7},{7,6},{8,9},{9,8},{10,11... | collective-permute-start | bytes 864008 | tf_op jit(solution)/shard_map/ppermute | solution.py:25
  3.2 9.8 %collective-permute-start = (f32[64,1125]{1,0:T(8,128)S(1)}, f32[64,1125]{1,0:T(8,128)S(1)}, u32[]{:S(2)}, u32[]{:S(2)}) collective-permute-start(f32[64,1125]{1,0:T(8,128)S(1)} %bitcast.75), channel_id=1, source_target_pairs={{0,2},{1,15},{2,4},{3,1},{4,6},{5,3},{6,8},{7,5},{8,10},{9,7},{10,... | collective-permute-start | bytes 864008 | tf_op jit(solution)/shard_map/ppermute | solution.py:25
  5.8 37.9 %collective-permute-start.5 = (f32[1125,480]{0,1:T(8,128)}, f32[1125,480]{0,1:T(8,128)S(1)}, u32[]{:S(2)}, u32[]{:S(2)}) collective-permute-start(f32[1125,480]{0,1:T(8,128)} %param.6), channel_id=1, source_target_pairs={{0,1},{1,0},{2,3},{3,2},{4,5},{5,4},{6,7},{7,6},{8,9},{9,8},{10,11... | collective-permute-start | bytes 6480008 | tf_op jit(solution)/shard_map/ppermute | solution.py:25
  7.7 9.8 %collective-permute-start.2 = (f32[64,1125]{1,0:T(8,128)S(1)}, f32[64,1125]{1,0:T(8,128)S(1)}, u32[]{:S(2)}, u32[]{:S(2)}) collective-permute-start(f32[64,1125]{1,0:T(8,128)S(1)} %collective-permute-done.1), channel_id=1, source_target_pairs={{0,2},{1,15},{2,4},{3,1},{4,6},{5,3},{6,8},{7,5},{8,10},{9,7},{10,... | collective-permute-start | bytes 864008 | tf_op jit(solution)/shard_map/ppermute | solution.py:25
  13.0 9.8 %collective-permute-start.3 = (f32[64,1125]{1,0:T(8,128)S(1)}, f32[64,1125]{1,0:T(8,128)S(1)}, u32[]{:S(2)}, u32[]{:S(2)}) collective-permute-start(f32[64,1125]{1,0:T(8,128)S(1)} %collective-permute-done), channel_id=1, source_target_pairs={{0,2},{1,15},{2,4},{3,1},{4,6},{5,3},{6,8},{7,5},{8,10},{9,7},{10,... | collective-permute-start | bytes 864008 | tf_op jit(solution)/shard_map/ppermute | solution.py:25
  17.5 9.8 %collective-permute-start.4 = (f32[64,1125]{1,0:T(8,128)S(1)}, f32[64,1125]{1,0:T(8,128)S(1)}, u32[]{:S(2)}, u32[]{:S(2)}) collective-permute-start(f32[64,1125]{1,0:T(8,128)S(1)} %collective-permute-done.2), channel_id=1, source_target_pairs={{0,2},{1,15},{2,4},{3,1},{4,6},{5,3},{6,8},{7,5},{8,10},{9,7},{10,... | collective-permute-start | bytes 864008 | tf_op jit(solution)/shard_map/ppermute | solution.py:25
  22.8 9.8 %collective-permute-start.9 = (f32[64,1125]{1,0:T(8,128)S(1)}, f32[64,1125]{1,0:T(8,128)S(1)}, u32[]{:S(2)}, u32[]{:S(2)}) collective-permute-start(f32[64,1125]{1,0:T(8,128)S(1)} %collective-permute-done.3), channel_id=1, source_target_pairs={{0,2},{1,15},{2,4},{3,1},{4,6},{5,3},{6,8},{7,5},{8,10},{9,7},{10,... | collective-permute-start | bytes 864008 | tf_op jit(solution)/shard_map/ppermute | solution.py:25
  27.4 9.8 %collective-permute-start.10 = (f32[64,1125]{1,0:T(8,128)S(1)}, f32[64,1125]{1,0:T(8,128)S(1)}, u32[]{:S(2)}, u32[]{:S(2)}) collective-permute-start(f32[64,1125]{1,0:T(8,128)S(1)} %collective-permute-done.4), channel_id=1, source_target_pairs={{0,2},{1,15},{2,4},{3,1},{4,6},{5,3},{6,8},{7,5},{8,10},{9,7},{10,... | collective-permute-start | bytes 864008 | tf_op jit(solution)/shard_map/ppermute | solution.py:25
  32.6 9.8 %collective-permute-start.11 = (f32[64,1125]{1,0:T(8,128)S(1)}, f32[64,1125]{1,0:T(8,128)S(1)}, u32[]{:S(2)}, u32[]{:S(2)}) collective-permute-start(f32[64,1125]{1,0:T(8,128)S(1)} %collective-permute-done.9), channel_id=1, source_target_pairs={{0,2},{1,15},{2,4},{3,1},{4,6},{5,3},{6,8},{7,5},{8,10},{9,7},{10,... | collective-permute-start | bytes 864008 | tf_op jit(solution)/shard_map/ppermute | solution.py:25
  45.0 20.9 %collective-permute-start.12 = (f32[3,2,16,480]{3,2,1,0:T(8,128)S(1)}, f32[3,2,16,480]{3,2,1,0:T(8,128)S(1)}, u32[]{:S(2)}, u32[]{:S(2)}) collective-permute-start(f32[3,2,16,480]{3,2,1,0:T(8,128)S(1)} %bitcast.82), channel_id=1, source_target_pairs={{0,16},{1,17},{2,18},{3,19},{4,20},{5,21},{6,22},{7,23},{8,24},{9,... | collective-permute-start | bytes 552968 | tf_op jit(solution)/shard_map/ppermute | solution.py:25
  52.4 17.8 %collective-permute-start.13 = (f32[3,2,16,480]{3,2,1,0:T(8,128)S(1)}, f32[3,2,16,480]{3,2,1,0:T(8,128)S(1)}, u32[]{:S(2)}, u32[]{:S(2)}) collective-permute-start(f32[3,2,16,480]{3,2,1,0:T(8,128)S(1)} %bitcast.80), channel_id=1, source_target_pairs={{0,48},{1,49},{2,50},{3,51},{4,52},{5,53},{6,54},{7,55},{8,56},{9,... | collective-permute-start | bytes 552968 | tf_op jit(solution)/shard_map/ppermute | solution.py:25
  54.3 15.9 %collective-permute-start.14 = (f32[3,2,16,480]{3,2,1,0:T(8,128)S(1)}, f32[3,2,16,480]{3,2,1,0:T(8,128)S(1)}, u32[]{:S(2)}, u32[]{:S(2)}) collective-permute-start(f32[3,2,16,480]{3,2,1,0:T(8,128)S(1)} %bitcast.81), channel_id=1, source_target_pairs={{0,32},{1,33},{2,34},{3,35},{4,36},{5,37},{6,38},{7,39},{8,40},{9,... | collective-permute-start | bytes 552968 | tf_op jit(solution)/shard_map/ppermute | solution.py:25
  59.4 13.5 %collective-permute-start.6 = (f32[5,2,16,480]{3,2,1,0:T(8,128)S(1)}, f32[5,2,16,480]{3,2,1,0:T(8,128)S(1)}, u32[]{:S(2)}, u32[]{:S(2)}) collective-permute-start(f32[5,2,16,480]{3,2,1,0:T(8,128)S(1)} %bitcast.77), channel_id=1, source_target_pairs={{0,16},{1,17},{2,18},{3,19},{4,20},{5,21},{6,22},{7,23},{8,24},{9,... | collective-permute-start | bytes 921608 | tf_op jit(solution)/shard_map/ppermute | solution.py:25
  63.2 16.3 %collective-permute-start.7 = (f32[5,2,16,480]{3,2,1,0:T(8,128)S(1)}, f32[5,2,16,480]{3,2,1,0:T(8,128)S(1)}, u32[]{:S(2)}, u32[]{:S(2)}) collective-permute-start(f32[5,2,16,480]{3,2,1,0:T(8,128)S(1)} %bitcast.78), channel_id=1, source_target_pairs={{0,48},{1,49},{2,50},{3,51},{4,52},{5,53},{6,54},{7,55},{8,56},{9,... | collective-permute-start | bytes 921608 | tf_op jit(solution)/shard_map/ppermute | solution.py:25
  66.0 13.5 %collective-permute-start.8 = (f32[5,2,16,480]{3,2,1,0:T(8,128)S(1)}, f32[5,2,16,480]{3,2,1,0:T(8,128)S(1)}, u32[]{:S(2)}, u32[]{:S(2)}) collective-permute-start(f32[5,2,16,480]{3,2,1,0:T(8,128)S(1)} %bitcast.79), channel_id=1, source_target_pairs={{0,32},{1,33},{2,34},{3,35},{4,36},{5,37},{6,38},{7,39},{8,40},{9,... | collective-permute-start | bytes 921608 | tf_op jit(solution)/shard_map/ppermute | solution.py:25
  79.4 19.9 %copy-start.1 = (f32[60]{0:T(128)S(1)}, f32[60]{0:T(128)}, u32[]{:S(2)}) copy-start(f32[60]{0:T(128)} %param.7) | copy-start | bytes 724
  79.4 19.9 %copy-start.2 = (f32[128]{0:T(128)S(1)}, f32[128]{0:T(128)}, u32[]{:S(2)}) copy-start(f32[128]{0:T(128)} %param.9) | copy-start | bytes 1540
  79.6 43.1 %copy-start.3 = (f32[16]{0:T(128)S(1)}, f32[16]{0:T(128)}, u32[]{:S(2)}) copy-start(f32[16]{0:T(128)} %param.8) | copy-start | bytes 196
  79.7 19.8 %collective-permute-start.15 = (f32[4,16,480]{2,1,0:T(8,128)S(1)}, f32[4,16,480]{2,1,0:T(8,128)S(1)}, u32[]{:S(2)}, u32[]{:S(2)}) collective-permute-start(f32[4,16,480]{2,1,0:T(8,128)S(1)} %get-tuple-element.13), channel_id=1, source_target_pairs={{0,960},{1,65},{2,962},{3,67},{4,964},{5,69},{6,966},{7,71},{8,968... | collective-permute-start | bytes 368648 | tf_op jit(solution)/shard_map/ppermute | solution.py:25
  93.5 8.1 %collective-permute-start.16 = (f32[4,16,480]{2,1,0:T(8,128)S(1)}, f32[4,16,480]{2,1,0:T(8,128)S(1)}, u32[]{:S(2)}, u32[]{:S(2)}) collective-permute-start(f32[4,16,480]{2,1,0:T(8,128)S(1)} %get-tuple-element.15), channel_id=1, source_target_pairs={{0,64},{1,961},{2,66},{3,963},{4,68},{5,965},{6,70},{7,967},{8,72}... | collective-permute-start | bytes 368648 | tf_op jit(solution)/shard_map/ppermute | solution.py:25
  95.4 8.4 %collective-permute-start.17 = (f32[4,16,480]{2,1,0:T(8,128)S(1)}, f32[4,16,480]{2,1,0:T(8,128)S(1)}, u32[]{:S(2)}, u32[]{:S(2)}) collective-permute-start(f32[4,16,480]{2,1,0:T(8,128)S(1)} %get-tuple-element.14), channel_id=1, source_target_pairs={{0,896},{1,129},{2,898},{3,131},{4,900},{5,133},{6,902},{7,135},{8... | collective-permute-start | bytes 368648 | tf_op jit(solution)/shard_map/ppermute | solution.py:25
  103.9 19.2 %collective-permute-start.18 = (f32[16,480]{1,0:T(8,128)S(1)}, f32[16,480]{1,0:T(8,128)S(1)}, u32[]{:S(2)}, u32[]{:S(2)}) collective-permute-start(f32[16,480]{1,0:T(8,128)S(1)} %get-tuple-element.16), channel_id=1, source_target_pairs={{0,0},{1,576},{2,962},{3,450},{4,261},{5,837},{6,199},{7,711},{8,3... | collective-permute-start | bytes 92168 | tf_op jit(solution)/shard_map/ppermute | solution.py:25
  106.0 17.1 %collective-permute-start.19 = (f32[16,480]{1,0:T(8,128)S(1)}, f32[16,480]{1,0:T(8,128)S(1)}, u32[]{:S(2)}, u32[]{:S(2)}) collective-permute-start(f32[16,480]{1,0:T(8,128)S(1)} %get-tuple-element.19), channel_id=1, source_target_pairs={{0,1},{1,385},{2,963},{3,259},{4,132},{5,836},{6,6},{7,710},{8,393... | collective-permute-start | bytes 92168 | tf_op jit(solution)/shard_map/ppermute | solution.py:25
  115.8 11.4 %collective-permute-start.20 = (f32[16,480]{1,0:T(8,128)S(1)}, f32[16,480]{1,0:T(8,128)S(1)}, u32[]{:S(2)}, u32[]{:S(2)}) collective-permute-start(f32[16,480]{1,0:T(8,128)S(1)} %get-tuple-element.18), channel_id=1, source_target_pairs={{0,896},{1,384},{2,770},{3,258},{4,133},{5,645},{6,7},{7,519},{8,5... | collective-permute-start | bytes 92168 | tf_op jit(solution)/shard_map/ppermute | solution.py:25
  120.8 13.6 %collective-permute-start.21 = (f32[16,480]{1,0:T(8,128)S(1)}, f32[16,480]{1,0:T(8,128)S(1)}, u32[]{:S(2)}, u32[]{:S(2)}) collective-permute-start(f32[16,480]{1,0:T(8,128)S(1)} %get-tuple-element.17), channel_id=1, source_target_pairs={{0,897},{1,577},{2,771},{3,451},{4,260},{5,644},{6,198},{7,518},{8... | collective-permute-start | bytes 92168 | tf_op jit(solution)/shard_map/ppermute | solution.py:25

commit v2 on v0

v2 whole, which is shorter than its diff:
```python
import jax
import jax.numpy as jnp
from jax import lax
from jax.sharding import PartitionSpec as P

Z, X, Y, CORES = 16, 4, 8, 2
AXES = ("wide", "narrow")
EVEN, ODD = (0, -2, -4, 2), (-1, 1, -3, 3)


def device(z, x, y, c):
    return (z % Z * X + x % X) * (Y * CORES) + y % Y * CORES + c


def table(move):
    return [
        (device(z, x, y, c), device(*move(z, x, y, c)))
        for z in range(Z)
        for x in range(X)
        for y in range(Y)
        for c in range(CORES)
    ]


def send(array, move):
    return lax.ppermute(array, AXES, table(move))


def other_core(z, x, y, c):
    return z, x, y, 1 - c


def along_y(step):
    return lambda z, x, y, c: (z, x, y + (step if c == 0 else -step), c)


def along_x(step):
    return lambda z, x, y, c: (z, x + step, y, c)


def far_step(z):
    return z % 4 // 2 * 4 - 2


def to_window(near, core):
    def move(z, x, y, c):
        if z % 2 == c:
            return (z if near else z + far_step(z)), x, y, 1 - core
        return (z + 1 if near else z - 1), x, y, core

    return move


def classes():
    groups = []
    for r in range(4):
        c = r % 2
        for x in range(X):
            for y in range(Y):
                offsets = EVEN if (2 * y + c) % 4 == r else ODD
                places = [2 * (y + (o if c == 0 else -o)) + c for o in offsets]
                for core in range(CORES):
                    groups.append([device(z, x, y, core) for z in places])
    return groups


def per_device(amplitudes, integrals, occupied_energy, virtual_energy_rows, virtual_energy_cols):
    wide, narrow = lax.axis_index("wide"), lax.axis_index("narrow")
    z, x, y, c = wide // X, wide % X, narrow // CORES, narrow % CORES
    rows, depth = amplitudes.shape
    cols = integrals.shape[1]
    share = rows // X

    block = jnp.pad(amplitudes.reshape(X, share, depth), ((0, 0), (0, 16 - share), (0, 0)))
    block = jnp.roll(block, -x, axis=0).reshape(X * 16, depth)
    f1 = send(block, along_y(1))
    h1 = send(block, along_y(-1))
    others = send(integrals, other_core)
    f2 = send(f1, along_y(1))
    h2 = send(h1, along_y(-1))

    def messages(blocks):
        tall = jnp.concatenate(blocks, 0)
        halves = [
            jnp.dot(tall, part, precision=lax.Precision.HIGH, preferred_element_type=jnp.float32)
            for part in (integrals, others)
        ]
        halves = jnp.stack([half.reshape(len(blocks), X, 16, cols) for half in halves], 1)
        return [halves[:, :, place] for place in range(X)]

    def sum_over_x(parts):
        return parts[0] + send(parts[1], along_x(1)) + send(parts[3], along_x(-1)) + send(parts[2], along_x(2))

    f2, others = lax.optimization_barrier((f2, others))
    f3 = send(f2, along_y(1))
    h3 = send(h2, along_y(-1))
    early = messages((block, f1, h1, f2, h2))
    f3, early = lax.optimization_barrier((f3, early))
    f4 = send(f3, along_y(1))
    first = sum_over_x(early)
    second = sum_over_x(messages((f3, h3, f4)))
    pieces = jnp.stack(
        [first[0], first[3], second[2], first[4], first[1], first[2], second[0], second[1]], 1
    )
    pieces = pieces.reshape(2, 2, 4, 16, cols)

    at_home = z % 2 == c
    total = 0.0
    for near in (True, False):
        place = jnp.where(at_home, z if near else z + 2, z + 1 if near else z - 1) % 4
        odd = (place != (2 * y + c) % 4).astype(jnp.int32)
        for core in range(CORES):
            half = (jnp.where(at_home, 1 - core, core) != c).astype(jnp.int32)
            part = lax.dynamic_slice(pieces, (half, odd, 0, 0, 0), (1, 1, 4, 16, cols))
            total = total + send(part.reshape(4, 16, cols), to_window(near, core))
    spread = lax.all_to_all(total, AXES, 0, 0, tiled=True, axis_index_groups=classes())
    cycle_term = spread[0] + spread[1] + spread[2] + spread[3]
    cycle_term = cycle_term[:share]

    row_energy = (occupied_energy[None, :] - virtual_energy_rows[:, None]).reshape(-1)
    col_energy = (occupied_energy[None, :] - virtual_energy_cols[:, None]).reshape(-1)
    row_part = lax.dynamic_slice_in_dim(row_energy, wide * share, share)
    col_part = lax.dynamic_slice_in_dim(col_energy, narrow * cols, cols)
    return cycle_term / (row_part[:, None] + col_part[None, :])


def solution(mesh):
    in_specs = (P("narrow", "wide"), P("wide", "narrow"), P(), P(), P())
    out_specs = P("wide", "narrow")
    return jax.shard_map(
        per_device, mesh=mesh, in_specs=in_specs, out_specs=out_specs, check_vma=False
    )
```

time: 264 us -> 128 us (0.48)
  the two profiles are of different devices: /device:TPU:68 before, /device:TPU:2 now
where the time goes in v2:
time: 128 us; the launch traced here: 127 us
  starting transfers between devices  75.2 us (59%)
  waiting for transfers between devices  42.2 us (33%)
  matrix products  5.42 us (4%)
  other arithmetic  2 us (2%)
  local copies, waits for them, and re-layouts  1.72 us (1%)
    ppermute x18, starting transfers between devices, send(): return lax.ppermute(array, AXES, table(move))  71 us
    ppermute x18, waiting for transfers between devices, send(): return lax.ppermute(array, AXES, table(move))  27.7 us
    all_to_all x1, waiting for transfers between devices, per_device(): lax.all_to_all(total, AXES, 0, 0, tiled=True, axis_index_groups=classes())  14.5 us
    dot_general x4, matrix products, messages(): jnp.dot(tall, part, precision=lax.Precision.HIGH, preferred_element_type=...  5.42 us
    all_to_all x1, starting transfers between devices, per_device(): lax.all_to_all(total, AXES, 0, 0, tiled=True, axis_index_groups=classes())  4.22 us
  transfers between devices with their start and end apart: 19, of which 9 were waited for; matrix products, arithmetic and copies ran while one was open for 6% of the time, Pallas kernels for 0%

profile of v2, /device:TPU:2, one launch (start us, length us, event | category | flops | bytes accessed | tf_op | source)
XLA Modules:
  0.0 127.3 jit_solution(16980863962922904061)
XLA Ops:
  0.0 1.9 %collective-permute-start.2 = (f32[1125,480]{0,1:T(8,128)}, f32[1125,480]{0,1:T(8,128)S(1)}, u32[]{:S(2)}, u32[]{:S(2)}) collective-permute-start(f32[1125,480]{0,1:T(8,128)} %param.6), channel_id=1, source_target_pairs={{0,1},{1,0},{2,3},{3,2},{4,5},{5,4},{6,7},{7,6},{8,9},{9,8},{10,11... | collective-permute-start | bytes 6480008 | tf_op jit(solution)/shard_map/ppermute | solution.py:26
  2.0 1.0 reshape.38
  3.0 0.1 fusion.7
  3.1 3.5 %collective-permute-start = (f32[64,1125]{1,0:T(8,128)S(1)}, f32[64,1125]{1,0:T(8,128)S(1)}, u32[]{:S(2)}, u32[]{:S(2)}) collective-permute-start(f32[64,1125]{1,0:T(8,128)S(1)} %bitcast.109), channel_id=1, source_target_pairs={{0,2},{1,15},{2,4},{3,1},{4,6},{5,3},{6,8},{7,5},{8,10},{9,7},{10,... | collective-permute-start | bytes 864008 | tf_op jit(solution)/shard_map/ppermute | solution.py:26
  6.6 3.8 %collective-permute-start.4 = (f32[64,1125]{1,0:T(8,128)S(1)}, f32[64,1125]{1,0:T(8,128)S(1)}, u32[]{:S(2)}, u32[]{:S(2)}) collective-permute-start(f32[64,1125]{1,0:T(8,128)S(1)} %bitcast.110), channel_id=1, source_target_pairs={{0,14},{1,3},{2,0},{3,5},{4,2},{5,7},{6,4},{7,9},{8,6},{9,11},{10,... | collective-permute-start | bytes 864008 | tf_op jit(solution)/shard_map/ppermute | solution.py:26
  10.5 0.0 copy-start
  10.5 2.6 %collective-permute-done = f32[64,1125]{1,0:T(8,128)S(1)} collective-permute-done((f32[64,1125]{1,0:T(8,128)S(1)}, f32[64,1125]{1,0:T(8,128)S(1)}, u32[]{:S(2)}, u32[]{:S(2)}) %collective-permute-start) | collective-permute-done | bytes 288032 | tf_op jit(solution)/shard_map/ppermute | solution.py:26
  13.1 2.6 %collective-permute-start.1 = (f32[64,1125]{1,0:T(8,128)S(1)}, f32[64,1125]{1,0:T(8,128)S(1)}, u32[]{:S(2)}, u32[]{:S(2)}) collective-permute-start(f32[64,1125]{1,0:T(8,128)S(1)} %collective-permute-done), channel_id=1, source_target_pairs={{0,2},{1,15},{2,4},{3,1},{4,6},{5,3},{6,8},{7,5},{8,10},{9,7},{10,... | collective-permute-start | bytes 864008 | tf_op jit(solution)/shard_map/ppermute | solution.py:26
  15.7 0.0 collective-permute-done.4
  15.7 5.2 %collective-permute-start.5 = (f32[64,1125]{1,0:T(8,128)S(1)}, f32[64,1125]{1,0:T(8,128)S(1)}, u32[]{:S(2)}, u32[]{:S(2)}) collective-permute-start(f32[64,1125]{1,0:T(8,128)S(1)} %collective-permute-done.4), channel_id=1, source_target_pairs={{0,14},{1,3},{2,0},{3,5},{4,2},{5,7},{6,4},{7,9},{8,6},{9,11},{10,... | collective-permute-start | bytes 864008 | tf_op jit(solution)/shard_map/ppermute | solution.py:26
  21.0 4.2 %collective-permute-done.5 = f32[64,1125]{1,0:T(8,128)S(1)} collective-permute-done((f32[64,1125]{1,0:T(8,128)S(1)}, f32[64,1125]{1,0:T(8,128)S(1)}, u32[]{:S(2)}, u32[]{:S(2)}) %collective-permute-start.5) | collective-permute-done | bytes 288032 | tf_op jit(solution)/shard_map/ppermute | solution.py:26
  25.2 5.6 %collective-permute-start.9 = (f32[64,1125]{1,0:T(8,128)S(1)}, f32[64,1125]{1,0:T(8,128)S(1)}, u32[]{:S(2)}, u32[]{:S(2)}) collective-permute-start(f32[64,1125]{1,0:T(8,128)S(1)} %collective-permute-done.5), channel_id=1, source_target_pairs={{0,14},{1,3},{2,0},{3,5},{4,2},{5,7},{6,4},{7,9},{8,6},{9,11},{10,... | collective-permute-start | bytes 864008 | tf_op jit(solution)/shard_map/ppermute | solution.py:26
  30.8 0.0 collective-permute-done.1
  30.8 0.0 collective-permute-done.2
  30.8 1.9 %collective-permute-start.3 = (f32[64,1125]{1,0:T(8,128)S(1)}, f32[64,1125]{1,0:T(8,128)S(1)}, u32[]{:S(2)}, u32[]{:S(2)}) collective-permute-start(f32[64,1125]{1,0:T(8,128)S(1)} %collective-permute-done.1), channel_id=1, source_target_pairs={{0,2},{1,15},{2,4},{3,1},{4,6},{5,3},{6,8},{7,5},{8,10},{9,7},{10,... | collective-permute-start | bytes 864008 | tf_op jit(solution)/shard_map/ppermute | solution.py:26
  32.8 0.0 copy-done
  32.8 1.6 %fusion.25 = f32[320,480]{1,0:T(8,128)S(1)} fusion(f32[320,1125]{1,0:T(8,128)S(1)} %constant_dynamic-update-slice_fusion, f32[1125,480]{0,1:T(8,128)S(1)} %copy-done), kind=kOutput, calls=%fused_computation.72 | convolution fusion | flops 1036800000 | bytes 4214400 | tf_op jit(solution)/shard_map/dot_general | solution.py:85
  34.4 1.5 %fusion.26 = f32[320,480]{1,0:T(8,128)S(1)} fusion(f32[320,1125]{1,0:T(8,128)S(1)} %constant_dynamic-update-slice_fusion, f32[1125,480]{0,1:T(8,128)S(1)} %collective-permute-done.2), kind=kOutput, calls=%fused_computation.73 | convolution fusion | flops 1036800000 | bytes 4214400 | tf_op jit(solution)/shard_map/dot_general | solution.py:85
  35.9 0.2 fusion.6
  36.0 4.6 %collective-permute-done.3 = f32[64,1125]{1,0:T(8,128)S(1)} collective-permute-done((f32[64,1125]{1,0:T(8,128)S(1)}, f32[64,1125]{1,0:T(8,128)S(1)}, u32[]{:S(2)}, u32[]{:S(2)}) %collective-permute-start.3) | collective-permute-done | bytes 288032 | tf_op jit(solution)/shard_map/ppermute | solution.py:26
  40.6 1.9 %collective-permute-start.10 = (f32[64,1125]{1,0:T(8,128)S(1)}, f32[64,1125]{1,0:T(8,128)S(1)}, u32[]{:S(2)}, u32[]{:S(2)}) collective-permute-start(f32[64,1125]{1,0:T(8,128)S(1)} %collective-permute-done.3), channel_id=1, source_target_pairs={{0,2},{1,15},{2,4},{3,1},{4,6},{5,3},{6,8},{7,5},{8,10},{9,7},{10,... | collective-permute-start | bytes 864008 | tf_op jit(solution)/shard_map/ppermute | solution.py:26
  42.6 3.4 %collective-permute-start.6 = (f32[5,2,16,480]{3,2,0,1:T(8,128)S(1)}, f32[5,2,16,480]{3,2,0,1:T(8,128)S(1)}, u32[]{:S(2)}, u32[]{:S(2)}) collective-permute-start(f32[5,2,16,480]{3,2,0,1:T(8,128)S(1)} %get-tuple-element.15), channel_id=1, source_target_pairs={{0,16},{1,17},{2,18},{3,19},{4,20},{5,21},{6,22},{7,23},{8,24},{9,... | collective-permute-start | bytes 921608 | tf_op jit(solution)/shard_map/ppermute | solution.py:26
  46.0 14.3 %collective-permute-start.7 = (f32[5,2,16,480]{3,2,0,1:T(8,128)S(1)}, f32[5,2,16,480]{3,2,0,1:T(8,128)S(1)}, u32[]{:S(2)}, u32[]{:S(2)}) collective-permute-start(f32[5,2,16,480]{3,2,0,1:T(8,128)S(1)} %get-tuple-element.16), channel_id=1, source_target_pairs={{0,48},{1,49},{2,50},{3,51},{4,52},{5,53},{6,54},{7,55},{8,56},{9,... | collective-permute-start | bytes 921608 | tf_op jit(solution)/shard_map/ppermute | solution.py:26
  60.2 4.0 %collective-permute-start.8 = (f32[5,2,16,480]{3,2,0,1:T(8,128)S(1)}, f32[5,2,16,480]{3,2,0,1:T(8,128)S(1)}, u32[]{:S(2)}, u32[]{:S(2)}) collective-permute-start(f32[5,2,16,480]{3,2,0,1:T(8,128)S(1)} %get-tuple-element.17), channel_id=1, source_target_pairs={{0,32},{1,33},{2,34},{3,35},{4,36},{5,37},{6,38},{7,39},{8,40},{9,... | collective-permute-start | bytes 921608 | tf_op jit(solution)/shard_map/ppermute | solution.py:26
  64.2 0.0 collective-permute-done.9
  64.3 0.0 collective-permute-done.10
  64.3 1.2 fusion.28
  65.5 1.2 fusion.27
  66.7 0.1 fusion.9
  66.8 4.5 %collective-permute-start.11 = (f32[3,2,16,480]{3,2,1,0:T(8,128)S(1)}, f32[3,2,16,480]{3,2,1,0:T(8,128)S(1)}, u32[]{:S(2)}, u32[]{:S(2)}) collective-permute-start(f32[3,2,16,480]{3,2,1,0:T(8,128)S(1)} %bitcast.113), channel_id=1, source_target_pairs={{0,16},{1,17},{2,18},{3,19},{4,20},{5,21},{6,22},{7,23},{8,24},{9,... | collective-permute-start | bytes 552968 | tf_op jit(solution)/shard_map/ppermute | solution.py:26
  71.3 1.9 %collective-permute-start.12 = (f32[3,2,16,480]{3,2,1,0:T(8,128)S(1)}, f32[3,2,16,480]{3,2,1,0:T(8,128)S(1)}, u32[]{:S(2)}, u32[]{:S(2)}) collective-permute-start(f32[3,2,16,480]{3,2,1,0:T(8,128)S(1)} %bitcast.114), channel_id=1, source_target_pairs={{0,48},{1,49},{2,50},{3,51},{4,52},{5,53},{6,54},{7,55},{8,56},{9,... | collective-permute-start | bytes 552968 | tf_op jit(solution)/shard_map/ppermute | solution.py:26
  73.3 0.0 collective-permute-done.6
  73.3 3.4 %collective-permute-start.13 = (f32[3,2,16,480]{3,2,1,0:T(8,128)S(1)}, f32[3,2,16,480]{3,2,1,0:T(8,128)S(1)}, u32[]{:S(2)}, u32[]{:S(2)}) collective-permute-start(f32[3,2,16,480]{3,2,1,0:T(8,128)S(1)} %bitcast.115), channel_id=1, source_target_pairs={{0,32},{1,33},{2,34},{3,35},{4,36},{5,37},{6,38},{7,39},{8,40},{9,... | collective-permute-start | bytes 552968 | tf_op jit(solution)/shard_map/ppermute | solution.py:26
  76.7 0.0 collective-permute-done.7
  76.7 1.2 collective-permute-done.8
  77.9 0.1 add_add_fusion
  78.1 0.0 collective-permute-done.11
  78.1 3.9 %collective-permute-done.12 = f32[3,2,16,480]{3,2,1,0:T(8,128)S(1)} collective-permute-done((f32[3,2,16,480]{3,2,1,0:T(8,128)S(1)}, f32[3,2,16,480]{3,2,1,0:T(8,128)S(1)}, u32[]{:S(2)}, u32[]{:S(2)}) %collective-permute-start.12) | collective-permute-done | bytes 184352 | tf_op jit(solution)/shard_map/ppermute | solution.py:26
  82.0 4.1 %collective-permute-done.13 = f32[3,2,16,480]{3,2,1,0:T(8,128)S(1)} collective-permute-done((f32[3,2,16,480]{3,2,1,0:T(8,128)S(1)}, f32[3,2,16,480]{3,2,1,0:T(8,128)S(1)}, u32[]{:S(2)}, u32[]{:S(2)}) %collective-permute-start.13) | collective-permute-done | bytes 184352 | tf_op jit(solution)/shard_map/ppermute | solution.py:26
  86.1 0.1 fusion.13
  86.2 0.0 copy-start.1
  86.2 0.0 copy-start.2
  86.2 0.0 copy-start.3
  86.3 0.1 dynamic-slice_bitcast_fusion.2
  86.4 1.9 %collective-permute-start.14 = (f32[4,16,480]{2,1,0:T(8,128)S(1)}, f32[4,16,480]{2,1,0:T(8,128)S(1)}, u32[]{:S(2)}, u32[]{:S(2)}) collective-permute-start(f32[4,16,480]{2,1,0:T(8,128)S(1)} %get-tuple-element.29), channel_id=1, source_target_pairs={{0,1},{1,64},{2,3},{3,66},{4,5},{5,68},{6,7},{7,70},{8,9},{9,72},{... | collective-permute-start | bytes 368648 | tf_op jit(solution)/shard_map/ppermute | solution.py:26
  88.3 0.7 collective-permute-start.15
  89.0 8.6 %collective-permute-start.16 = (f32[4,16,480]{2,1,0:T(8,128)S(1)}, f32[4,16,480]{2,1,0:T(8,128)S(1)}, u32[]{:S(2)}, u32[]{:S(2)}) collective-permute-start(f32[4,16,480]{2,1,0:T(8,128)S(1)} %get-tuple-element.28), channel_id=1, source_target_pairs={{0,897},{1,960},{2,899},{3,962},{4,901},{5,964},{6,903},{7,966},{8... | collective-permute-start | bytes 368648 | tf_op jit(solution)/shard_map/ppermute | solution.py:26
  97.6 1.9 %collective-permute-start.17 = (f32[4,16,480]{2,1,0:T(8,128)S(1)}, f32[4,16,480]{2,1,0:T(8,128)S(1)}, u32[]{:S(2)}, u32[]{:S(2)}) collective-permute-start(f32[4,16,480]{2,1,0:T(8,128)S(1)} %get-tuple-element.30), channel_id=1, source_target_pairs={{0,896},{1,961},{2,898},{3,963},{4,900},{5,965},{6,902},{7,967},{8... | collective-permute-start | bytes 368648 | tf_op jit(solution)/shard_map/ppermute | solution.py:26
  99.5 0.0 collective-permute-done.14
  99.5 0.0 collective-permute-done.15
  99.5 4.1 %collective-permute-done.16 = f32[4,16,480]{2,1,0:T(8,128)S(1)} collective-permute-done((f32[4,16,480]{2,1,0:T(8,128)S(1)}, f32[4,16,480]{2,1,0:T(8,128)S(1)}, u32[]{:S(2)}, u32[]{:S(2)}) %collective-permute-start.16) | collective-permute-done | bytes 122912 | tf_op jit(solution)/shard_map/ppermute | solution.py:26
  103.7 2.9 %collective-permute-done.17 = f32[4,16,480]{2,1,0:T(8,128)S(1)} collective-permute-done((f32[4,16,480]{2,1,0:T(8,128)S(1)}, f32[4,16,480]{2,1,0:T(8,128)S(1)}, u32[]{:S(2)}, u32[]{:S(2)}) %collective-permute-start.17) | collective-permute-done | bytes 122912 | tf_op jit(solution)/shard_map/ppermute | solution.py:26
  106.6 0.7 add_add_fusion.1
  107.2 4.2 %all-to-all-start = ((f32[4,16,480]{2,1,0:T(8,128)}), f32[4,16,480]{2,1,0:T(8,128)S(1)}, u32[]{:S(2)}, u32[]{:S(2)}) async-start(f32[4,16,480]{2,1,0:T(8,128)} %add_add_fusion.1), calls=%async_computation | async-start | bytes 262144 | tf_op jit(solution)/shard_map/all_to_all | solution.py:116
  111.5 0.0 copy-done.1
  111.5 0.1 broadcast_subtract_fusion
  111.6 0.1 sub.59
  111.7 0.0 copy-done.3
  111.7 0.1 broadcast_subtract_fusion.1
  111.8 0.1 sub.55
  111.8 0.1 dynamic_slice.28
  111.9 0.1 dynamic_slice.27
  112.0 14.5 %all-to-all-done = f32[4,16,480]{2,1,0:T(8,128)S(1)} async-done(((f32[4,16,480]{2,1,0:T(8,128)}), f32[4,16,480]{2,1,0:T(8,128)S(1)}, u32[]{:S(2)}, u32[]{:S(2)}) %all-to-all-start) | async-done | bytes 122912 | tf_op jit(solution)/shard_map/all_to_all | solution.py:116
  126.6 0.7 fusion.23
  (22 shorter events, 0.3 us)
Async XLA Ops:
  0.0 30.8 %collective-permute-start.2 = (f32[1125,480]{0,1:T(8,128)}, f32[1125,480]{0,1:T(8,128)S(1)}, u32[]{:S(2)}, u32[]{:S(2)}) collective-permute-start(f32[1125,480]{0,1:T(8,128)} %param.6), channel_id=1, source_target_pairs={{0,1},{1,0},{2,3},{3,2},{4,5},{5,4},{6,7},{7,6},{8,9},{9,8},{10,11... | collective-permute-start | bytes 6480008 | tf_op jit(solution)/shard_map/ppermute | solution.py:26
  3.1 10.1 %collective-permute-start = (f32[64,1125]{1,0:T(8,128)S(1)}, f32[64,1125]{1,0:T(8,128)S(1)}, u32[]{:S(2)}, u32[]{:S(2)}) collective-permute-start(f32[64,1125]{1,0:T(8,128)S(1)} %bitcast.109), channel_id=1, source_target_pairs={{0,2},{1,15},{2,4},{3,1},{4,6},{5,3},{6,8},{7,5},{8,10},{9,7},{10,... | collective-permute-start | bytes 864008 | tf_op jit(solution)/shard_map/ppermute | solution.py:26
  6.6 9.2 %collective-permute-start.4 = (f32[64,1125]{1,0:T(8,128)S(1)}, f32[64,1125]{1,0:T(8,128)S(1)}, u32[]{:S(2)}, u32[]{:S(2)}) collective-permute-start(f32[64,1125]{1,0:T(8,128)S(1)} %bitcast.110), channel_id=1, source_target_pairs={{0,14},{1,3},{2,0},{3,5},{4,2},{5,7},{6,4},{7,9},{8,6},{9,11},{10,... | collective-permute-start | bytes 864008 | tf_op jit(solution)/shard_map/ppermute | solution.py:26
  10.5 22.3 %copy-start = (f32[1125,480]{0,1:T(8,128)S(1)}, f32[1125,480]{0,1:T(8,128)}, u32[]{:S(2)}) copy-start(f32[1125,480]{0,1:T(8,128)} %param.6) | copy-start | bytes 6480004
  13.1 17.6 %collective-permute-start.1 = (f32[64,1125]{1,0:T(8,128)S(1)}, f32[64,1125]{1,0:T(8,128)S(1)}, u32[]{:S(2)}, u32[]{:S(2)}) collective-permute-start(f32[64,1125]{1,0:T(8,128)S(1)} %collective-permute-done), channel_id=1, source_target_pairs={{0,2},{1,15},{2,4},{3,1},{4,6},{5,3},{6,8},{7,5},{8,10},{9,7},{10,... | collective-permute-start | bytes 864008 | tf_op jit(solution)/shard_map/ppermute | solution.py:26
  15.7 9.4 %collective-permute-start.5 = (f32[64,1125]{1,0:T(8,128)S(1)}, f32[64,1125]{1,0:T(8,128)S(1)}, u32[]{:S(2)}, u32[]{:S(2)}) collective-permute-start(f32[64,1125]{1,0:T(8,128)S(1)} %collective-permute-done.4), channel_id=1, source_target_pairs={{0,14},{1,3},{2,0},{3,5},{4,2},{5,7},{6,4},{7,9},{8,6},{9,11},{10,... | collective-permute-start | bytes 864008 | tf_op jit(solution)/shard_map/ppermute | solution.py:26
  25.2 39.1 %collective-permute-start.9 = (f32[64,1125]{1,0:T(8,128)S(1)}, f32[64,1125]{1,0:T(8,128)S(1)}, u32[]{:S(2)}, u32[]{:S(2)}) collective-permute-start(f32[64,1125]{1,0:T(8,128)S(1)} %collective-permute-done.5), channel_id=1, source_target_pairs={{0,14},{1,3},{2,0},{3,5},{4,2},{5,7},{6,4},{7,9},{8,6},{9,11},{10,... | collective-permute-start | bytes 864008 | tf_op jit(solution)/shard_map/ppermute | solution.py:26
  30.8 9.8 %collective-permute-start.3 = (f32[64,1125]{1,0:T(8,128)S(1)}, f32[64,1125]{1,0:T(8,128)S(1)}, u32[]{:S(2)}, u32[]{:S(2)}) collective-permute-start(f32[64,1125]{1,0:T(8,128)S(1)} %collective-permute-done.1), channel_id=1, source_target_pairs={{0,2},{1,15},{2,4},{3,1},{4,6},{5,3},{6,8},{7,5},{8,10},{9,7},{10,... | collective-permute-start | bytes 864008 | tf_op jit(solution)/shard_map/ppermute | solution.py:26
  40.6 23.6 %collective-permute-start.10 = (f32[64,1125]{1,0:T(8,128)S(1)}, f32[64,1125]{1,0:T(8,128)S(1)}, u32[]{:S(2)}, u32[]{:S(2)}) collective-permute-start(f32[64,1125]{1,0:T(8,128)S(1)} %collective-permute-done.3), channel_id=1, source_target_pairs={{0,2},{1,15},{2,4},{3,1},{4,6},{5,3},{6,8},{7,5},{8,10},{9,7},{10,... | collective-permute-start | bytes 864008 | tf_op jit(solution)/shard_map/ppermute | solution.py:26
  42.6 30.7 %collective-permute-start.6 = (f32[5,2,16,480]{3,2,0,1:T(8,128)S(1)}, f32[5,2,16,480]{3,2,0,1:T(8,128)S(1)}, u32[]{:S(2)}, u32[]{:S(2)}) collective-permute-start(f32[5,2,16,480]{3,2,0,1:T(8,128)S(1)} %get-tuple-element.15), channel_id=1, source_target_pairs={{0,16},{1,17},{2,18},{3,19},{4,20},{5,21},{6,22},{7,23},{8,24},{9,... | collective-permute-start | bytes 921608 | tf_op jit(solution)/shard_map/ppermute | solution.py:26
  46.0 30.7 %collective-permute-start.7 = (f32[5,2,16,480]{3,2,0,1:T(8,128)S(1)}, f32[5,2,16,480]{3,2,0,1:T(8,128)S(1)}, u32[]{:S(2)}, u32[]{:S(2)}) collective-permute-start(f32[5,2,16,480]{3,2,0,1:T(8,128)S(1)} %get-tuple-element.16), channel_id=1, source_target_pairs={{0,48},{1,49},{2,50},{3,51},{4,52},{5,53},{6,54},{7,55},{8,56},{9,... | collective-permute-start | bytes 921608 | tf_op jit(solution)/shard_map/ppermute | solution.py:26
  60.2 17.7 %collective-permute-start.8 = (f32[5,2,16,480]{3,2,0,1:T(8,128)S(1)}, f32[5,2,16,480]{3,2,0,1:T(8,128)S(1)}, u32[]{:S(2)}, u32[]{:S(2)}) collective-permute-start(f32[5,2,16,480]{3,2,0,1:T(8,128)S(1)} %get-tuple-element.17), channel_id=1, source_target_pairs={{0,32},{1,33},{2,34},{3,35},{4,36},{5,37},{6,38},{7,39},{8,40},{9,... | collective-permute-start | bytes 921608 | tf_op jit(solution)/shard_map/ppermute | solution.py:26
  66.8 11.3 %collective-permute-start.11 = (f32[3,2,16,480]{3,2,1,0:T(8,128)S(1)}, f32[3,2,16,480]{3,2,1,0:T(8,128)S(1)}, u32[]{:S(2)}, u32[]{:S(2)}) collective-permute-start(f32[3,2,16,480]{3,2,1,0:T(8,128)S(1)} %bitcast.113), channel_id=1, source_target_pairs={{0,16},{1,17},{2,18},{3,19},{4,20},{5,21},{6,22},{7,23},{8,24},{9,... | collective-permute-start | bytes 552968 | tf_op jit(solution)/shard_map/ppermute | solution.py:26
  71.3 10.7 %collective-permute-start.12 = (f32[3,2,16,480]{3,2,1,0:T(8,128)S(1)}, f32[3,2,16,480]{3,2,1,0:T(8,128)S(1)}, u32[]{:S(2)}, u32[]{:S(2)}) collective-permute-start(f32[3,2,16,480]{3,2,1,0:T(8,128)S(1)} %bitcast.114), channel_id=1, source_target_pairs={{0,48},{1,49},{2,50},{3,51},{4,52},{5,53},{6,54},{7,55},{8,56},{9,... | collective-permute-start | bytes 552968 | tf_op jit(solution)/shard_map/ppermute | solution.py:26
  73.3 12.8 %collective-permute-start.13 = (f32[3,2,16,480]{3,2,1,0:T(8,128)S(1)}, f32[3,2,16,480]{3,2,1,0:T(8,128)S(1)}, u32[]{:S(2)}, u32[]{:S(2)}) collective-permute-start(f32[3,2,16,480]{3,2,1,0:T(8,128)S(1)} %bitcast.115), channel_id=1, source_target_pairs={{0,32},{1,33},{2,34},{3,35},{4,36},{5,37},{6,38},{7,39},{8,40},{9,... | collective-permute-start | bytes 552968 | tf_op jit(solution)/shard_map/ppermute | solution.py:26
  86.2 25.3 %copy-start.1 = (f32[60]{0:T(128)S(1)}, f32[60]{0:T(128)}, u32[]{:S(2)}) copy-start(f32[60]{0:T(128)} %param.7) | copy-start | bytes 724
  86.2 25.3 %copy-start.2 = (f32[128]{0:T(128)S(1)}, f32[128]{0:T(128)}, u32[]{:S(2)}) copy-start(f32[128]{0:T(128)} %param.9) | copy-start | bytes 1540
  86.2 25.5 %copy-start.3 = (f32[16]{0:T(128)S(1)}, f32[16]{0:T(128)}, u32[]{:S(2)}) copy-start(f32[16]{0:T(128)} %param.8) | copy-start | bytes 196
  86.4 13.2 %collective-permute-start.14 = (f32[4,16,480]{2,1,0:T(8,128)S(1)}, f32[4,16,480]{2,1,0:T(8,128)S(1)}, u32[]{:S(2)}, u32[]{:S(2)}) collective-permute-start(f32[4,16,480]{2,1,0:T(8,128)S(1)} %get-tuple-element.29), channel_id=1, source_target_pairs={{0,1},{1,64},{2,3},{3,66},{4,5},{5,68},{6,7},{7,70},{8,9},{9,72},{... | collective-permute-start | bytes 368648 | tf_op jit(solution)/shard_map/ppermute | solution.py:26
  88.3 11.2 %collective-permute-start.15 = (f32[4,16,480]{2,1,0:T(8,128)S(1)}, f32[4,16,480]{2,1,0:T(8,128)S(1)}, u32[]{:S(2)}, u32[]{:S(2)}) collective-permute-start(f32[4,16,480]{2,1,0:T(8,128)S(1)} %get-tuple-element.27), channel_id=1, source_target_pairs={{0,0},{1,65},{2,2},{3,67},{4,4},{5,69},{6,6},{7,71},{8,8},{9,73},{... | collective-permute-start | bytes 368648 | tf_op jit(solution)/shard_map/ppermute | solution.py:26
  89.0 14.7 %collective-permute-start.16 = (f32[4,16,480]{2,1,0:T(8,128)S(1)}, f32[4,16,480]{2,1,0:T(8,128)S(1)}, u32[]{:S(2)}, u32[]{:S(2)}) collective-permute-start(f32[4,16,480]{2,1,0:T(8,128)S(1)} %get-tuple-element.28), channel_id=1, source_target_pairs={{0,897},{1,960},{2,899},{3,962},{4,901},{5,964},{6,903},{7,966},{8... | collective-permute-start | bytes 368648 | tf_op jit(solution)/shard_map/ppermute | solution.py:26
  97.6 9.0 %collective-permute-start.17 = (f32[4,16,480]{2,1,0:T(8,128)S(1)}, f32[4,16,480]{2,1,0:T(8,128)S(1)}, u32[]{:S(2)}, u32[]{:S(2)}) collective-permute-start(f32[4,16,480]{2,1,0:T(8,128)S(1)} %get-tuple-element.30), channel_id=1, source_target_pairs={{0,896},{1,961},{2,898},{3,963},{4,900},{5,965},{6,902},{7,967},{8... | collective-permute-start | bytes 368648 | tf_op jit(solution)/shard_map/ppermute | solution.py:26
  107.2 19.3 %all-to-all-start = ((f32[4,16,480]{2,1,0:T(8,128)}), f32[4,16,480]{2,1,0:T(8,128)S(1)}, u32[]{:S(2)}, u32[]{:S(2)}) async-start(f32[4,16,480]{2,1,0:T(8,128)} %add_add_fusion.1), calls=%async_computation | async-start | bytes 262144 | tf_op jit(solution)/shard_map/all_to_all | solution.py:116

commit v3 on v2

v3 whole, which is shorter than its diff:
```python
import jax
import jax.numpy as jnp
from jax import lax
from jax.sharding import PartitionSpec as P

Z, X, Y, CORES = 16, 4, 8, 2
AXES = ("wide", "narrow")
EVEN, ODD = (0, -2, -4, 2), (-1, 1, -3, 3)


def device(z, x, y, c):
    return (z % Z * X + x % X) * (Y * CORES) + y % Y * CORES + c


def table(move):
    return [
        (device(z, x, y, c), device(*move(z, x, y, c)))
        for z in range(Z)
        for x in range(X)
        for y in range(Y)
        for c in range(CORES)
    ]


def send(array, move):
    return lax.ppermute(array, AXES, table(move))


def other_core(z, x, y, c):
    return z, x, y, 1 - c


def along_y(step):
    return lambda z, x, y, c: (z, x, y + (step if c == 0 else -step), c)


def swap_z(first):
    def move(z, x, y, c):
        return z + (1 if (z % 2 == 0) == (first == (c == 0)) else -1), x, y, c

    return move


def planes():
    return [
        [device(z, x, y, c) for x in range(X) for c in range(CORES)] for z in range(Z) for y in range(Y)
    ]


def classes():
    groups = []
    for r in range(4):
        c = r % 2
        for x in range(X):
            for y in range(Y):
                offsets = EVEN if (2 * y + c) % 4 == r else ODD
                places = [2 * (y + (o if c == 0 else -o)) + c for o in offsets]
                for core in range(CORES):
                    groups.append([device(z, x, y, core) for z in places])
    return groups


def per_device(amplitudes, integrals, occupied_energy, virtual_energy_rows, virtual_energy_cols):
    wide, narrow = lax.axis_index("wide"), lax.axis_index("narrow")
    z, y, c = wide // X, narrow // CORES, narrow % CORES
    rows, depth = amplitudes.shape
    cols = integrals.shape[1]
    share = rows // X

    block = jnp.pad(amplitudes.reshape(X, share, depth), ((0, 0), (0, 16 - share), (0, 0)))
    block = block.reshape(X * 16, depth)
    block, integrals = lax.optimization_barrier((block, integrals))
    f1 = send(block, along_y(1))
    h1 = send(block, along_y(-1))
    others = send(integrals, other_core)
    f2 = send(f1, along_y(1))
    h2 = send(h1, along_y(-1))

    def sums_over_x(blocks):
        tall = jnp.concatenate(blocks, 0)
        own, other = (
            jnp.dot(tall, part, precision=lax.Precision.HIGH, preferred_element_type=jnp.float32).reshape(
                len(blocks), X, 16, cols
            )
            for part in (integrals, others)
        )
        halves = jnp.stack([jnp.where(c == 0, own, other), jnp.where(c == 0, other, own)], 0)
        return halves.transpose(2, 0, 1, 3, 4).reshape(X * CORES, len(blocks), 16, cols)

    def exchange_x(parts):
        parts = lax.all_to_all(parts, AXES, 0, 0, tiled=True, axis_index_groups=planes())
        return parts.reshape(X, CORES, *parts.shape[1:]).sum(0)

    f2, h2, others = lax.optimization_barrier((f2, h2, others))
    h3 = send(h2, along_y(-1))
    f3 = send(f2, along_y(1))
    early = sums_over_x((block, f1, h1, f2, h2))
    f3, early = lax.optimization_barrier((f3, early))
    f4 = send(f3, along_y(1))
    first = exchange_x(early)
    late = sums_over_x((f3, h3, f4))
    first, late = lax.optimization_barrier((first, late))
    second = exchange_x(late)
    even = jnp.stack([first[:, 0], first[:, 3], second[:, 2], first[:, 4]], 1)
    odd = jnp.stack([first[:, 1], first[:, 2], second[:, 0], second[:, 1]], 1)
    pieces = jnp.concatenate([even, odd], 0)

    def class_of(place):
        return lax.dynamic_index_in_dim(pieces, (place - 2 * y) % 4, 0, keepdims=False)

    one = jnp.where((z % 2 == 0) == (c == 0), 1, -1)
    sent = jnp.stack([class_of(z + one), class_of(z + 2 * one)], 0)
    kept = jnp.stack([class_of(z), class_of(z - one)], 0)
    kept = kept + send(sent, swap_z(True))
    total = kept[0] + send(kept[1], swap_z(False))
    spread = lax.all_to_all(total, AXES, 0, 0, tiled=True, axis_index_groups=classes())
    cycle_term = spread[0] + spread[1] + spread[2] + spread[3]
    cycle_term = cycle_term[:share]

    row_energy = (occupied_energy[None, :] - virtual_energy_rows[:, None]).reshape(-1)
    col_energy = (occupied_energy[None, :] - virtual_energy_cols[:, None]).reshape(-1)
    row_part = lax.dynamic_slice_in_dim(row_energy, wide * share, share)
    col_part = lax.dynamic_slice_in_dim(col_energy, narrow * cols, cols)
    return cycle_term / (row_part[:, None] + col_part[None, :])


def solution(mesh):
    in_specs = (P("narrow", "wide"), P("wide", "narrow"), P(), P(), P())
    out_specs = P("wide", "narrow")
    return jax.shard_map(
        per_device, mesh=mesh, in_specs=in_specs, out_specs=out_specs, check_vma=False
    )
```

time: 128 us -> 138 us (1.078)
  starting transfers between devices: 75.2 us -> 61.2 us
  waiting for transfers between devices: 42.2 us -> 55.3 us
  local copies, waits for them, and re-layouts: 1.72 us -> 9.81 us
  matrix products: 5.42 us -> 8.88 us
    ppermute x18 -> x10, starting transfers between devices: 71 us -> 38.3 us  [send(): return lax.ppermute(array, AXES, table(move))]
    all_to_all x0 -> x2, waiting for transfers between devices: none -> 20.4 us  [exchange_x(): lax.all_to_all(parts, AXES, 0, 0, tiled=True, axis_index_groups=planes())]
    all_to_all x0 -> x2, starting transfers between devices: none -> 17.2 us  [exchange_x(): lax.all_to_all(parts, AXES, 0, 0, tiled=True, axis_index_groups=planes())]
    ppermute x18 -> x10, waiting for transfers between devices: 27.7 us -> 21 us  [send(): return lax.ppermute(array, AXES, table(move))]
    dot_general x4, matrix products: 5.42 us -> 8.88 us  [sums_over_x(): jnp.dot(tall, part, precision=lax.Precision.HIGH, preferred_element_type=...]
    unnamed x24 -> x16, local copies, waits for them, and re-layouts: 0.25 us -> 3.51 us
    concatenate x2, local copies, waits for them, and re-layouts: 0.04 us -> 2.69 us  [sums_over_x(): tall = jnp.concatenate(blocks, 0)]
    another operation x1 -> x2, local copies, waits for them, and re-layouts: 0.01 us -> 2.14 us  [sums_over_x(): jnp.stack([jnp.where(c == 0, own, other), jnp.where(c == 0, other, own)], 0)]
  transfers between devices with their start and end apart: 19 -> 13, of which waited for: 9 -> 8; matrix products, arithmetic and copies ran while one was open for 6% -> 13% of each run, Pallas kernels for 0% -> 0%
where the time goes in v3:
time: 138 us
  starting transfers between devices  61.2 us (44%)
  waiting for transfers between devices  55.3 us (40%)
  local copies, waits for them, and re-layouts  9.81 us (7%)
  matrix products  8.88 us (6%)
  other arithmetic  2.01 us (1%)
    ppermute x10, starting transfers between devices, send(): return lax.ppermute(array, AXES, table(move))  38.3 us
    ppermute x10, waiting for transfers between devices, send(): return lax.ppermute(array, AXES, table(move))  21 us
    all_to_all x2, waiting for transfers between devices, exchange_x(): lax.all_to_all(parts, AXES, 0, 0, tiled=True, axis_index_groups=planes())  20.4 us
    all_to_all x2, starting transfers between devices, exchange_x(): lax.all_to_all(parts, AXES, 0, 0, tiled=True, axis_index_groups=planes())  17.2 us
    all_to_all x1, waiting for transfers between devices, per_device(): lax.all_to_all(total, AXES, 0, 0, tiled=True, axis_index_groups=classes())  14 us
    dot_general x4, matrix products, sums_over_x(): jnp.dot(tall, part, precision=lax.Precision.HIGH, preferred_element_type=...  8.88 us
    all_to_all x1, starting transfers between devices, per_device(): lax.all_to_all(total, AXES, 0, 0, tiled=True, axis_index_groups=classes())  5.63 us
    unnamed x16, local copies, waits for them, and re-layouts  3.51 us
  transfers between devices with their start and end apart: 13, of which 8 were waited for; matrix products, arithmetic and copies ran while one was open for 13% of the time, Pallas kernels for 0%

profile of v3, /device:TPU:2, one launch (start us, length us, event | category | flops | bytes accessed | tf_op | source)
XLA Modules:
  0.0 137.6 jit_solution(5189876799025028365)
XLA Ops:
  0.0 1.0 reshape.115
  1.0 1.9 %collective-permute-start.4 = (f32[1125,480]{0,1:T(8,128)}, f32[1125,480]{0,1:T(8,128)}, u32[]{:S(2)}, u32[]{:S(2)}) collective-permute-start(f32[1125,480]{0,1:T(8,128)} %param.6), channel_id=1, source_target_pairs={{0,1},{1,0},{2,3},{3,2},{4,5},{5,4},{6,7},{7,6},{8,9},{9,8},{10,11... | collective-permute-start | bytes 6480008 | tf_op jit(solution)/shard_map/ppermute | solution.py:26
  3.0 5.4 %collective-permute-start.2 = (f32[64,1125]{1,0:T(8,128)S(1)}, f32[64,1125]{1,0:T(8,128)S(1)}, u32[]{:S(2)}, u32[]{:S(2)}) collective-permute-start(f32[64,1125]{1,0:T(8,128)S(1)} %bitcast.37), channel_id=1, source_target_pairs={{0,14},{1,3},{2,0},{3,5},{4,2},{5,7},{6,4},{7,9},{8,6},{9,11},{10,... | collective-permute-start | bytes 864008 | tf_op jit(solution)/shard_map/ppermute | solution.py:26
  8.3 1.9 %collective-permute-start = (f32[64,1125]{1,0:T(8,128)S(1)}, f32[64,1125]{1,0:T(8,128)S(1)}, u32[]{:S(2)}, u32[]{:S(2)}) collective-permute-start(f32[64,1125]{1,0:T(8,128)S(1)} %bitcast.38), channel_id=1, source_target_pairs={{0,2},{1,15},{2,4},{3,1},{4,6},{5,3},{6,8},{7,5},{8,10},{9,7},{10,... | collective-permute-start | bytes 864008 | tf_op jit(solution)/shard_map/ppermute | solution.py:26
  10.3 0.0 copy-start
  10.3 3.9 %collective-permute-done.2 = f32[64,1125]{1,0:T(8,128)S(1)} collective-permute-done((f32[64,1125]{1,0:T(8,128)S(1)}, f32[64,1125]{1,0:T(8,128)S(1)}, u32[]{:S(2)}, u32[]{:S(2)}) %collective-permute-start.2) | collective-permute-done | bytes 288032 | tf_op jit(solution)/shard_map/ppermute | solution.py:26
  14.2 5.6 %collective-permute-start.3 = (f32[64,1125]{1,0:T(8,128)S(1)}, f32[64,1125]{1,0:T(8,128)}, u32[]{:S(2)}, u32[]{:S(2)}) collective-permute-start(f32[64,1125]{1,0:T(8,128)S(1)} %collective-permute-done.2), channel_id=1, source_target_pairs={{0,14},{1,3},{2,0},{3,5},{4,2},{5,7},{6,4},{7,9},{8,6},{9,11},{10,... | collective-permute-start | bytes 864008 | tf_op jit(solution)/shard_map/ppermute | solution.py:26
  19.8 0.0 collective-permute-done
  19.8 1.9 %collective-permute-start.1 = (f32[64,1125]{1,0:T(8,128)S(1)}, f32[64,1125]{1,0:T(8,128)S(1)}, u32[]{:S(2)}, u32[]{:S(2)}) collective-permute-start(f32[64,1125]{1,0:T(8,128)S(1)} %collective-permute-done), channel_id=1, source_target_pairs={{0,2},{1,15},{2,4},{3,1},{4,6},{5,3},{6,8},{7,5},{8,10},{9,7},{10,... | collective-permute-start | bytes 864008 | tf_op jit(solution)/shard_map/ppermute | solution.py:26
  21.8 5.1 %collective-permute-done.3 = f32[64,1125]{1,0:T(8,128)} collective-permute-done((f32[64,1125]{1,0:T(8,128)S(1)}, f32[64,1125]{1,0:T(8,128)}, u32[]{:S(2)}, u32[]{:S(2)}) %collective-permute-start.3) | collective-permute-done | bytes 288032 | tf_op jit(solution)/shard_map/ppermute | solution.py:26
  26.9 2.7 %collective-permute-done.1 = f32[64,1125]{1,0:T(8,128)S(1)} collective-permute-done((f32[64,1125]{1,0:T(8,128)S(1)}, f32[64,1125]{1,0:T(8,128)S(1)}, u32[]{:S(2)}, u32[]{:S(2)}) %collective-permute-start.1) | collective-permute-done | bytes 288032 | tf_op jit(solution)/shard_map/ppermute | solution.py:26
  29.6 0.0 collective-permute-done.4
  29.6 1.9 %collective-permute-start.5 = (f32[64,1125]{1,0:T(8,128)S(1)}, f32[64,1125]{1,0:T(8,128)}, u32[]{:S(2)}, u32[]{:S(2)}) collective-permute-start(f32[64,1125]{1,0:T(8,128)S(1)} %collective-permute-done.1), channel_id=1, source_target_pairs={{0,2},{1,15},{2,4},{3,1},{4,6},{5,3},{6,8},{7,5},{8,10},{9,7},{10,... | collective-permute-start | bytes 864008 | tf_op jit(solution)/shard_map/ppermute | solution.py:26
  31.6 5.1 %collective-permute-start.6 = (f32[64,1125]{1,0:T(8,128)}, f32[64,1125]{1,0:T(8,128)}, u32[]{:S(2)}, u32[]{:S(2)}) collective-permute-start(f32[64,1125]{1,0:T(8,128)} %collective-permute-done.3), channel_id=1, source_target_pairs={{0,14},{1,3},{2,0},{3,5},{4,2},{5,7},{6,4},{7,9},{8,6},{9,11},{10,... | collective-permute-start | bytes 864008 | tf_op jit(solution)/shard_map/ppermute | solution.py:26
  36.7 1.0 constant_dynamic-update-slice_fusion
  37.7 0.0 copy-done
  37.7 1.5 %fusion.5 = f32[320,480]{1,0:T(8,128)S(1)} fusion(f32[320,1125]{1,0:T(8,128)S(1)} %constant_dynamic-update-slice_fusion, f32[1125,480]{0,1:T(8,128)S(1)} %copy-done), kind=kOutput, calls=%fused_computation.33 | convolution fusion | flops 1036800000 | bytes 4214400 | tf_op jit(solution)/shard_map/dot_general | solution.py:82
  39.2 3.1 %broadcast_select_fusion.1 = (f32[320,480]{1,0:T(8,128)S(1)}, f32[320,480]{1,0:T(8,128)S(1)}) fusion(f32[320,480]{1,0:T(8,128)S(1)} %fusion.5, pred[]{:T(512)S(6)} %eq.20, f32[320,1125]{1,0:T(8,128)S(1)} %constant_dynamic-update-slice_fusion, f32[1125,480]{0,1:T(8,128)} %collective-permute-done.4), kind=kOutput, calls=%fused_computation.4 | convolution fusion | flops 1037107200 | bytes 5443201 | tf_op jit(solution)/shard_map/dot_general | solution.py:82
  42.4 0.1 pad_maximum_fusion
  42.5 1.2 copy.10
  43.7 0.0 collective-permute-done.5
  43.7 1.9 %collective-permute-start.7 = (f32[64,1125]{1,0:T(8,128)}, f32[64,1125]{1,0:T(8,128)}, u32[]{:S(2)}, u32[]{:S(2)}) collective-permute-start(f32[64,1125]{1,0:T(8,128)} %collective-permute-done.5), channel_id=1, source_target_pairs={{0,2},{1,15},{2,4},{3,1},{4,6},{5,3},{6,8},{7,5},{8,10},{9,7},{10,... | collective-permute-start | bytes 864008 | tf_op jit(solution)/shard_map/ppermute | solution.py:26
  45.7 1.7 %constant_dynamic-update-slice_fusion.7 = f32[192,1125]{1,0:T(8,128)} fusion(f32[64,1125]{1,0:T(8,128)} %collective-permute-done.5), kind=kLoop, calls=%fused_computation.25 | loop fusion | bytes 582912
  47.4 12.3 %all-to-all-start = ((f32[8,5,16,480]{3,2,1,0:T(8,128)}), f32[8,5,16,480]{3,2,1,0:T(8,128)S(1)}, u32[]{:S(2)}, u32[]{:S(2)}) async-start(f32[8,5,16,480]{3,2,1,0:T(8,128)} %bitcast.4), calls=%async_computation | async-start | bytes 2621440 | tf_op jit(solution)/shard_map/all_to_all | solution.py:91
  59.7 0.0 collective-permute-done.6
  59.7 1.7 %constant_dynamic-update-slice_fusion.6 = f32[192,1125]{1,0:T(8,128)} fusion(f32[192,1125]{1,0:T(8,128)} %constant_dynamic-update-slice_fusion.7, f32[64,1125]{1,0:T(8,128)} %collective-permute-done.6), kind=kLoop, calls=%fused_computation.24 | loop fusion | bytes 589824
  61.4 0.0 collective-permute-done.7
  61.4 1.7 %constant_dynamic-update-slice_fusion.5 = f32[192,1125]{1,0:T(8,128)} fusion(f32[192,1125]{1,0:T(8,128)} %constant_dynamic-update-slice_fusion.6, f32[64,1125]{1,0:T(8,128)} %collective-permute-done.7), kind=kLoop, calls=%fused_computation.23 | loop fusion | bytes 589824 | tf_op jit(solution)/shard_map/concatenate | solution.py:80
  63.1 0.0 copy-start.1
  63.1 3.1 %fusion.6 = f32[192,480]{1,0:T(8,128)S(1)} fusion(f32[192,1125]{1,0:T(8,128)} %constant_dynamic-update-slice_fusion.5, f32[1125,480]{0,1:T(8,128)} %collective-permute-done.4), kind=kOutput, calls=%fused_computation.34 | convolution fusion | flops 622080000 | bytes 3392640 | tf_op jit(solution)/shard_map/dot_general | solution.py:82
  66.2 0.0 copy-done.1
  66.2 1.2 broadcast_select_fusion.3
  67.4 0.1 pad_maximum_fusion.1
  67.4 0.9 copy.11
  68.4 8.7 %all-to-all-done = f32[8,5,16,480]{3,2,1,0:T(8,128)S(1)} async-done(((f32[8,5,16,480]{3,2,1,0:T(8,128)}), f32[8,5,16,480]{3,2,1,0:T(8,128)S(1)}, u32[]{:S(2)}, u32[]{:S(2)}) %all-to-all-start) | async-done | bytes 1228832 | tf_op jit(solution)/shard_map/all_to_all | solution.py:91
  77.0 0.1 reduce_sum.18
  77.2 4.9 %all-to-all-start.1 = ((f32[8,3,16,480]{3,2,1,0:T(8,128)}), f32[8,3,16,480]{3,2,1,0:T(8,128)S(1)}, u32[]{:S(2)}, u32[]{:S(2)}) async-start(f32[8,3,16,480]{3,2,1,0:T(8,128)} %bitcast.9), calls=%async_computation.1 | async-start | bytes 1572864 | tf_op jit(solution)/shard_map/all_to_all | solution.py:91
  82.1 11.7 %all-to-all-done.1 = f32[8,3,16,480]{3,2,1,0:T(8,128)S(1)} async-done(((f32[8,3,16,480]{3,2,1,0:T(8,128)}), f32[8,3,16,480]{3,2,1,0:T(8,128)S(1)}, u32[]{:S(2)}, u32[]{:S(2)}) %all-to-all-start.1) | async-done | bytes 737312 | tf_op jit(solution)/shard_map/all_to_all | solution.py:91
  93.8 0.1 reduce_sum.19
  94.0 0.0 copy-start.2
  94.0 0.0 copy-start.4
  94.0 0.0 copy-start.3
  94.0 0.1 constant_dynamic-slice_fusion.3
  94.1 1.9 %collective-permute-start.8 = (f32[2,4,16,480]{3,2,1,0:T(8,128)S(1)}, f32[2,4,16,480]{3,2,1,0:T(8,128)S(1)}, u32[]{:S(2)}, u32[]{:S(2)}) collective-permute-start(f32[2,4,16,480]{3,2,1,0:T(8,128)S(1)} %pad_maximum_fusion.2), channel_id=1, source_target_pairs={{0,64},{1,961},{2,66},{3,963},{4,68},{5,965},{6,70},{7,967},{8,72}... | collective-permute-start | bytes 737288 | tf_op jit(solution)/shard_map/ppermute | solution.py:26
  96.0 6.3 %collective-permute-done.8 = f32[2,4,16,480]{3,2,1,0:T(8,128)S(1)} collective-permute-done((f32[2,4,16,480]{3,2,1,0:T(8,128)S(1)}, f32[2,4,16,480]{3,2,1,0:T(8,128)S(1)}, u32[]{:S(2)}, u32[]{:S(2)}) %collective-permute-start.8) | collective-permute-done | bytes 245792 | tf_op jit(solution)/shard_map/ppermute | solution.py:26
  102.4 10.7 %collective-permute-start.9 = (f32[4,16,480]{2,1,0:T(8,128)S(1)}, f32[4,16,480]{2,1,0:T(8,128)S(1)}, u32[]{:S(2)}, u32[]{:S(2)}) collective-permute-start(f32[4,16,480]{2,1,0:T(8,128)S(1)} %slice_bitcast_fusion), channel_id=1, source_target_pairs={{0,960},{1,65},{2,962},{3,67},{4,964},{5,69},{6,966},{7,71},{8,968... | collective-permute-start | bytes 368648 | tf_op jit(solution)/shard_map/ppermute | solution.py:26
  113.1 2.9 %collective-permute-done.9 = f32[4,16,480]{2,1,0:T(8,128)S(1)} collective-permute-done((f32[4,16,480]{2,1,0:T(8,128)S(1)}, f32[4,16,480]{2,1,0:T(8,128)S(1)}, u32[]{:S(2)}, u32[]{:S(2)}) %collective-permute-start.9) | collective-permute-done | bytes 122912 | tf_op jit(solution)/shard_map/ppermute | solution.py:26
  116.1 0.7 fusion
  116.7 5.6 %all-to-all-start.2 = ((f32[4,16,480]{2,1,0:T(8,128)}), f32[4,16,480]{2,1,0:T(8,128)S(1)}, u32[]{:S(2)}, u32[]{:S(2)}) async-start(f32[4,16,480]{2,1,0:T(8,128)} %fusion), calls=%async_computation.2 | async-start | bytes 262144 | tf_op jit(solution)/shard_map/all_to_all | solution.py:116
  122.4 0.0 copy-done.2
  122.4 0.0 copy-done.4
  122.4 0.1 broadcast_subtract_fusion.1
  122.5 0.1 sub.66
  122.5 0.0 copy-done.3
  122.6 0.1 broadcast_subtract_fusion
  122.6 0.1 sub.70
  122.7 0.1 dynamic_slice.23
  122.8 0.1 dynamic_slice.24
  122.9 14.0 %all-to-all-done.2 = f32[4,16,480]{2,1,0:T(8,128)S(1)} async-done(((f32[4,16,480]{2,1,0:T(8,128)}), f32[4,16,480]{2,1,0:T(8,128)S(1)}, u32[]{:S(2)}, u32[]{:S(2)}) %all-to-all-start.2) | async-done | bytes 122912 | tf_op jit(solution)/shard_map/all_to_all | solution.py:116
  136.9 0.7 fusion.2
  (14 shorter events, 0.3 us)
Async XLA Ops:
  1.0 28.6 %collective-permute-start.4 = (f32[1125,480]{0,1:T(8,128)}, f32[1125,480]{0,1:T(8,128)}, u32[]{:S(2)}, u32[]{:S(2)}) collective-permute-start(f32[1125,480]{0,1:T(8,128)} %param.6), channel_id=1, source_target_pairs={{0,1},{1,0},{2,3},{3,2},{4,5},{5,4},{6,7},{7,6},{8,9},{9,8},{10,11... | collective-permute-start | bytes 6480008 | tf_op jit(solution)/shard_map/ppermute | solution.py:26
  3.0 11.2 %collective-permute-start.2 = (f32[64,1125]{1,0:T(8,128)S(1)}, f32[64,1125]{1,0:T(8,128)S(1)}, u32[]{:S(2)}, u32[]{:S(2)}) collective-permute-start(f32[64,1125]{1,0:T(8,128)S(1)} %bitcast.37), channel_id=1, source_target_pairs={{0,14},{1,3},{2,0},{3,5},{4,2},{5,7},{6,4},{7,9},{8,6},{9,11},{10,... | collective-permute-start | bytes 864008 | tf_op jit(solution)/shard_map/ppermute | solution.py:26
  8.3 11.5 %collective-permute-start = (f32[64,1125]{1,0:T(8,128)S(1)}, f32[64,1125]{1,0:T(8,128)S(1)}, u32[]{:S(2)}, u32[]{:S(2)}) collective-permute-start(f32[64,1125]{1,0:T(8,128)S(1)} %bitcast.38), channel_id=1, source_target_pairs={{0,2},{1,15},{2,4},{3,1},{4,6},{5,3},{6,8},{7,5},{8,10},{9,7},{10,... | collective-permute-start | bytes 864008 | tf_op jit(solution)/shard_map/ppermute | solution.py:26
  10.3 27.4 %copy-start = (f32[1125,480]{0,1:T(8,128)S(1)}, f32[1125,480]{0,1:T(8,128)}, u32[]{:S(2)}) copy-start(f32[1125,480]{0,1:T(8,128)} %param.6) | copy-start | bytes 6480004
  14.2 12.7 %collective-permute-start.3 = (f32[64,1125]{1,0:T(8,128)S(1)}, f32[64,1125]{1,0:T(8,128)}, u32[]{:S(2)}, u32[]{:S(2)}) collective-permute-start(f32[64,1125]{1,0:T(8,128)S(1)} %collective-permute-done.2), channel_id=1, source_target_pairs={{0,14},{1,3},{2,0},{3,5},{4,2},{5,7},{6,4},{7,9},{8,6},{9,11},{10,... | collective-permute-start | bytes 864008 | tf_op jit(solution)/shard_map/ppermute | solution.py:26
  19.8 9.8 %collective-permute-start.1 = (f32[64,1125]{1,0:T(8,128)S(1)}, f32[64,1125]{1,0:T(8,128)S(1)}, u32[]{:S(2)}, u32[]{:S(2)}) collective-permute-start(f32[64,1125]{1,0:T(8,128)S(1)} %collective-permute-done), channel_id=1, source_target_pairs={{0,2},{1,15},{2,4},{3,1},{4,6},{5,3},{6,8},{7,5},{8,10},{9,7},{10,... | collective-permute-start | bytes 864008 | tf_op jit(solution)/shard_map/ppermute | solution.py:26
  29.6 14.1 %collective-permute-start.5 = (f32[64,1125]{1,0:T(8,128)S(1)}, f32[64,1125]{1,0:T(8,128)}, u32[]{:S(2)}, u32[]{:S(2)}) collective-permute-start(f32[64,1125]{1,0:T(8,128)S(1)} %collective-permute-done.1), channel_id=1, source_target_pairs={{0,2},{1,15},{2,4},{3,1},{4,6},{5,3},{6,8},{7,5},{8,10},{9,7},{10,... | collective-permute-start | bytes 864008 | tf_op jit(solution)/shard_map/ppermute | solution.py:26
  31.6 28.1 %collective-permute-start.6 = (f32[64,1125]{1,0:T(8,128)}, f32[64,1125]{1,0:T(8,128)}, u32[]{:S(2)}, u32[]{:S(2)}) collective-permute-start(f32[64,1125]{1,0:T(8,128)} %collective-permute-done.3), channel_id=1, source_target_pairs={{0,14},{1,3},{2,0},{3,5},{4,2},{5,7},{6,4},{7,9},{8,6},{9,11},{10,... | collective-permute-start | bytes 864008 | tf_op jit(solution)/shard_map/ppermute | solution.py:26
  43.7 17.6 %collective-permute-start.7 = (f32[64,1125]{1,0:T(8,128)}, f32[64,1125]{1,0:T(8,128)}, u32[]{:S(2)}, u32[]{:S(2)}) collective-permute-start(f32[64,1125]{1,0:T(8,128)} %collective-permute-done.5), channel_id=1, source_target_pairs={{0,2},{1,15},{2,4},{3,1},{4,6},{5,3},{6,8},{7,5},{8,10},{9,7},{10,... | collective-permute-start | bytes 864008 | tf_op jit(solution)/shard_map/ppermute | solution.py:26
  47.4 29.7 %all-to-all-start = ((f32[8,5,16,480]{3,2,1,0:T(8,128)}), f32[8,5,16,480]{3,2,1,0:T(8,128)S(1)}, u32[]{:S(2)}, u32[]{:S(2)}) async-start(f32[8,5,16,480]{3,2,1,0:T(8,128)} %bitcast.4), calls=%async_computation | async-start | bytes 2621440 | tf_op jit(solution)/shard_map/all_to_all | solution.py:91
  63.1 3.1 %copy-start.1 = (f32[192,1125]{1,0:T(8,128)S(1)}, f32[192,1125]{1,0:T(8,128)}, u32[]{:S(2)}) copy-start(f32[192,1125]{1,0:T(8,128)} %constant_dynamic-update-slice_fusion.5) | copy-start | bytes 2592004
  77.2 16.6 %all-to-all-start.1 = ((f32[8,3,16,480]{3,2,1,0:T(8,128)}), f32[8,3,16,480]{3,2,1,0:T(8,128)S(1)}, u32[]{:S(2)}, u32[]{:S(2)}) async-start(f32[8,3,16,480]{3,2,1,0:T(8,128)} %bitcast.9), calls=%async_computation.1 | async-start | bytes 1572864 | tf_op jit(solution)/shard_map/all_to_all | solution.py:91
  94.0 28.4 %copy-start.2 = (f32[60]{0:T(128)S(1)}, f32[60]{0:T(128)}, u32[]{:S(2)}) copy-start(f32[60]{0:T(128)} %param.7) | copy-start | bytes 724
  94.0 28.4 %copy-start.4 = (f32[16]{0:T(128)S(1)}, f32[16]{0:T(128)}, u32[]{:S(2)}) copy-start(f32[16]{0:T(128)} %param.8) | copy-start | bytes 196
  94.0 28.6 %copy-start.3 = (f32[128]{0:T(128)S(1)}, f32[128]{0:T(128)}, u32[]{:S(2)}) copy-start(f32[128]{0:T(128)} %param.9) | copy-start | bytes 1540
  94.1 8.3 %collective-permute-start.8 = (f32[2,4,16,480]{3,2,1,0:T(8,128)S(1)}, f32[2,4,16,480]{3,2,1,0:T(8,128)S(1)}, u32[]{:S(2)}, u32[]{:S(2)}) collective-permute-start(f32[2,4,16,480]{3,2,1,0:T(8,128)S(1)} %pad_maximum_fusion.2), channel_id=1, source_target_pairs={{0,64},{1,961},{2,66},{3,963},{4,68},{5,965},{6,70},{7,967},{8,72}... | collective-permute-start | bytes 737288 | tf_op jit(solution)/shard_map/ppermute | solution.py:26
  102.4 13.7 %collective-permute-start.9 = (f32[4,16,480]{2,1,0:T(8,128)S(1)}, f32[4,16,480]{2,1,0:T(8,128)S(1)}, u32[]{:S(2)}, u32[]{:S(2)}) collective-permute-start(f32[4,16,480]{2,1,0:T(8,128)S(1)} %slice_bitcast_fusion), channel_id=1, source_target_pairs={{0,960},{1,65},{2,962},{3,67},{4,964},{5,69},{6,966},{7,71},{8,968... | collective-permute-start | bytes 368648 | tf_op jit(solution)/shard_map/ppermute | solution.py:26
  116.7 20.1 %all-to-all-start.2 = ((f32[4,16,480]{2,1,0:T(8,128)}), f32[4,16,480]{2,1,0:T(8,128)S(1)}, u32[]{:S(2)}, u32[]{:S(2)}) async-start(f32[4,16,480]{2,1,0:T(8,128)} %fusion), calls=%async_computation.2 | async-start | bytes 262144 | tf_op jit(solution)/shard_map/all_to_all | solution.py:116

commit v4 on v2

--- a/solution.py
+++ b/solution.py
@@ -74,18 +74,26 @@
     block = jnp.pad(amplitudes.reshape(X, share, depth), ((0, 0), (0, 16 - share), (0, 0)))
     block = jnp.roll(block, -x, axis=0).reshape(X * 16, depth)
     f1 = send(block, along_y(1))
-    h1 = send(block, along_y(-1))
+    block_after, occupied_energy = lax.optimization_barrier((block, occupied_energy))
+    row_energy = (occupied_energy[None, :] - virtual_energy_rows[:, None]).reshape(-1)
+    col_energy = (occupied_energy[None, :] - virtual_energy_cols[:, None]).reshape(-1)
+    row_part = lax.dynamic_slice_in_dim(row_energy, wide * share, share)
+    col_part = lax.dynamic_slice_in_dim(col_energy, narrow * cols, cols)
+    denominator = row_part[:, None] + col_part[None, :]
+    block_after, denominator = lax.optimization_barrier((block_after, denominator))
+    h1 = send(block_after, along_y(-1))
     others = send(integrals, other_core)
     f2 = send(f1, along_y(1))
-    h2 = send(h1, along_y(-1))
+    nearest = jnp.concatenate([block, f1], 0)
+    h1_after, nearest = lax.optimization_barrier((h1, nearest))
+    h2 = send(h1_after, along_y(-1))
 
-    def messages(blocks):
-        tall = jnp.concatenate(blocks, 0)
+    def messages(tall):
         halves = [
             jnp.dot(tall, part, precision=lax.Precision.HIGH, preferred_element_type=jnp.float32)
             for part in (integrals, others)
         ]
-        halves = jnp.stack([half.reshape(len(blocks), X, 16, cols) for half in halves], 1)
+        halves = jnp.stack([half.reshape(-1, X, 16, cols) for half in halves], 1)
         return [halves[:, :, place] for place in range(X)]
 
     def sum_over_x(parts):
@@ -93,12 +101,13 @@
 
     f2, others = lax.optimization_barrier((f2, others))
     f3 = send(f2, along_y(1))
-    h3 = send(h2, along_y(-1))
-    early = messages((block, f1, h1, f2, h2))
+    h2_after, _ = lax.optimization_barrier((h2, f2))
+    h3 = send(h2_after, along_y(-1))
+    early = messages(jnp.concatenate([nearest, h1, f2, h2], 0))
     f3, early = lax.optimization_barrier((f3, early))
     f4 = send(f3, along_y(1))
     first = sum_over_x(early)
-    second = sum_over_x(messages((f3, h3, f4)))
+    second = sum_over_x(messages(jnp.concatenate([f3, h3, f4], 0)))
     pieces = jnp.stack(
         [first[0], first[3], second[2], first[4], first[1], first[2], second[0], second[1]], 1
     )
@@ -117,11 +126,7 @@
     cycle_term = spread[0] + spread[1] + spread[2] + spread[3]
     cycle_term = cycle_term[:share]
 
-    row_energy = (occupied_energy[None, :] - virtual_energy_rows[:, None]).reshape(-1)
-    col_energy = (occupied_energy[None, :] - virtual_energy_cols[:, None]).reshape(-1)
-    row_part = lax.dynamic_slice_in_dim(row_energy, wide * share, share)
-    col_part = lax.dynamic_slice_in_dim(col_energy, narrow * cols, cols)
-    return cycle_term / (row_part[:, None] + col_part[None, :])
+    return cycle_term / denominator
 
 
 def solution(mesh):

time: 128 us -> 127 us (level)
  the two profiles are of different devices: /device:TPU:2 before, /device:TPU:70 now
where the time goes in v4:
time: 127 us; the launch traced here: 126 us
  starting transfers between devices  68.4 us (54%)
  blocking collectives  25.4 us (20%)
  waiting for transfers between devices  23 us (18%)
  matrix products  5.42 us (4%)
  local copies, waits for them, and re-layouts  1.71 us (1%)
  other arithmetic  1.4 us (1%)
    ppermute x18, starting transfers between devices, send(): return lax.ppermute(array, AXES, table(move))  68.4 us
    all_to_all x1, blocking collectives, per_device(): lax.all_to_all(total, AXES, 0, 0, tiled=True, axis_index_groups=classes())  25.4 us
    ppermute x18, waiting for transfers between devices, send(): return lax.ppermute(array, AXES, table(move))  23 us
    dot_general x4, matrix products, messages(): jnp.dot(tall, part, precision=lax.Precision.HIGH, preferred_element_type=...  5.42 us
  transfers between devices with their start and end apart: 18, of which 7 were waited for; matrix products, arithmetic and copies ran while one was open for 6% of the time, Pallas kernels for 0%

profile of v4, /device:TPU:70, one launch (start us, length us, event | category | flops | bytes accessed | tf_op | source)
XLA Modules:
  0.0 126.0 jit_solution(17376073609707232090)
XLA Ops:
  0.0 0.0 copy-start.1
  0.0 0.0 copy-start.2
  0.0 0.0 copy-start.3
  0.0 2.1 %collective-permute-start.2 = (f32[1125,480]{0,1:T(8,128)}, f32[1125,480]{0,1:T(8,128)S(1)}, u32[]{:S(2)}, u32[]{:S(2)}) collective-permute-start(f32[1125,480]{0,1:T(8,128)} %param.6), channel_id=1, source_target_pairs={{0,1},{1,0},{2,3},{3,2},{4,5},{5,4},{6,7},{7,6},{8,9},{9,8},{10,11... | collective-permute-start | bytes 6480008 | tf_op jit(solution)/shard_map/ppermute | solution.py:26
  2.1 1.0 reshape.38
  3.1 0.1 fusion.7
  3.2 3.5 %collective-permute-start = (f32[64,1125]{1,0:T(8,128)S(1)}, f32[64,1125]{1,0:T(8,128)S(1)}, u32[]{:S(2)}, u32[]{:S(2)}) collective-permute-start(f32[64,1125]{1,0:T(8,128)S(1)} %bitcast.109), channel_id=1, source_target_pairs={{0,2},{1,15},{2,4},{3,1},{4,6},{5,3},{6,8},{7,5},{8,10},{9,7},{10,... | collective-permute-start | bytes 864008 | tf_op jit(solution)/shard_map/ppermute | solution.py:26
  6.7 0.0 copy-done.1
  6.7 0.0 copy-done.2
  6.7 0.1 broadcast_subtract_fusion
  6.8 0.0 copy-done.3
  6.8 0.1 broadcast_subtract_fusion.1
  6.9 0.1 sub.52
  7.0 0.1 sub.56
  7.1 0.1 dynamic_slice.23
  7.2 0.1 dynamic_slice.24
  7.3 0.1 broadcast_add_fusion
  7.3 3.8 %collective-permute-start.4 = (f32[64,1125]{1,0:T(8,128)S(1)}, f32[64,1125]{1,0:T(8,128)S(1)}, u32[]{:S(2)}, u32[]{:S(2)}) collective-permute-start(f32[64,1125]{1,0:T(8,128)S(1)} %bitcast.110), channel_id=1, source_target_pairs={{0,14},{1,3},{2,0},{3,5},{4,2},{5,7},{6,4},{7,9},{8,6},{9,11},{10,... | collective-permute-start | bytes 864008 | tf_op jit(solution)/shard_map/ppermute | solution.py:26
  11.2 2.0 %collective-permute-done = f32[64,1125]{1,0:T(8,128)S(1)} collective-permute-done((f32[64,1125]{1,0:T(8,128)S(1)}, f32[64,1125]{1,0:T(8,128)S(1)}, u32[]{:S(2)}, u32[]{:S(2)}) %collective-permute-start) | collective-permute-done | bytes 288032 | tf_op jit(solution)/shard_map/ppermute | solution.py:26
  13.3 0.0 copy-start
  13.3 2.6 %collective-permute-done.4 = f32[64,1125]{1,0:T(8,128)S(1)} collective-permute-done((f32[64,1125]{1,0:T(8,128)S(1)}, f32[64,1125]{1,0:T(8,128)S(1)}, u32[]{:S(2)}, u32[]{:S(2)}) %collective-permute-start.4) | collective-permute-done | bytes 288032 | tf_op jit(solution)/shard_map/ppermute | solution.py:26
  15.9 5.2 %collective-permute-start.5 = (f32[64,1125]{1,0:T(8,128)S(1)}, f32[64,1125]{1,0:T(8,128)S(1)}, u32[]{:S(2)}, u32[]{:S(2)}) collective-permute-start(f32[64,1125]{1,0:T(8,128)S(1)} %collective-permute-done.4), channel_id=1, source_target_pairs={{0,14},{1,3},{2,0},{3,5},{4,2},{5,7},{6,4},{7,9},{8,6},{9,11},{10,... | collective-permute-start | bytes 864008 | tf_op jit(solution)/shard_map/ppermute | solution.py:26
  21.1 1.9 %collective-permute-start.1 = (f32[64,1125]{1,0:T(8,128)S(1)}, f32[64,1125]{1,0:T(8,128)S(1)}, u32[]{:S(2)}, u32[]{:S(2)}) collective-permute-start(f32[64,1125]{1,0:T(8,128)S(1)} %collective-permute-done), channel_id=1, source_target_pairs={{0,2},{1,15},{2,4},{3,1},{4,6},{5,3},{6,8},{7,5},{8,10},{9,7},{10,... | collective-permute-start | bytes 864008 | tf_op jit(solution)/shard_map/ppermute | solution.py:26
  23.1 7.8 %collective-permute-done.1 = f32[64,1125]{1,0:T(8,128)S(1)} collective-permute-done((f32[64,1125]{1,0:T(8,128)S(1)}, f32[64,1125]{1,0:T(8,128)S(1)}, u32[]{:S(2)}, u32[]{:S(2)}) %collective-permute-start.1) | collective-permute-done | bytes 288032 | tf_op jit(solution)/shard_map/ppermute | solution.py:26
  30.9 0.0 collective-permute-done.2
  30.9 1.9 %collective-permute-start.3 = (f32[64,1125]{1,0:T(8,128)S(1)}, f32[64,1125]{1,0:T(8,128)S(1)}, u32[]{:S(2)}, u32[]{:S(2)}) collective-permute-start(f32[64,1125]{1,0:T(8,128)S(1)} %collective-permute-done.1), channel_id=1, source_target_pairs={{0,2},{1,15},{2,4},{3,1},{4,6},{5,3},{6,8},{7,5},{8,10},{9,7},{10,... | collective-permute-start | bytes 864008 | tf_op jit(solution)/shard_map/ppermute | solution.py:26
  32.9 0.0 collective-permute-done.5
  32.9 5.1 %collective-permute-start.9 = (f32[64,1125]{1,0:T(8,128)S(1)}, f32[64,1125]{1,0:T(8,128)S(1)}, u32[]{:S(2)}, u32[]{:S(2)}) collective-permute-start(f32[64,1125]{1,0:T(8,128)S(1)} %collective-permute-done.5), channel_id=1, source_target_pairs={{0,14},{1,3},{2,0},{3,5},{4,2},{5,7},{6,4},{7,9},{8,6},{9,11},{10,... | collective-permute-start | bytes 864008 | tf_op jit(solution)/shard_map/ppermute | solution.py:26
  38.1 0.0 copy-done
  38.1 1.6 %fusion.25 = f32[320,480]{1,0:T(8,128)S(1)} fusion(f32[320,1125]{1,0:T(8,128)S(1)} %constant_dynamic-update-slice_fusion, f32[1125,480]{0,1:T(8,128)S(1)} %copy-done), kind=kOutput, calls=%fused_computation.73 | convolution fusion | flops 1036800000 | bytes 4214400 | tf_op jit(solution)/shard_map/dot_general | solution.py:93
  39.6 1.5 %fusion.26 = f32[320,480]{1,0:T(8,128)S(1)} fusion(f32[320,1125]{1,0:T(8,128)S(1)} %constant_dynamic-update-slice_fusion, f32[1125,480]{0,1:T(8,128)S(1)} %collective-permute-done.2), kind=kOutput, calls=%fused_computation.74 | convolution fusion | flops 1036800000 | bytes 4214400 | tf_op jit(solution)/shard_map/dot_general | solution.py:93
  41.1 0.2 fusion.6
  41.3 0.8 collective-permute-done.3
  42.1 1.9 %collective-permute-start.10 = (f32[64,1125]{1,0:T(8,128)S(1)}, f32[64,1125]{1,0:T(8,128)S(1)}, u32[]{:S(2)}, u32[]{:S(2)}) collective-permute-start(f32[64,1125]{1,0:T(8,128)S(1)} %collective-permute-done.3), channel_id=1, source_target_pairs={{0,2},{1,15},{2,4},{3,1},{4,6},{5,3},{6,8},{7,5},{8,10},{9,7},{10,... | collective-permute-start | bytes 864008 | tf_op jit(solution)/shard_map/ppermute | solution.py:26
  44.0 2.4 %collective-permute-start.6 = (f32[5,2,16,480]{3,2,0,1:T(8,128)S(1)}, f32[5,2,16,480]{3,2,0,1:T(8,128)S(1)}, u32[]{:S(2)}, u32[]{:S(2)}) collective-permute-start(f32[5,2,16,480]{3,2,0,1:T(8,128)S(1)} %get-tuple-element.27), channel_id=1, source_target_pairs={{0,16},{1,17},{2,18},{3,19},{4,20},{5,21},{6,22},{7,23},{8,24},{9,... | collective-permute-start | bytes 921608 | tf_op jit(solution)/shard_map/ppermute | solution.py:26
  46.4 3.5 %collective-permute-start.7 = (f32[5,2,16,480]{3,2,0,1:T(8,128)S(1)}, f32[5,2,16,480]{3,2,0,1:T(8,128)S(1)}, u32[]{:S(2)}, u32[]{:S(2)}) collective-permute-start(f32[5,2,16,480]{3,2,0,1:T(8,128)S(1)} %get-tuple-element.28), channel_id=1, source_target_pairs={{0,48},{1,49},{2,50},{3,51},{4,52},{5,53},{6,54},{7,55},{8,56},{9,... | collective-permute-start | bytes 921608 | tf_op jit(solution)/shard_map/ppermute | solution.py:26
  49.9 3.3 %collective-permute-start.8 = (f32[5,2,16,480]{3,2,0,1:T(8,128)S(1)}, f32[5,2,16,480]{3,2,0,1:T(8,128)S(1)}, u32[]{:S(2)}, u32[]{:S(2)}) collective-permute-start(f32[5,2,16,480]{3,2,0,1:T(8,128)S(1)} %get-tuple-element.29), channel_id=1, source_target_pairs={{0,32},{1,33},{2,34},{3,35},{4,36},{5,37},{6,38},{7,39},{8,40},{9,... | collective-permute-start | bytes 921608 | tf_op jit(solution)/shard_map/ppermute | solution.py:26
  53.2 0.0 collective-permute-done.9
  53.2 0.0 collective-permute-done.10
  53.3 1.2 fusion.28
  54.4 1.2 fusion.27
  55.7 0.1 fusion.9
  55.8 3.0 %collective-permute-start.12 = (f32[3,2,16,480]{3,2,1,0:T(8,128)S(1)}, f32[3,2,16,480]{3,2,1,0:T(8,128)S(1)}, u32[]{:S(2)}, u32[]{:S(2)}) collective-permute-start(f32[3,2,16,480]{3,2,1,0:T(8,128)S(1)} %bitcast.115), channel_id=1, source_target_pairs={{0,48},{1,49},{2,50},{3,51},{4,52},{5,53},{6,54},{7,55},{8,56},{9,... | collective-permute-start | bytes 552968 | tf_op jit(solution)/shard_map/ppermute | solution.py:26
  58.9 4.3 %collective-permute-start.13 = (f32[3,2,16,480]{3,2,1,0:T(8,128)S(1)}, f32[3,2,16,480]{3,2,1,0:T(8,128)S(1)}, u32[]{:S(2)}, u32[]{:S(2)}) collective-permute-start(f32[3,2,16,480]{3,2,1,0:T(8,128)S(1)} %bitcast.114), channel_id=1, source_target_pairs={{0,32},{1,33},{2,34},{3,35},{4,36},{5,37},{6,38},{7,39},{8,40},{9,... | collective-permute-start | bytes 552968 | tf_op jit(solution)/shard_map/ppermute | solution.py:26
  63.2 0.0 collective-permute-done.6
  63.2 3.1 %collective-permute-start.11 = (f32[3,2,16,480]{3,2,1,0:T(8,128)S(1)}, f32[3,2,16,480]{3,2,1,0:T(8,128)S(1)}, u32[]{:S(2)}, u32[]{:S(2)}) collective-permute-start(f32[3,2,16,480]{3,2,1,0:T(8,128)S(1)} %bitcast.113), channel_id=1, source_target_pairs={{0,16},{1,17},{2,18},{3,19},{4,20},{5,21},{6,22},{7,23},{8,24},{9,... | collective-permute-start | bytes 552968 | tf_op jit(solution)/shard_map/ppermute | solution.py:26
  66.3 0.0 collective-permute-done.7
  66.3 0.6 collective-permute-done.8
  67.0 0.1 add_add_fusion
  67.1 6.7 %collective-permute-done.12 = f32[3,2,16,480]{3,2,1,0:T(8,128)S(1)} collective-permute-done((f32[3,2,16,480]{3,2,1,0:T(8,128)S(1)}, f32[3,2,16,480]{3,2,1,0:T(8,128)S(1)}, u32[]{:S(2)}, u32[]{:S(2)}) %collective-permute-start.12) | collective-permute-done | bytes 184352 | tf_op jit(solution)/shard_map/ppermute | solution.py:26
  73.8 0.0 collective-permute-done.13
  73.8 0.0 collective-permute-done.11
  73.8 0.1 fusion.13
  73.9 0.1 dynamic-slice_bitcast_fusion.2
  74.0 3.9 %collective-permute-start.15 = (f32[4,16,480]{2,1,0:T(8,128)S(1)}, f32[4,16,480]{2,1,0:T(8,128)S(1)}, u32[]{:S(2)}, u32[]{:S(2)}) collective-permute-start(f32[4,16,480]{2,1,0:T(8,128)S(1)} %get-tuple-element.41), channel_id=1, source_target_pairs={{0,0},{1,65},{2,2},{3,67},{4,4},{5,69},{6,6},{7,71},{8,8},{9,73},{... | collective-permute-start | bytes 368648 | tf_op jit(solution)/shard_map/ppermute | solution.py:26
  77.9 10.6 %collective-permute-start.16 = (f32[4,16,480]{2,1,0:T(8,128)S(1)}, f32[4,16,480]{2,1,0:T(8,128)S(1)}, u32[]{:S(2)}, u32[]{:S(2)}) collective-permute-start(f32[4,16,480]{2,1,0:T(8,128)S(1)} %get-tuple-element.42), channel_id=1, source_target_pairs={{0,897},{1,960},{2,899},{3,962},{4,901},{5,964},{6,903},{7,966},{8... | collective-permute-start | bytes 368648 | tf_op jit(solution)/shard_map/ppermute | solution.py:26
  88.5 1.9 %collective-permute-start.14 = (f32[4,16,480]{2,1,0:T(8,128)S(1)}, f32[4,16,480]{2,1,0:T(8,128)S(1)}, u32[]{:S(2)}, u32[]{:S(2)}) collective-permute-start(f32[4,16,480]{2,1,0:T(8,128)S(1)} %get-tuple-element.43), channel_id=1, source_target_pairs={{0,1},{1,64},{2,3},{3,66},{4,5},{5,68},{6,7},{7,70},{8,9},{9,72},{... | collective-permute-start | bytes 368648 | tf_op jit(solution)/shard_map/ppermute | solution.py:26
  90.4 7.0 %collective-permute-start.17 = (f32[4,16,480]{2,1,0:T(8,128)S(1)}, f32[4,16,480]{2,1,0:T(8,128)S(1)}, u32[]{:S(2)}, u32[]{:S(2)}) collective-permute-start(f32[4,16,480]{2,1,0:T(8,128)S(1)} %get-tuple-element.44), channel_id=1, source_target_pairs={{0,896},{1,961},{2,898},{3,963},{4,900},{5,965},{6,902},{7,967},{8... | collective-permute-start | bytes 368648 | tf_op jit(solution)/shard_map/ppermute | solution.py:26
  97.4 0.0 collective-permute-done.15
  97.4 0.0 collective-permute-done.16
  97.4 2.5 %collective-permute-done.14 = f32[4,16,480]{2,1,0:T(8,128)S(1)} collective-permute-done((f32[4,16,480]{2,1,0:T(8,128)S(1)}, f32[4,16,480]{2,1,0:T(8,128)S(1)}, u32[]{:S(2)}, u32[]{:S(2)}) %collective-permute-start.14) | collective-permute-done | bytes 122912 | tf_op jit(solution)/shard_map/ppermute | solution.py:26
  99.9 0.0 collective-permute-done.17
  99.9 25.4 %all_to_all.5 = f32[4,16,480]{2,1,0:T(8,128)S(1)} all-to-all(f32[4,16,480]{2,1,0:T(8,128)S(1)} %add_add_fusion.1), channel_id=1, replica_groups={{0,768,512,256},{1,769,513,257},{2,258,770,514},{3,259,771,515},{260,4,..., dimensions={0} | all-to-all | bytes 245760 | tf_op jit(solution)/shard_map/all_to_all | solution.py:125
  125.3 0.6 fusion.23
  (22 shorter events, 0.4 us)
Async XLA Ops:
  0.0 6.7 %copy-start.1 = (f32[60]{0:T(128)S(1)}, f32[60]{0:T(128)}, u32[]{:S(2)}) copy-start(f32[60]{0:T(128)} %param.7) | copy-start | bytes 724
  0.0 6.7 %copy-start.2 = (f32[128]{0:T(128)S(1)}, f32[128]{0:T(128)}, u32[]{:S(2)}) copy-start(f32[128]{0:T(128)} %param.9) | copy-start | bytes 1540
  0.0 6.8 %copy-start.3 = (f32[16]{0:T(128)S(1)}, f32[16]{0:T(128)}, u32[]{:S(2)}) copy-start(f32[16]{0:T(128)} %param.8) | copy-start | bytes 196
  0.0 30.9 %collective-permute-start.2 = (f32[1125,480]{0,1:T(8,128)}, f32[1125,480]{0,1:T(8,128)S(1)}, u32[]{:S(2)}, u32[]{:S(2)}) collective-permute-start(f32[1125,480]{0,1:T(8,128)} %param.6), channel_id=1, source_target_pairs={{0,1},{1,0},{2,3},{3,2},{4,5},{5,4},{6,7},{7,6},{8,9},{9,8},{10,11... | collective-permute-start | bytes 6480008 | tf_op jit(solution)/shard_map/ppermute | solution.py:26
  3.2 10.1 %collective-permute-start = (f32[64,1125]{1,0:T(8,128)S(1)}, f32[64,1125]{1,0:T(8,128)S(1)}, u32[]{:S(2)}, u32[]{:S(2)}) collective-permute-start(f32[64,1125]{1,0:T(8,128)S(1)} %bitcast.109), channel_id=1, source_target_pairs={{0,2},{1,15},{2,4},{3,1},{4,6},{5,3},{6,8},{7,5},{8,10},{9,7},{10,... | collective-permute-start | bytes 864008 | tf_op jit(solution)/shard_map/ppermute | solution.py:26
  7.3 8.6 %collective-permute-start.4 = (f32[64,1125]{1,0:T(8,128)S(1)}, f32[64,1125]{1,0:T(8,128)S(1)}, u32[]{:S(2)}, u32[]{:S(2)}) collective-permute-start(f32[64,1125]{1,0:T(8,128)S(1)} %bitcast.110), channel_id=1, source_target_pairs={{0,14},{1,3},{2,0},{3,5},{4,2},{5,7},{6,4},{7,9},{8,6},{9,11},{10,... | collective-permute-start | bytes 864008 | tf_op jit(solution)/shard_map/ppermute | solution.py:26
  13.3 24.7 %copy-start = (f32[1125,480]{0,1:T(8,128)S(1)}, f32[1125,480]{0,1:T(8,128)}, u32[]{:S(2)}) copy-start(f32[1125,480]{0,1:T(8,128)} %param.6) | copy-start | bytes 6480004
  15.9 17.0 %collective-permute-start.5 = (f32[64,1125]{1,0:T(8,128)S(1)}, f32[64,1125]{1,0:T(8,128)S(1)}, u32[]{:S(2)}, u32[]{:S(2)}) collective-permute-start(f32[64,1125]{1,0:T(8,128)S(1)} %collective-permute-done.4), channel_id=1, source_target_pairs={{0,14},{1,3},{2,0},{3,5},{4,2},{5,7},{6,4},{7,9},{8,6},{9,11},{10,... | collective-permute-start | bytes 864008 | tf_op jit(solution)/shard_map/ppermute | solution.py:26
  21.1 9.8 %collective-permute-start.1 = (f32[64,1125]{1,0:T(8,128)S(1)}, f32[64,1125]{1,0:T(8,128)S(1)}, u32[]{:S(2)}, u32[]{:S(2)}) collective-permute-start(f32[64,1125]{1,0:T(8,128)S(1)} %collective-permute-done), channel_id=1, source_target_pairs={{0,2},{1,15},{2,4},{3,1},{4,6},{5,3},{6,8},{7,5},{8,10},{9,7},{10,... | collective-permute-start | bytes 864008 | tf_op jit(solution)/shard_map/ppermute | solution.py:26
  30.9 11.1 %collective-permute-start.3 = (f32[64,1125]{1,0:T(8,128)S(1)}, f32[64,1125]{1,0:T(8,128)S(1)}, u32[]{:S(2)}, u32[]{:S(2)}) collective-permute-start(f32[64,1125]{1,0:T(8,128)S(1)} %collective-permute-done.1), channel_id=1, source_target_pairs={{0,2},{1,15},{2,4},{3,1},{4,6},{5,3},{6,8},{7,5},{8,10},{9,7},{10,... | collective-permute-start | bytes 864008 | tf_op jit(solution)/shard_map/ppermute | solution.py:26
  32.9 20.3 %collective-permute-start.9 = (f32[64,1125]{1,0:T(8,128)S(1)}, f32[64,1125]{1,0:T(8,128)S(1)}, u32[]{:S(2)}, u32[]{:S(2)}) collective-permute-start(f32[64,1125]{1,0:T(8,128)S(1)} %collective-permute-done.5), channel_id=1, source_target_pairs={{0,14},{1,3},{2,0},{3,5},{4,2},{5,7},{6,4},{7,9},{8,6},{9,11},{10,... | collective-permute-start | bytes 864008 | tf_op jit(solution)/shard_map/ppermute | solution.py:26
  42.1 11.2 %collective-permute-start.10 = (f32[64,1125]{1,0:T(8,128)S(1)}, f32[64,1125]{1,0:T(8,128)S(1)}, u32[]{:S(2)}, u32[]{:S(2)}) collective-permute-start(f32[64,1125]{1,0:T(8,128)S(1)} %collective-permute-done.3), channel_id=1, source_target_pairs={{0,2},{1,15},{2,4},{3,1},{4,6},{5,3},{6,8},{7,5},{8,10},{9,7},{10,... | collective-permute-start | bytes 864008 | tf_op jit(solution)/shard_map/ppermute | solution.py:26
  44.0 19.2 %collective-permute-start.6 = (f32[5,2,16,480]{3,2,0,1:T(8,128)S(1)}, f32[5,2,16,480]{3,2,0,1:T(8,128)S(1)}, u32[]{:S(2)}, u32[]{:S(2)}) collective-permute-start(f32[5,2,16,480]{3,2,0,1:T(8,128)S(1)} %get-tuple-element.27), channel_id=1, source_target_pairs={{0,16},{1,17},{2,18},{3,19},{4,20},{5,21},{6,22},{7,23},{8,24},{9,... | collective-permute-start | bytes 921608 | tf_op jit(solution)/shard_map/ppermute | solution.py:26
  46.4 19.9 %collective-permute-start.7 = (f32[5,2,16,480]{3,2,0,1:T(8,128)S(1)}, f32[5,2,16,480]{3,2,0,1:T(8,128)S(1)}, u32[]{:S(2)}, u32[]{:S(2)}) collective-permute-start(f32[5,2,16,480]{3,2,0,1:T(8,128)S(1)} %get-tuple-element.28), channel_id=1, source_target_pairs={{0,48},{1,49},{2,50},{3,51},{4,52},{5,53},{6,54},{7,55},{8,56},{9,... | collective-permute-start | bytes 921608 | tf_op jit(solution)/shard_map/ppermute | solution.py:26
  49.9 17.1 %collective-permute-start.8 = (f32[5,2,16,480]{3,2,0,1:T(8,128)S(1)}, f32[5,2,16,480]{3,2,0,1:T(8,128)S(1)}, u32[]{:S(2)}, u32[]{:S(2)}) collective-permute-start(f32[5,2,16,480]{3,2,0,1:T(8,128)S(1)} %get-tuple-element.29), channel_id=1, source_target_pairs={{0,32},{1,33},{2,34},{3,35},{4,36},{5,37},{6,38},{7,39},{8,40},{9,... | collective-permute-start | bytes 921608 | tf_op jit(solution)/shard_map/ppermute | solution.py:26
  55.8 18.0 %collective-permute-start.12 = (f32[3,2,16,480]{3,2,1,0:T(8,128)S(1)}, f32[3,2,16,480]{3,2,1,0:T(8,128)S(1)}, u32[]{:S(2)}, u32[]{:S(2)}) collective-permute-start(f32[3,2,16,480]{3,2,1,0:T(8,128)S(1)} %bitcast.115), channel_id=1, source_target_pairs={{0,48},{1,49},{2,50},{3,51},{4,52},{5,53},{6,54},{7,55},{8,56},{9,... | collective-permute-start | bytes 552968 | tf_op jit(solution)/shard_map/ppermute | solution.py:26
  58.9 14.9 %collective-permute-start.13 = (f32[3,2,16,480]{3,2,1,0:T(8,128)S(1)}, f32[3,2,16,480]{3,2,1,0:T(8,128)S(1)}, u32[]{:S(2)}, u32[]{:S(2)}) collective-permute-start(f32[3,2,16,480]{3,2,1,0:T(8,128)S(1)} %bitcast.114), channel_id=1, source_target_pairs={{0,32},{1,33},{2,34},{3,35},{4,36},{5,37},{6,38},{7,39},{8,40},{9,... | collective-permute-start | bytes 552968 | tf_op jit(solution)/shard_map/ppermute | solution.py:26
  63.2 10.6 %collective-permute-start.11 = (f32[3,2,16,480]{3,2,1,0:T(8,128)S(1)}, f32[3,2,16,480]{3,2,1,0:T(8,128)S(1)}, u32[]{:S(2)}, u32[]{:S(2)}) collective-permute-start(f32[3,2,16,480]{3,2,1,0:T(8,128)S(1)} %bitcast.113), channel_id=1, source_target_pairs={{0,16},{1,17},{2,18},{3,19},{4,20},{5,21},{6,22},{7,23},{8,24},{9,... | collective-permute-start | bytes 552968 | tf_op jit(solution)/shard_map/ppermute | solution.py:26
  74.0 23.4 %collective-permute-start.15 = (f32[4,16,480]{2,1,0:T(8,128)S(1)}, f32[4,16,480]{2,1,0:T(8,128)S(1)}, u32[]{:S(2)}, u32[]{:S(2)}) collective-permute-start(f32[4,16,480]{2,1,0:T(8,128)S(1)} %get-tuple-element.41), channel_id=1, source_target_pairs={{0,0},{1,65},{2,2},{3,67},{4,4},{5,69},{6,6},{7,71},{8,8},{9,73},{... | collective-permute-start | bytes 368648 | tf_op jit(solution)/shard_map/ppermute | solution.py:26
  77.9 19.5 %collective-permute-start.16 = (f32[4,16,480]{2,1,0:T(8,128)S(1)}, f32[4,16,480]{2,1,0:T(8,128)S(1)}, u32[]{:S(2)}, u32[]{:S(2)}) collective-permute-start(f32[4,16,480]{2,1,0:T(8,128)S(1)} %get-tuple-element.42), channel_id=1, source_target_pairs={{0,897},{1,960},{2,899},{3,962},{4,901},{5,964},{6,903},{7,966},{8... | collective-permute-start | bytes 368648 | tf_op jit(solution)/shard_map/ppermute | solution.py:26
  88.5 11.4 %collective-permute-start.14 = (f32[4,16,480]{2,1,0:T(8,128)S(1)}, f32[4,16,480]{2,1,0:T(8,128)S(1)}, u32[]{:S(2)}, u32[]{:S(2)}) collective-permute-start(f32[4,16,480]{2,1,0:T(8,128)S(1)} %get-tuple-element.43), channel_id=1, source_target_pairs={{0,1},{1,64},{2,3},{3,66},{4,5},{5,68},{6,7},{7,70},{8,9},{9,72},{... | collective-permute-start | bytes 368648 | tf_op jit(solution)/shard_map/ppermute | solution.py:26
  90.4 9.5 %collective-permute-start.17 = (f32[4,16,480]{2,1,0:T(8,128)S(1)}, f32[4,16,480]{2,1,0:T(8,128)S(1)}, u32[]{:S(2)}, u32[]{:S(2)}) collective-permute-start(f32[4,16,480]{2,1,0:T(8,128)S(1)} %get-tuple-element.44), channel_id=1, source_target_pairs={{0,896},{1,961},{2,898},{3,963},{4,900},{5,965},{6,902},{7,967},{8... | collective-permute-start | bytes 368648 | tf_op jit(solution)/shard_map/ppermute | solution.py:26

commit v5 on v2

--- a/solution.py
+++ b/solution.py
@@ -91,14 +91,13 @@
     def sum_over_x(parts):
         return parts[0] + send(parts[1], along_x(1)) + send(parts[3], along_x(-1)) + send(parts[2], along_x(2))
 
-    f2, others = lax.optimization_barrier((f2, others))
     f3 = send(f2, along_y(1))
     h3 = send(h2, along_y(-1))
     early = messages((block, f1, h1, f2, h2))
-    f3, early = lax.optimization_barrier((f3, early))
-    f4 = send(f3, along_y(1))
+    h3_after, early = lax.optimization_barrier((h3, early))
+    h4 = send(h3_after, along_y(-1))
     first = sum_over_x(early)
-    second = sum_over_x(messages((f3, h3, f4)))
+    second = sum_over_x(messages((f3, h3, h4)))
     pieces = jnp.stack(
         [first[0], first[3], second[2], first[4], first[1], first[2], second[0], second[1]], 1
     )

time: 128 us -> 127 us (level)
  the two profiles are of different devices: /device:TPU:2 before, /device:TPU:1 now
where the time goes in v5:
time: 127 us; the launch traced here: 126 us
  starting transfers between devices  81.9 us (64%)
  waiting for transfers between devices  34.5 us (27%)
  matrix products  5.42 us (4%)
  other arithmetic  2 us (2%)
  local copies, waits for them, and re-layouts  1.72 us (1%)
    ppermute x18, starting transfers between devices, send(): return lax.ppermute(array, AXES, table(move))  78.5 us
    ppermute x18, waiting for transfers between devices, send(): return lax.ppermute(array, AXES, table(move))  20.5 us
    all_to_all x1, waiting for transfers between devices, per_device(): lax.all_to_all(total, AXES, 0, 0, tiled=True, axis_index_groups=classes())  14 us
    dot_general x4, matrix products, messages(): jnp.dot(tall, part, precision=lax.Precision.HIGH, preferred_element_type=...  5.42 us
    all_to_all x1, starting transfers between devices, per_device(): lax.all_to_all(total, AXES, 0, 0, tiled=True, axis_index_groups=classes())  3.32 us
  transfers between devices with their start and end apart: 19, of which 10 were waited for; matrix products, arithmetic and copies ran while one was open for 6% of the time, Pallas kernels for 0%

profile of v5, /device:TPU:1, one launch (start us, length us, event | category | flops | bytes accessed | tf_op | source)
XLA Modules:
  0.0 126.2 jit_solution(12440910036215884076)
XLA Ops:
  0.0 16.1 %collective-permute-start.5 = (f32[1125,480]{0,1:T(8,128)}, f32[1125,480]{0,1:T(8,128)S(1)}, u32[]{:S(2)}, u32[]{:S(2)}) collective-permute-start(f32[1125,480]{0,1:T(8,128)} %param.6), channel_id=1, source_target_pairs={{0,1},{1,0},{2,3},{3,2},{4,5},{5,4},{6,7},{7,6},{8,9},{9,8},{10,11... | collective-permute-start | bytes 6480008 | tf_op jit(solution)/shard_map/ppermute | solution.py:26
  16.1 1.0 reshape.38
  17.1 0.1 fusion.7
  17.2 1.9 %collective-permute-start = (f32[64,1125]{1,0:T(8,128)S(1)}, f32[64,1125]{1,0:T(8,128)S(1)}, u32[]{:S(2)}, u32[]{:S(2)}) collective-permute-start(f32[64,1125]{1,0:T(8,128)S(1)} %bitcast.109), channel_id=1, source_target_pairs={{0,14},{1,3},{2,0},{3,5},{4,2},{5,7},{6,4},{7,9},{8,6},{9,11},{10,... | collective-permute-start | bytes 864008 | tf_op jit(solution)/shard_map/ppermute | solution.py:26
  19.1 4.6 %collective-permute-start.3 = (f32[64,1125]{1,0:T(8,128)S(1)}, f32[64,1125]{1,0:T(8,128)S(1)}, u32[]{:S(2)}, u32[]{:S(2)}) collective-permute-start(f32[64,1125]{1,0:T(8,128)S(1)} %bitcast.110), channel_id=1, source_target_pairs={{0,2},{1,15},{2,4},{3,1},{4,6},{5,3},{6,8},{7,5},{8,10},{9,7},{10,... | collective-permute-start | bytes 864008 | tf_op jit(solution)/shard_map/ppermute | solution.py:26
  23.8 0.0 copy-start
  23.9 3.0 %collective-permute-done = f32[64,1125]{1,0:T(8,128)S(1)} collective-permute-done((f32[64,1125]{1,0:T(8,128)S(1)}, f32[64,1125]{1,0:T(8,128)S(1)}, u32[]{:S(2)}, u32[]{:S(2)}) %collective-permute-start) | collective-permute-done | bytes 288032 | tf_op jit(solution)/shard_map/ppermute | solution.py:26
  26.9 1.9 %collective-permute-start.1 = (f32[64,1125]{1,0:T(8,128)S(1)}, f32[64,1125]{1,0:T(8,128)S(1)}, u32[]{:S(2)}, u32[]{:S(2)}) collective-permute-start(f32[64,1125]{1,0:T(8,128)S(1)} %collective-permute-done), channel_id=1, source_target_pairs={{0,14},{1,3},{2,0},{3,5},{4,2},{5,7},{6,4},{7,9},{8,6},{9,11},{10,... | collective-permute-start | bytes 864008 | tf_op jit(solution)/shard_map/ppermute | solution.py:26
  28.8 0.0 collective-permute-done.3
  28.8 4.6 %collective-permute-start.4 = (f32[64,1125]{1,0:T(8,128)S(1)}, f32[64,1125]{1,0:T(8,128)S(1)}, u32[]{:S(2)}, u32[]{:S(2)}) collective-permute-start(f32[64,1125]{1,0:T(8,128)S(1)} %collective-permute-done.3), channel_id=1, source_target_pairs={{0,2},{1,15},{2,4},{3,1},{4,6},{5,3},{6,8},{7,5},{8,10},{9,7},{10,... | collective-permute-start | bytes 864008 | tf_op jit(solution)/shard_map/ppermute | solution.py:26
  33.4 2.1 %collective-permute-done.1 = f32[64,1125]{1,0:T(8,128)S(1)} collective-permute-done((f32[64,1125]{1,0:T(8,128)S(1)}, f32[64,1125]{1,0:T(8,128)S(1)}, u32[]{:S(2)}, u32[]{:S(2)}) %collective-permute-start.1) | collective-permute-done | bytes 288032 | tf_op jit(solution)/shard_map/ppermute | solution.py:26
  35.5 1.9 %collective-permute-start.2 = (f32[64,1125]{1,0:T(8,128)S(1)}, f32[64,1125]{1,0:T(8,128)S(1)}, u32[]{:S(2)}, u32[]{:S(2)}) collective-permute-start(f32[64,1125]{1,0:T(8,128)S(1)} %collective-permute-done.1), channel_id=1, source_target_pairs={{0,14},{1,3},{2,0},{3,5},{4,2},{5,7},{6,4},{7,9},{8,6},{9,11},{10,... | collective-permute-start | bytes 864008 | tf_op jit(solution)/shard_map/ppermute | solution.py:26
  37.5 1.4 %collective-permute-done.4 = f32[64,1125]{1,0:T(8,128)S(1)} collective-permute-done((f32[64,1125]{1,0:T(8,128)S(1)}, f32[64,1125]{1,0:T(8,128)S(1)}, u32[]{:S(2)}, u32[]{:S(2)}) %collective-permute-start.4) | collective-permute-done | bytes 288032 | tf_op jit(solution)/shard_map/ppermute | solution.py:26
  38.8 3.2 %collective-permute-start.9 = (f32[64,1125]{1,0:T(8,128)S(1)}, f32[64,1125]{1,0:T(8,128)S(1)}, u32[]{:S(2)}, u32[]{:S(2)}) collective-permute-start(f32[64,1125]{1,0:T(8,128)S(1)} %collective-permute-done.4), channel_id=1, source_target_pairs={{0,2},{1,15},{2,4},{3,1},{4,6},{5,3},{6,8},{7,5},{8,10},{9,7},{10,... | collective-permute-start | bytes 864008 | tf_op jit(solution)/shard_map/ppermute | solution.py:26
  42.1 0.0 copy-done
  42.1 1.6 %fusion.25 = f32[320,480]{1,0:T(8,128)S(1)} fusion(f32[320,1125]{1,0:T(8,128)S(1)} %constant_dynamic-update-slice_fusion, f32[1125,480]{0,1:T(8,128)S(1)} %copy-done), kind=kOutput, calls=%fused_computation.72 | convolution fusion | flops 1036800000 | bytes 4214400 | tf_op jit(solution)/shard_map/dot_general | solution.py:85
  43.7 0.0 collective-permute-done.5
  43.7 1.5 %fusion.26 = f32[320,480]{1,0:T(8,128)S(1)} fusion(f32[320,1125]{1,0:T(8,128)S(1)} %constant_dynamic-update-slice_fusion, f32[1125,480]{0,1:T(8,128)S(1)} %collective-permute-done.5), kind=kOutput, calls=%fused_computation.73 | convolution fusion | flops 1036800000 | bytes 4214400 | tf_op jit(solution)/shard_map/dot_general | solution.py:85
  45.2 0.2 fusion.6
  45.4 0.0 collective-permute-done.2
  45.4 2.1 %collective-permute-start.10 = (f32[64,1125]{1,0:T(8,128)S(1)}, f32[64,1125]{1,0:T(8,128)S(1)}, u32[]{:S(2)}, u32[]{:S(2)}) collective-permute-start(f32[64,1125]{1,0:T(8,128)S(1)} %collective-permute-done.2), channel_id=1, source_target_pairs={{0,14},{1,3},{2,0},{3,5},{4,2},{5,7},{6,4},{7,9},{8,6},{9,11},{10,... | collective-permute-start | bytes 864008 | tf_op jit(solution)/shard_map/ppermute | solution.py:26
  47.5 2.3 %collective-permute-done.9 = f32[64,1125]{1,0:T(8,128)S(1)} collective-permute-done((f32[64,1125]{1,0:T(8,128)S(1)}, f32[64,1125]{1,0:T(8,128)S(1)}, u32[]{:S(2)}, u32[]{:S(2)}) %collective-permute-start.9) | collective-permute-done | bytes 288032 | tf_op jit(solution)/shard_map/ppermute | solution.py:26
  49.8 1.9 %collective-permute-start.8 = (f32[5,2,16,480]{3,2,0,1:T(8,128)S(1)}, f32[5,2,16,480]{3,2,0,1:T(8,128)S(1)}, u32[]{:S(2)}, u32[]{:S(2)}) collective-permute-start(f32[5,2,16,480]{3,2,0,1:T(8,128)S(1)} %get-tuple-element.13), channel_id=1, source_target_pairs={{0,32},{1,33},{2,34},{3,35},{4,36},{5,37},{6,38},{7,39},{8,40},{9,... | collective-permute-start | bytes 921608 | tf_op jit(solution)/shard_map/ppermute | solution.py:26
  51.7 1.9 %collective-permute-start.7 = (f32[5,2,16,480]{3,2,0,1:T(8,128)S(1)}, f32[5,2,16,480]{3,2,0,1:T(8,128)S(1)}, u32[]{:S(2)}, u32[]{:S(2)}) collective-permute-start(f32[5,2,16,480]{3,2,0,1:T(8,128)S(1)} %get-tuple-element.12), channel_id=1, source_target_pairs={{0,48},{1,49},{2,50},{3,51},{4,52},{5,53},{6,54},{7,55},{8,56},{9,... | collective-permute-start | bytes 921608 | tf_op jit(solution)/shard_map/ppermute | solution.py:26
  53.7 3.4 %collective-permute-start.6 = (f32[5,2,16,480]{3,2,0,1:T(8,128)S(1)}, f32[5,2,16,480]{3,2,0,1:T(8,128)S(1)}, u32[]{:S(2)}, u32[]{:S(2)}) collective-permute-start(f32[5,2,16,480]{3,2,0,1:T(8,128)S(1)} %get-tuple-element.11), channel_id=1, source_target_pairs={{0,16},{1,17},{2,18},{3,19},{4,20},{5,21},{6,22},{7,23},{8,24},{9,... | collective-permute-start | bytes 921608 | tf_op jit(solution)/shard_map/ppermute | solution.py:26
  57.0 0.0 collective-permute-done.10
  57.1 1.2 fusion.27
  58.3 1.2 fusion.28
  59.5 0.1 fusion.9
  59.6 4.9 %collective-permute-start.13 = (f32[3,2,16,480]{3,2,1,0:T(8,128)S(1)}, f32[3,2,16,480]{3,2,1,0:T(8,128)S(1)}, u32[]{:S(2)}, u32[]{:S(2)}) collective-permute-start(f32[3,2,16,480]{3,2,1,0:T(8,128)S(1)} %bitcast.113), channel_id=1, source_target_pairs={{0,32},{1,33},{2,34},{3,35},{4,36},{5,37},{6,38},{7,39},{8,40},{9,... | collective-permute-start | bytes 552968 | tf_op jit(solution)/shard_map/ppermute | solution.py:26
  64.4 2.5 %collective-permute-start.12 = (f32[3,2,16,480]{3,2,1,0:T(8,128)S(1)}, f32[3,2,16,480]{3,2,1,0:T(8,128)S(1)}, u32[]{:S(2)}, u32[]{:S(2)}) collective-permute-start(f32[3,2,16,480]{3,2,1,0:T(8,128)S(1)} %bitcast.114), channel_id=1, source_target_pairs={{0,48},{1,49},{2,50},{3,51},{4,52},{5,53},{6,54},{7,55},{8,56},{9,... | collective-permute-start | bytes 552968 | tf_op jit(solution)/shard_map/ppermute | solution.py:26
  67.0 0.0 collective-permute-done.8
  67.0 2.8 %collective-permute-start.11 = (f32[3,2,16,480]{3,2,1,0:T(8,128)S(1)}, f32[3,2,16,480]{3,2,1,0:T(8,128)S(1)}, u32[]{:S(2)}, u32[]{:S(2)}) collective-permute-start(f32[3,2,16,480]{3,2,1,0:T(8,128)S(1)} %bitcast.115), channel_id=1, source_target_pairs={{0,16},{1,17},{2,18},{3,19},{4,20},{5,21},{6,22},{7,23},{8,24},{9,... | collective-permute-start | bytes 552968 | tf_op jit(solution)/shard_map/ppermute | solution.py:26
  69.8 0.0 collective-permute-done.7
  69.8 0.0 collective-permute-done.6
  69.8 0.1 add_add_fusion
  70.0 2.6 %collective-permute-done.13 = f32[3,2,16,480]{3,2,1,0:T(8,128)S(1)} collective-permute-done((f32[3,2,16,480]{3,2,1,0:T(8,128)S(1)}, f32[3,2,16,480]{3,2,1,0:T(8,128)S(1)}, u32[]{:S(2)}, u32[]{:S(2)}) %collective-permute-start.13) | collective-permute-done | bytes 184352 | tf_op jit(solution)/shard_map/ppermute | solution.py:26
  72.5 0.1 collective-permute-done.12
  72.6 3.5 %collective-permute-done.11 = f32[3,2,16,480]{3,2,1,0:T(8,128)S(1)} collective-permute-done((f32[3,2,16,480]{3,2,1,0:T(8,128)S(1)}, f32[3,2,16,480]{3,2,1,0:T(8,128)S(1)}, u32[]{:S(2)}, u32[]{:S(2)}) %collective-permute-start.11) | collective-permute-done | bytes 184352 | tf_op jit(solution)/shard_map/ppermute | solution.py:26
  76.1 0.1 fusion.13
  76.2 0.0 copy-start.1
  76.2 0.0 copy-start.2
  76.2 0.0 copy-start.3
  76.3 0.1 dynamic-slice_bitcast_fusion.2
  76.4 11.1 %collective-permute-start.17 = (f32[4,16,480]{2,1,0:T(8,128)S(1)}, f32[4,16,480]{2,1,0:T(8,128)S(1)}, u32[]{:S(2)}, u32[]{:S(2)}) collective-permute-start(f32[4,16,480]{2,1,0:T(8,128)S(1)} %get-tuple-element.26), channel_id=1, source_target_pairs={{0,896},{1,961},{2,898},{3,963},{4,900},{5,965},{6,902},{7,967},{8... | collective-permute-start | bytes 368648 | tf_op jit(solution)/shard_map/ppermute | solution.py:26
  87.5 8.1 %collective-permute-start.16 = (f32[4,16,480]{2,1,0:T(8,128)S(1)}, f32[4,16,480]{2,1,0:T(8,128)S(1)}, u32[]{:S(2)}, u32[]{:S(2)}) collective-permute-start(f32[4,16,480]{2,1,0:T(8,128)S(1)} %get-tuple-element.24), channel_id=1, source_target_pairs={{0,897},{1,960},{2,899},{3,962},{4,901},{5,964},{6,903},{7,966},{8... | collective-permute-start | bytes 368648 | tf_op jit(solution)/shard_map/ppermute | solution.py:26
  95.5 3.9 %collective-permute-start.14 = (f32[4,16,480]{2,1,0:T(8,128)S(1)}, f32[4,16,480]{2,1,0:T(8,128)S(1)}, u32[]{:S(2)}, u32[]{:S(2)}) collective-permute-start(f32[4,16,480]{2,1,0:T(8,128)S(1)} %get-tuple-element.25), channel_id=1, source_target_pairs={{0,1},{1,64},{2,3},{3,66},{4,5},{5,68},{6,7},{7,70},{8,9},{9,72},{... | collective-permute-start | bytes 368648 | tf_op jit(solution)/shard_map/ppermute | solution.py:26
  99.5 1.9 %collective-permute-start.15 = (f32[4,16,480]{2,1,0:T(8,128)S(1)}, f32[4,16,480]{2,1,0:T(8,128)S(1)}, u32[]{:S(2)}, u32[]{:S(2)}) collective-permute-start(f32[4,16,480]{2,1,0:T(8,128)S(1)} %get-tuple-element.23), channel_id=1, source_target_pairs={{0,0},{1,65},{2,2},{3,67},{4,4},{5,69},{6,6},{7,71},{8,8},{9,73},{... | collective-permute-start | bytes 368648 | tf_op jit(solution)/shard_map/ppermute | solution.py:26
  101.4 0.0 collective-permute-done.17
  101.4 0.0 collective-permute-done.16
  101.4 0.7 collective-permute-done.14
  102.1 4.8 %collective-permute-done.15 = f32[4,16,480]{2,1,0:T(8,128)S(1)} collective-permute-done((f32[4,16,480]{2,1,0:T(8,128)S(1)}, f32[4,16,480]{2,1,0:T(8,128)S(1)}, u32[]{:S(2)}, u32[]{:S(2)}) %collective-permute-start.15) | collective-permute-done | bytes 122912 | tf_op jit(solution)/shard_map/ppermute | solution.py:26
  107.0 0.7 add_add_fusion.1
  107.6 3.3 %all-to-all-start = ((f32[4,16,480]{2,1,0:T(8,128)}), f32[4,16,480]{2,1,0:T(8,128)S(1)}, u32[]{:S(2)}, u32[]{:S(2)}) async-start(f32[4,16,480]{2,1,0:T(8,128)} %add_add_fusion.1), calls=%async_computation | async-start | bytes 262144 | tf_op jit(solution)/shard_map/all_to_all | solution.py:115
  111.0 0.0 copy-done.1
  111.0 0.1 broadcast_subtract_fusion
  111.1 0.1 sub.59
  111.2 0.0 copy-done.3
  111.2 0.1 broadcast_subtract_fusion.1
  111.3 0.1 sub.55
  111.4 0.1 dynamic_slice.28
  111.5 0.1 dynamic_slice.27
  111.5 14.0 %all-to-all-done = f32[4,16,480]{2,1,0:T(8,128)S(1)} async-done(((f32[4,16,480]{2,1,0:T(8,128)}), f32[4,16,480]{2,1,0:T(8,128)S(1)}, u32[]{:S(2)}, u32[]{:S(2)}) %all-to-all-start) | async-done | bytes 122912 | tf_op jit(solution)/shard_map/all_to_all | solution.py:115
  125.5 0.7 fusion.23
  (22 shorter events, 0.3 us)
Async XLA Ops:
  0.0 43.7 %collective-permute-start.5 = (f32[1125,480]{0,1:T(8,128)}, f32[1125,480]{0,1:T(8,128)S(1)}, u32[]{:S(2)}, u32[]{:S(2)}) collective-permute-start(f32[1125,480]{0,1:T(8,128)} %param.6), channel_id=1, source_target_pairs={{0,1},{1,0},{2,3},{3,2},{4,5},{5,4},{6,7},{7,6},{8,9},{9,8},{10,11... | collective-permute-start | bytes 6480008 | tf_op jit(solution)/shard_map/ppermute | solution.py:26
  17.2 9.7 %collective-permute-start = (f32[64,1125]{1,0:T(8,128)S(1)}, f32[64,1125]{1,0:T(8,128)S(1)}, u32[]{:S(2)}, u32[]{:S(2)}) collective-permute-start(f32[64,1125]{1,0:T(8,128)S(1)} %bitcast.109), channel_id=1, source_target_pairs={{0,14},{1,3},{2,0},{3,5},{4,2},{5,7},{6,4},{7,9},{8,6},{9,11},{10,... | collective-permute-start | bytes 864008 | tf_op jit(solution)/shard_map/ppermute | solution.py:26
  19.1 9.7 %collective-permute-start.3 = (f32[64,1125]{1,0:T(8,128)S(1)}, f32[64,1125]{1,0:T(8,128)S(1)}, u32[]{:S(2)}, u32[]{:S(2)}) collective-permute-start(f32[64,1125]{1,0:T(8,128)S(1)} %bitcast.110), channel_id=1, source_target_pairs={{0,2},{1,15},{2,4},{3,1},{4,6},{5,3},{6,8},{7,5},{8,10},{9,7},{10,... | collective-permute-start | bytes 864008 | tf_op jit(solution)/shard_map/ppermute | solution.py:26
  23.8 18.3 %copy-start = (f32[1125,480]{0,1:T(8,128)S(1)}, f32[1125,480]{0,1:T(8,128)}, u32[]{:S(2)}) copy-start(f32[1125,480]{0,1:T(8,128)} %param.6) | copy-start | bytes 6480004
  26.9 8.7 %collective-permute-start.1 = (f32[64,1125]{1,0:T(8,128)S(1)}, f32[64,1125]{1,0:T(8,128)S(1)}, u32[]{:S(2)}, u32[]{:S(2)}) collective-permute-start(f32[64,1125]{1,0:T(8,128)S(1)} %collective-permute-done), channel_id=1, source_target_pairs={{0,14},{1,3},{2,0},{3,5},{4,2},{5,7},{6,4},{7,9},{8,6},{9,11},{10,... | collective-permute-start | bytes 864008 | tf_op jit(solution)/shard_map/ppermute | solution.py:26
  28.8 10.0 %collective-permute-start.4 = (f32[64,1125]{1,0:T(8,128)S(1)}, f32[64,1125]{1,0:T(8,128)S(1)}, u32[]{:S(2)}, u32[]{:S(2)}) collective-permute-start(f32[64,1125]{1,0:T(8,128)S(1)} %collective-permute-done.3), channel_id=1, source_target_pairs={{0,2},{1,15},{2,4},{3,1},{4,6},{5,3},{6,8},{7,5},{8,10},{9,7},{10,... | collective-permute-start | bytes 864008 | tf_op jit(solution)/shard_map/ppermute | solution.py:26
  35.5 9.8 %collective-permute-start.2 = (f32[64,1125]{1,0:T(8,128)S(1)}, f32[64,1125]{1,0:T(8,128)S(1)}, u32[]{:S(2)}, u32[]{:S(2)}) collective-permute-start(f32[64,1125]{1,0:T(8,128)S(1)} %collective-permute-done.1), channel_id=1, source_target_pairs={{0,14},{1,3},{2,0},{3,5},{4,2},{5,7},{6,4},{7,9},{8,6},{9,11},{10,... | collective-permute-start | bytes 864008 | tf_op jit(solution)/shard_map/ppermute | solution.py:26
  38.8 10.9 %collective-permute-start.9 = (f32[64,1125]{1,0:T(8,128)S(1)}, f32[64,1125]{1,0:T(8,128)S(1)}, u32[]{:S(2)}, u32[]{:S(2)}) collective-permute-start(f32[64,1125]{1,0:T(8,128)S(1)} %collective-permute-done.4), channel_id=1, source_target_pairs={{0,2},{1,15},{2,4},{3,1},{4,6},{5,3},{6,8},{7,5},{8,10},{9,7},{10,... | collective-permute-start | bytes 864008 | tf_op jit(solution)/shard_map/ppermute | solution.py:26
  45.4 11.7 %collective-permute-start.10 = (f32[64,1125]{1,0:T(8,128)S(1)}, f32[64,1125]{1,0:T(8,128)S(1)}, u32[]{:S(2)}, u32[]{:S(2)}) collective-permute-start(f32[64,1125]{1,0:T(8,128)S(1)} %collective-permute-done.2), channel_id=1, source_target_pairs={{0,14},{1,3},{2,0},{3,5},{4,2},{5,7},{6,4},{7,9},{8,6},{9,11},{10,... | collective-permute-start | bytes 864008 | tf_op jit(solution)/shard_map/ppermute | solution.py:26
  49.8 17.2 %collective-permute-start.8 = (f32[5,2,16,480]{3,2,0,1:T(8,128)S(1)}, f32[5,2,16,480]{3,2,0,1:T(8,128)S(1)}, u32[]{:S(2)}, u32[]{:S(2)}) collective-permute-start(f32[5,2,16,480]{3,2,0,1:T(8,128)S(1)} %get-tuple-element.13), channel_id=1, source_target_pairs={{0,32},{1,33},{2,34},{3,35},{4,36},{5,37},{6,38},{7,39},{8,40},{9,... | collective-permute-start | bytes 921608 | tf_op jit(solution)/shard_map/ppermute | solution.py:26
  51.7 18.1 %collective-permute-start.7 = (f32[5,2,16,480]{3,2,0,1:T(8,128)S(1)}, f32[5,2,16,480]{3,2,0,1:T(8,128)S(1)}, u32[]{:S(2)}, u32[]{:S(2)}) collective-permute-start(f32[5,2,16,480]{3,2,0,1:T(8,128)S(1)} %get-tuple-element.12), channel_id=1, source_target_pairs={{0,48},{1,49},{2,50},{3,51},{4,52},{5,53},{6,54},{7,55},{8,56},{9,... | collective-permute-start | bytes 921608 | tf_op jit(solution)/shard_map/ppermute | solution.py:26
  53.7 16.1 %collective-permute-start.6 = (f32[5,2,16,480]{3,2,0,1:T(8,128)S(1)}, f32[5,2,16,480]{3,2,0,1:T(8,128)S(1)}, u32[]{:S(2)}, u32[]{:S(2)}) collective-permute-start(f32[5,2,16,480]{3,2,0,1:T(8,128)S(1)} %get-tuple-element.11), channel_id=1, source_target_pairs={{0,16},{1,17},{2,18},{3,19},{4,20},{5,21},{6,22},{7,23},{8,24},{9,... | collective-permute-start | bytes 921608 | tf_op jit(solution)/shard_map/ppermute | solution.py:26
  59.6 13.0 %collective-permute-start.13 = (f32[3,2,16,480]{3,2,1,0:T(8,128)S(1)}, f32[3,2,16,480]{3,2,1,0:T(8,128)S(1)}, u32[]{:S(2)}, u32[]{:S(2)}) collective-permute-start(f32[3,2,16,480]{3,2,1,0:T(8,128)S(1)} %bitcast.113), channel_id=1, source_target_pairs={{0,32},{1,33},{2,34},{3,35},{4,36},{5,37},{6,38},{7,39},{8,40},{9,... | collective-permute-start | bytes 552968 | tf_op jit(solution)/shard_map/ppermute | solution.py:26
  64.4 8.2 %collective-permute-start.12 = (f32[3,2,16,480]{3,2,1,0:T(8,128)S(1)}, f32[3,2,16,480]{3,2,1,0:T(8,128)S(1)}, u32[]{:S(2)}, u32[]{:S(2)}) collective-permute-start(f32[3,2,16,480]{3,2,1,0:T(8,128)S(1)} %bitcast.114), channel_id=1, source_target_pairs={{0,48},{1,49},{2,50},{3,51},{4,52},{5,53},{6,54},{7,55},{8,56},{9,... | collective-permute-start | bytes 552968 | tf_op jit(solution)/shard_map/ppermute | solution.py:26
  67.0 9.1 %collective-permute-start.11 = (f32[3,2,16,480]{3,2,1,0:T(8,128)S(1)}, f32[3,2,16,480]{3,2,1,0:T(8,128)S(1)}, u32[]{:S(2)}, u32[]{:S(2)}) collective-permute-start(f32[3,2,16,480]{3,2,1,0:T(8,128)S(1)} %bitcast.115), channel_id=1, source_target_pairs={{0,16},{1,17},{2,18},{3,19},{4,20},{5,21},{6,22},{7,23},{8,24},{9,... | collective-permute-start | bytes 552968 | tf_op jit(solution)/shard_map/ppermute | solution.py:26
  76.2 34.8 %copy-start.1 = (f32[60]{0:T(128)S(1)}, f32[60]{0:T(128)}, u32[]{:S(2)}) copy-start(f32[60]{0:T(128)} %param.7) | copy-start | bytes 724
  76.2 34.8 %copy-start.2 = (f32[128]{0:T(128)S(1)}, f32[128]{0:T(128)}, u32[]{:S(2)}) copy-start(f32[128]{0:T(128)} %param.9) | copy-start | bytes 1540
  76.2 35.0 %copy-start.3 = (f32[16]{0:T(128)S(1)}, f32[16]{0:T(128)}, u32[]{:S(2)}) copy-start(f32[16]{0:T(128)} %param.8) | copy-start | bytes 196
  76.4 25.0 %collective-permute-start.17 = (f32[4,16,480]{2,1,0:T(8,128)S(1)}, f32[4,16,480]{2,1,0:T(8,128)S(1)}, u32[]{:S(2)}, u32[]{:S(2)}) collective-permute-start(f32[4,16,480]{2,1,0:T(8,128)S(1)} %get-tuple-element.26), channel_id=1, source_target_pairs={{0,896},{1,961},{2,898},{3,963},{4,900},{5,965},{6,902},{7,967},{8... | collective-permute-start | bytes 368648 | tf_op jit(solution)/shard_map/ppermute | solution.py:26
  87.5 14.0 %collective-permute-start.16 = (f32[4,16,480]{2,1,0:T(8,128)S(1)}, f32[4,16,480]{2,1,0:T(8,128)S(1)}, u32[]{:S(2)}, u32[]{:S(2)}) collective-permute-start(f32[4,16,480]{2,1,0:T(8,128)S(1)} %get-tuple-element.24), channel_id=1, source_target_pairs={{0,897},{1,960},{2,899},{3,962},{4,901},{5,964},{6,903},{7,966},{8... | collective-permute-start | bytes 368648 | tf_op jit(solution)/shard_map/ppermute | solution.py:26
  95.5 6.6 %collective-permute-start.14 = (f32[4,16,480]{2,1,0:T(8,128)S(1)}, f32[4,16,480]{2,1,0:T(8,128)S(1)}, u32[]{:S(2)}, u32[]{:S(2)}) collective-permute-start(f32[4,16,480]{2,1,0:T(8,128)S(1)} %get-tuple-element.25), channel_id=1, source_target_pairs={{0,1},{1,64},{2,3},{3,66},{4,5},{5,68},{6,7},{7,70},{8,9},{9,72},{... | collective-permute-start | bytes 368648 | tf_op jit(solution)/shard_map/ppermute | solution.py:26
  99.5 7.5 %collective-permute-start.15 = (f32[4,16,480]{2,1,0:T(8,128)S(1)}, f32[4,16,480]{2,1,0:T(8,128)S(1)}, u32[]{:S(2)}, u32[]{:S(2)}) collective-permute-start(f32[4,16,480]{2,1,0:T(8,128)S(1)} %get-tuple-element.23), channel_id=1, source_target_pairs={{0,0},{1,65},{2,2},{3,67},{4,4},{5,69},{6,6},{7,71},{8,8},{9,73},{... | collective-permute-start | bytes 368648 | tf_op jit(solution)/shard_map/ppermute | solution.py:26
  107.6 17.9 %all-to-all-start = ((f32[4,16,480]{2,1,0:T(8,128)}), f32[4,16,480]{2,1,0:T(8,128)S(1)}, u32[]{:S(2)}, u32[]{:S(2)}) async-start(f32[4,16,480]{2,1,0:T(8,128)} %add_add_fusion.1), calls=%async_computation | async-start | bytes 262144 | tf_op jit(solution)/shard_map/all_to_all | solution.py:115

commit v6 on v5

--- a/solution.py
+++ b/solution.py
@@ -34,8 +34,12 @@
     return lambda z, x, y, c: (z, x, y + (step if c == 0 else -step), c)
 
 
+def side_of(x, c):
+    return 1 if (x % 2 == 0) == (c == 0) else -1
+
+
 def along_x(step):
-    return lambda z, x, y, c: (z, x + step, y, c)
+    return lambda z, x, y, c: (z, x + step * side_of(x, c), y, c)
 
 
 def far_step(z):
@@ -71,33 +75,40 @@
     cols = integrals.shape[1]
     share = rows // X
 
+    side = jnp.where((x % 2 == 0) == (c == 0), 1, -1)
     block = jnp.pad(amplitudes.reshape(X, share, depth), ((0, 0), (0, 16 - share), (0, 0)))
-    block = jnp.roll(block, -x, axis=0).reshape(X * 16, depth)
+    block = jnp.concatenate(
+        [lax.dynamic_index_in_dim(block, (x + side * k) % X, 0, keepdims=False) for k in range(X)], 0
+    )
     f1 = send(block, along_y(1))
     h1 = send(block, along_y(-1))
     others = send(integrals, other_core)
     f2 = send(f1, along_y(1))
     h2 = send(h1, along_y(-1))
 
-    def messages(blocks):
+    def partial_sums(blocks):
         tall = jnp.concatenate(blocks, 0)
         halves = [
             jnp.dot(tall, part, precision=lax.Precision.HIGH, preferred_element_type=jnp.float32)
             for part in (integrals, others)
         ]
-        halves = jnp.stack([half.reshape(len(blocks), X, 16, cols) for half in halves], 1)
-        return [halves[:, :, place] for place in range(X)]
+        return jnp.stack([half.reshape(len(blocks), X, 16, cols) for half in halves], 1)
 
-    def sum_over_x(parts):
-        return parts[0] + send(parts[1], along_x(1)) + send(parts[3], along_x(-1)) + send(parts[2], along_x(2))
+    def halving_sum(parts):
+        arrived = send(parts[:, :, 1:3], along_x(1))
+        passed_on = parts[:, :, 3] + arrived[:, :, 1]
+        return parts[:, :, 0] + arrived[:, :, 0] + send(passed_on, along_x(-1))
+
+    def direct_sum(parts):
+        return parts[:, :, 0] + send(parts[:, :, 1], along_x(1)) + send(parts[:, :, 3], along_x(-1)) + send(parts[:, :, 2], along_x(2))
 
     f3 = send(f2, along_y(1))
     h3 = send(h2, along_y(-1))
-    early = messages((block, f1, h1, f2, h2))
-    h3_after, early = lax.optimization_barrier((h3, early))
-    h4 = send(h3_after, along_y(-1))
-    first = sum_over_x(early)
-    second = sum_over_x(messages((f3, h3, h4)))
+    early = partial_sums((block, f1, h1, f2, h2))
+    f3_after, early = lax.optimization_barrier((f3, early))
+    f4 = send(f3_after, along_y(1))
+    first = halving_sum(early)
+    second = direct_sum(partial_sums((f3, h3, f4)))
     pieces = jnp.stack(
         [first[0], first[3], second[2], first[4], first[1], first[2], second[0], second[1]], 1
     )

time: 127 us -> 126 us (level)
  the two profiles are of different devices: /device:TPU:1 before, /device:TPU:25 now
where the time goes in v6:
time: 126 us; the launch traced here: 125 us
  starting transfers between devices  85.2 us (68%)
  waiting for transfers between devices  27.7 us (22%)
  matrix products  5.42 us (4%)
  other arithmetic  2.9 us (2%)
  local copies, waits for them, and re-layouts  2.74 us (2%)
    ppermute x17, starting transfers between devices, send(): return lax.ppermute(array, AXES, table(move))  74.5 us
    ppermute x17, waiting for transfers between devices, send(): return lax.ppermute(array, AXES, table(move))  19.9 us
    all_to_all x1, starting transfers between devices, per_device(): lax.all_to_all(total, AXES, 0, 0, tiled=True, axis_index_groups=classes())  10.7 us
    all_to_all x1, waiting for transfers between devices, per_device(): lax.all_to_all(total, AXES, 0, 0, tiled=True, axis_index_groups=classes())  7.73 us
    dot_general x4, matrix products, partial_sums(): jnp.dot(tall, part, precision=lax.Precision.HIGH, preferred_element_type=...  5.42 us
  transfers between devices with their start and end apart: 18, of which 11 were waited for; matrix products, arithmetic and copies ran while one was open for 6% of the time, Pallas kernels for 0%

profile of v6, /device:TPU:25, one launch (start us, length us, event | category | flops | bytes accessed | tf_op | source)
XLA Modules:
  0.0 124.7 jit_solution(10510999212225592964)
XLA Ops:
  0.0 2.6 %collective-permute-start.5 = (f32[1125,480]{0,1:T(8,128)}, f32[1125,480]{0,1:T(8,128)S(1)}, u32[]{:S(2)}, u32[]{:S(2)}) collective-permute-start(f32[1125,480]{0,1:T(8,128)} %param.6), channel_id=1, source_target_pairs={{0,1},{1,0},{2,3},{3,2},{4,5},{5,4},{6,7},{7,6},{8,9},{9,8},{10,11... | collective-permute-start | bytes 6480008 | tf_op jit(solution)/shard_map/ppermute | solution.py:26
  2.7 1.0 reshape.37
  3.8 0.0 copy-start
  3.9 2.2 %collective-permute-start = (f32[64,1125]{1,0:T(8,128)S(1)}, f32[64,1125]{1,0:T(8,128)S(1)}, u32[]{:S(2)}, u32[]{:S(2)}) collective-permute-start(f32[64,1125]{1,0:T(8,128)S(1)} %pad_maximum_fusion.1), channel_id=1, source_target_pairs={{0,2},{1,15},{2,4},{3,1},{4,6},{5,3},{6,8},{7,5},{8,10},{9,7},{10,... | collective-permute-start | bytes 864008 | tf_op jit(solution)/shard_map/ppermute | solution.py:26
  6.1 4.4 %collective-permute-start.3 = (f32[64,1125]{1,0:T(8,128)S(1)}, f32[64,1125]{1,0:T(8,128)S(1)}, u32[]{:S(2)}, u32[]{:S(2)}) collective-permute-start(f32[64,1125]{1,0:T(8,128)S(1)} %pad_maximum_fusion.1), channel_id=1, source_target_pairs={{0,14},{1,3},{2,0},{3,5},{4,2},{5,7},{6,4},{7,9},{8,6},{9,11},{10,... | collective-permute-start | bytes 864008 | tf_op jit(solution)/shard_map/ppermute | solution.py:26
  10.5 2.2 %collective-permute-done = f32[64,1125]{1,0:T(8,128)S(1)} collective-permute-done((f32[64,1125]{1,0:T(8,128)S(1)}, f32[64,1125]{1,0:T(8,128)S(1)}, u32[]{:S(2)}, u32[]{:S(2)}) %collective-permute-start) | collective-permute-done | bytes 288032 | tf_op jit(solution)/shard_map/ppermute | solution.py:26
  12.7 1.9 %collective-permute-start.1 = (f32[64,1125]{1,0:T(8,128)S(1)}, f32[64,1125]{1,0:T(8,128)S(1)}, u32[]{:S(2)}, u32[]{:S(2)}) collective-permute-start(f32[64,1125]{1,0:T(8,128)S(1)} %collective-permute-done), channel_id=1, source_target_pairs={{0,2},{1,15},{2,4},{3,1},{4,6},{5,3},{6,8},{7,5},{8,10},{9,7},{10,... | collective-permute-start | bytes 864008 | tf_op jit(solution)/shard_map/ppermute | solution.py:26
  14.6 1.1 collective-permute-done.3
  15.7 5.0 %collective-permute-start.4 = (f32[64,1125]{1,0:T(8,128)S(1)}, f32[64,1125]{1,0:T(8,128)S(1)}, u32[]{:S(2)}, u32[]{:S(2)}) collective-permute-start(f32[64,1125]{1,0:T(8,128)S(1)} %collective-permute-done.3), channel_id=1, source_target_pairs={{0,14},{1,3},{2,0},{3,5},{4,2},{5,7},{6,4},{7,9},{8,6},{9,11},{10,... | collective-permute-start | bytes 864008 | tf_op jit(solution)/shard_map/ppermute | solution.py:26
  20.8 0.6 collective-permute-done.1
  21.4 9.5 %collective-permute-start.2 = (f32[64,1125]{1,0:T(8,128)S(1)}, f32[64,1125]{1,0:T(8,128)S(1)}, u32[]{:S(2)}, u32[]{:S(2)}) collective-permute-start(f32[64,1125]{1,0:T(8,128)S(1)} %collective-permute-done.1), channel_id=1, source_target_pairs={{0,2},{1,15},{2,4},{3,1},{4,6},{5,3},{6,8},{7,5},{8,10},{9,7},{10,... | collective-permute-start | bytes 864008 | tf_op jit(solution)/shard_map/ppermute | solution.py:26
  30.9 0.8 collective-permute-done.4
  31.7 1.9 %collective-permute-start.8 = (f32[64,1125]{1,0:T(8,128)S(1)}, f32[64,1125]{1,0:T(8,128)S(1)}, u32[]{:S(2)}, u32[]{:S(2)}) collective-permute-start(f32[64,1125]{1,0:T(8,128)S(1)} %collective-permute-done.4), channel_id=1, source_target_pairs={{0,14},{1,3},{2,0},{3,5},{4,2},{5,7},{6,4},{7,9},{8,6},{9,11},{10,... | collective-permute-start | bytes 864008 | tf_op jit(solution)/shard_map/ppermute | solution.py:26
  33.7 0.0 copy-done
  33.7 1.6 %fusion.29 = f32[320,480]{1,0:T(8,128)S(1)} fusion(f32[320,1125]{1,0:T(8,128)S(1)} %constant_dynamic-update-slice_fusion, f32[1125,480]{0,1:T(8,128)S(1)} %copy-done), kind=kOutput, calls=%fused_computation.73 | convolution fusion | flops 1036800000 | bytes 4214400 | tf_op jit(solution)/shard_map/dot_general | solution.py:92
  35.2 0.0 collective-permute-done.5
  35.2 1.5 %fusion.30 = f32[320,480]{1,0:T(8,128)S(1)} fusion(f32[320,1125]{1,0:T(8,128)S(1)} %constant_dynamic-update-slice_fusion, f32[1125,480]{0,1:T(8,128)S(1)} %collective-permute-done.5), kind=kOutput, calls=%fused_computation.74 | convolution fusion | flops 1036800000 | bytes 4214400 | tf_op jit(solution)/shard_map/dot_general | solution.py:92
  36.8 0.1 pad_maximum_fusion
  36.9 0.0 collective-permute-done.2
  36.9 3.8 %collective-permute-start.9 = (f32[64,1125]{1,0:T(8,128)S(1)}, f32[64,1125]{1,0:T(8,128)S(1)}, u32[]{:S(2)}, u32[]{:S(2)}) collective-permute-start(f32[64,1125]{1,0:T(8,128)S(1)} %collective-permute-done.2), channel_id=1, source_target_pairs={{0,2},{1,15},{2,4},{3,1},{4,6},{5,3},{6,8},{7,5},{8,10},{9,7},{10,... | collective-permute-start | bytes 864008 | tf_op jit(solution)/shard_map/ppermute | solution.py:26
  40.7 0.0 collective-permute-done.8
  40.8 0.1 copy.19
  40.9 1.9 %collective-permute-start.6 = (f32[5,2,2,16,480]{4,3,0,1,2:T(8,128)S(1)}, f32[5,2,2,16,480]{4,3,0,1,2:T(8,128)S(1)}, u32[]{:S(2)}, u32[]{:S(2)}) collective-permute-start(f32[5,2,2,16,480]{4,3,0,1,2:T(8,128)S(1)} %slice.93), channel_id=1, source_target_pairs={{0,16},{1,49},{2,18},{3,51},{4,20},{5,53},{6,22},{7,55},{8,24},{9,... | collective-permute-start | bytes 1843208 | tf_op jit(solution)/shard_map/ppermute | solution.py:26
  42.9 2.7 %collective-permute-done.9 = f32[64,1125]{1,0:T(8,128)S(1)} collective-permute-done((f32[64,1125]{1,0:T(8,128)S(1)}, f32[64,1125]{1,0:T(8,128)S(1)}, u32[]{:S(2)}, u32[]{:S(2)}) %collective-permute-start.9) | collective-permute-done | bytes 288032 | tf_op jit(solution)/shard_map/ppermute | solution.py:26
  45.6 1.2 fusion.31
  46.8 1.2 fusion.32
  48.0 0.1 fusion.5
  48.1 3.6 %collective-permute-start.10 = (f32[3,2,16,480]{3,2,1,0:T(8,128)S(1)}, f32[3,2,16,480]{3,2,1,0:T(8,128)S(1)}, u32[]{:S(2)}, u32[]{:S(2)}) collective-permute-start(f32[3,2,16,480]{3,2,1,0:T(8,128)S(1)} %bitcast.119), channel_id=1, source_target_pairs={{0,16},{1,49},{2,18},{3,51},{4,20},{5,53},{6,22},{7,55},{8,24},{9,... | collective-permute-start | bytes 552968 | tf_op jit(solution)/shard_map/ppermute | solution.py:26
  51.7 1.9 %collective-permute-start.11 = (f32[3,2,16,480]{3,2,1,0:T(8,128)S(1)}, f32[3,2,16,480]{3,2,1,0:T(8,128)S(1)}, u32[]{:S(2)}, u32[]{:S(2)}) collective-permute-start(f32[3,2,16,480]{3,2,1,0:T(8,128)S(1)} %bitcast.120), channel_id=1, source_target_pairs={{0,48},{1,17},{2,50},{3,19},{4,52},{5,21},{6,54},{7,23},{8,56},{9,... | collective-permute-start | bytes 552968 | tf_op jit(solution)/shard_map/ppermute | solution.py:26
  53.7 4.0 %collective-permute-start.12 = (f32[3,2,16,480]{3,2,1,0:T(8,128)S(1)}, f32[3,2,16,480]{3,2,1,0:T(8,128)S(1)}, u32[]{:S(2)}, u32[]{:S(2)}) collective-permute-start(f32[3,2,16,480]{3,2,1,0:T(8,128)S(1)} %bitcast.121), channel_id=1, source_target_pairs={{0,32},{1,33},{2,34},{3,35},{4,36},{5,37},{6,38},{7,39},{8,40},{9,... | collective-permute-start | bytes 552968 | tf_op jit(solution)/shard_map/ppermute | solution.py:26
  57.7 0.0 collective-permute-done.6
  57.8 0.0 copy-start.1
  57.8 0.8 copy-done.1
  58.7 1.9 %collective-permute-start.7 = (f32[5,2,16,480]{3,2,0,1:T(8,128)S(1)}, f32[5,2,16,480]{3,2,0,1:T(8,128)S(1)}, u32[]{:S(2)}, u32[]{:S(2)}) collective-permute-start(f32[5,2,16,480]{3,2,0,1:T(8,128)S(1)} %fusion.1), channel_id=1, source_target_pairs={{0,48},{1,17},{2,50},{3,19},{4,52},{5,21},{6,54},{7,23},{8,56},{9,... | collective-permute-start | bytes 921608 | tf_op jit(solution)/shard_map/ppermute | solution.py:26
  60.7 0.0 collective-permute-done.10
  60.7 0.0 collective-permute-done.11
  60.7 4.5 %collective-permute-done.12 = f32[3,2,16,480]{3,2,1,0:T(8,128)S(1)} collective-permute-done((f32[3,2,16,480]{3,2,1,0:T(8,128)S(1)}, f32[3,2,16,480]{3,2,1,0:T(8,128)S(1)}, u32[]{:S(2)}, u32[]{:S(2)}) %collective-permute-start.12) | collective-permute-done | bytes 184352 | tf_op jit(solution)/shard_map/ppermute | solution.py:26
  65.2 0.1 fusion.9
  65.3 2.3 %collective-permute-done.7 = f32[5,2,16,480]{3,2,0,1:T(8,128)S(1)} collective-permute-done((f32[5,2,16,480]{3,2,0,1:T(8,128)S(1)}, f32[5,2,16,480]{3,2,0,1:T(8,128)S(1)}, u32[]{:S(2)}, u32[]{:S(2)}) %collective-permute-start.7) | collective-permute-done | bytes 307232 | tf_op jit(solution)/shard_map/ppermute | solution.py:26
  67.6 1.0 fusion.3
  68.7 0.0 copy-start.2
  68.7 0.0 copy-start.3
  68.7 0.0 copy-start.4
  68.8 0.1 dynamic-slice_bitcast_fusion.2
  68.9 10.0 %collective-permute-start.13 = (f32[4,16,480]{2,1,0:T(8,128)S(1)}, f32[4,16,480]{2,1,0:T(8,128)S(1)}, u32[]{:S(2)}, u32[]{:S(2)}) collective-permute-start(f32[4,16,480]{2,1,0:T(8,128)S(1)} %get-tuple-element.23), channel_id=1, source_target_pairs={{0,1},{1,64},{2,3},{3,66},{4,5},{5,68},{6,7},{7,70},{8,9},{9,72},{... | collective-permute-start | bytes 368648 | tf_op jit(solution)/shard_map/ppermute | solution.py:26
  78.8 1.9 %collective-permute-start.14 = (f32[4,16,480]{2,1,0:T(8,128)S(1)}, f32[4,16,480]{2,1,0:T(8,128)S(1)}, u32[]{:S(2)}, u32[]{:S(2)}) collective-permute-start(f32[4,16,480]{2,1,0:T(8,128)S(1)} %get-tuple-element.21), channel_id=1, source_target_pairs={{0,0},{1,65},{2,2},{3,67},{4,4},{5,69},{6,6},{7,71},{8,8},{9,73},{... | collective-permute-start | bytes 368648 | tf_op jit(solution)/shard_map/ppermute | solution.py:26
  80.8 15.9 %collective-permute-start.15 = (f32[4,16,480]{2,1,0:T(8,128)S(1)}, f32[4,16,480]{2,1,0:T(8,128)S(1)}, u32[]{:S(2)}, u32[]{:S(2)}) collective-permute-start(f32[4,16,480]{2,1,0:T(8,128)S(1)} %get-tuple-element.22), channel_id=1, source_target_pairs={{0,897},{1,960},{2,899},{3,962},{4,901},{5,964},{6,903},{7,966},{8... | collective-permute-start | bytes 368648 | tf_op jit(solution)/shard_map/ppermute | solution.py:26
  96.6 2.0 %collective-permute-start.16 = (f32[4,16,480]{2,1,0:T(8,128)S(1)}, f32[4,16,480]{2,1,0:T(8,128)S(1)}, u32[]{:S(2)}, u32[]{:S(2)}) collective-permute-start(f32[4,16,480]{2,1,0:T(8,128)S(1)} %get-tuple-element.24), channel_id=1, source_target_pairs={{0,896},{1,961},{2,898},{3,963},{4,900},{5,965},{6,902},{7,967},{8... | collective-permute-start | bytes 368648 | tf_op jit(solution)/shard_map/ppermute | solution.py:26
  98.6 0.0 collective-permute-done.13
  98.7 0.1 collective-permute-done.14
  98.8 1.3 %collective-permute-done.15 = f32[4,16,480]{2,1,0:T(8,128)S(1)} collective-permute-done((f32[4,16,480]{2,1,0:T(8,128)S(1)}, f32[4,16,480]{2,1,0:T(8,128)S(1)}, u32[]{:S(2)}, u32[]{:S(2)}) %collective-permute-start.15) | collective-permute-done | bytes 122912 | tf_op jit(solution)/shard_map/ppermute | solution.py:26
  100.0 4.4 %collective-permute-done.16 = f32[4,16,480]{2,1,0:T(8,128)S(1)} collective-permute-done((f32[4,16,480]{2,1,0:T(8,128)S(1)}, f32[4,16,480]{2,1,0:T(8,128)S(1)}, u32[]{:S(2)}, u32[]{:S(2)}) %collective-permute-start.16) | collective-permute-done | bytes 122912 | tf_op jit(solution)/shard_map/ppermute | solution.py:26
  104.4 0.7 add_add_fusion
  105.0 10.7 %all-to-all-start = ((f32[4,16,480]{2,1,0:T(8,128)}), f32[4,16,480]{2,1,0:T(8,128)S(1)}, u32[]{:S(2)}, u32[]{:S(2)}) async-start(f32[4,16,480]{2,1,0:T(8,128)} %add_add_fusion), calls=%async_computation | async-start | bytes 262144 | tf_op jit(solution)/shard_map/all_to_all | solution.py:126
  115.8 0.0 copy-done.2
  115.8 0.0 copy-done.3
  115.8 0.1 broadcast_subtract_fusion
  115.9 0.1 sub.54
  116.0 0.1 broadcast_subtract_fusion.1
  116.1 0.1 sub.50
  116.1 0.1 dynamic_slice.40
  116.2 0.1 dynamic_slice.39
  116.3 7.7 %all-to-all-done = f32[4,16,480]{2,1,0:T(8,128)S(1)} async-done(((f32[4,16,480]{2,1,0:T(8,128)}), f32[4,16,480]{2,1,0:T(8,128)S(1)}, u32[]{:S(2)}, u32[]{:S(2)}) %all-to-all-start) | async-done | bytes 122912 | tf_op jit(solution)/shard_map/all_to_all | solution.py:126
  124.0 0.7 fusion.23
  (27 shorter events, 0.5 us)
Async XLA Ops:
  0.0 35.2 %collective-permute-start.5 = (f32[1125,480]{0,1:T(8,128)}, f32[1125,480]{0,1:T(8,128)S(1)}, u32[]{:S(2)}, u32[]{:S(2)}) collective-permute-start(f32[1125,480]{0,1:T(8,128)} %param.6), channel_id=1, source_target_pairs={{0,1},{1,0},{2,3},{3,2},{4,5},{5,4},{6,7},{7,6},{8,9},{9,8},{10,11... | collective-permute-start | bytes 6480008 | tf_op jit(solution)/shard_map/ppermute | solution.py:26
  3.8 29.8 %copy-start = (f32[1125,480]{0,1:T(8,128)S(1)}, f32[1125,480]{0,1:T(8,128)}, u32[]{:S(2)}) copy-start(f32[1125,480]{0,1:T(8,128)} %param.6) | copy-start | bytes 6480004
  3.9 8.8 %collective-permute-start = (f32[64,1125]{1,0:T(8,128)S(1)}, f32[64,1125]{1,0:T(8,128)S(1)}, u32[]{:S(2)}, u32[]{:S(2)}) collective-permute-start(f32[64,1125]{1,0:T(8,128)S(1)} %pad_maximum_fusion.1), channel_id=1, source_target_pairs={{0,2},{1,15},{2,4},{3,1},{4,6},{5,3},{6,8},{7,5},{8,10},{9,7},{10,... | collective-permute-start | bytes 864008 | tf_op jit(solution)/shard_map/ppermute | solution.py:26
  6.1 9.6 %collective-permute-start.3 = (f32[64,1125]{1,0:T(8,128)S(1)}, f32[64,1125]{1,0:T(8,128)S(1)}, u32[]{:S(2)}, u32[]{:S(2)}) collective-permute-start(f32[64,1125]{1,0:T(8,128)S(1)} %pad_maximum_fusion.1), channel_id=1, source_target_pairs={{0,14},{1,3},{2,0},{3,5},{4,2},{5,7},{6,4},{7,9},{8,6},{9,11},{10,... | collective-permute-start | bytes 864008 | tf_op jit(solution)/shard_map/ppermute | solution.py:26
  12.7 8.7 %collective-permute-start.1 = (f32[64,1125]{1,0:T(8,128)S(1)}, f32[64,1125]{1,0:T(8,128)S(1)}, u32[]{:S(2)}, u32[]{:S(2)}) collective-permute-start(f32[64,1125]{1,0:T(8,128)S(1)} %collective-permute-done), channel_id=1, source_target_pairs={{0,2},{1,15},{2,4},{3,1},{4,6},{5,3},{6,8},{7,5},{8,10},{9,7},{10,... | collective-permute-start | bytes 864008 | tf_op jit(solution)/shard_map/ppermute | solution.py:26
  15.7 16.0 %collective-permute-start.4 = (f32[64,1125]{1,0:T(8,128)S(1)}, f32[64,1125]{1,0:T(8,128)S(1)}, u32[]{:S(2)}, u32[]{:S(2)}) collective-permute-start(f32[64,1125]{1,0:T(8,128)S(1)} %collective-permute-done.3), channel_id=1, source_target_pairs={{0,14},{1,3},{2,0},{3,5},{4,2},{5,7},{6,4},{7,9},{8,6},{9,11},{10,... | collective-permute-start | bytes 864008 | tf_op jit(solution)/shard_map/ppermute | solution.py:26
  21.4 15.6 %collective-permute-start.2 = (f32[64,1125]{1,0:T(8,128)S(1)}, f32[64,1125]{1,0:T(8,128)S(1)}, u32[]{:S(2)}, u32[]{:S(2)}) collective-permute-start(f32[64,1125]{1,0:T(8,128)S(1)} %collective-permute-done.1), channel_id=1, source_target_pairs={{0,2},{1,15},{2,4},{3,1},{4,6},{5,3},{6,8},{7,5},{8,10},{9,7},{10,... | collective-permute-start | bytes 864008 | tf_op jit(solution)/shard_map/ppermute | solution.py:26
  31.7 9.0 %collective-permute-start.8 = (f32[64,1125]{1,0:T(8,128)S(1)}, f32[64,1125]{1,0:T(8,128)S(1)}, u32[]{:S(2)}, u32[]{:S(2)}) collective-permute-start(f32[64,1125]{1,0:T(8,128)S(1)} %collective-permute-done.4), channel_id=1, source_target_pairs={{0,14},{1,3},{2,0},{3,5},{4,2},{5,7},{6,4},{7,9},{8,6},{9,11},{10,... | collective-permute-start | bytes 864008 | tf_op jit(solution)/shard_map/ppermute | solution.py:26
  36.9 8.7 %collective-permute-start.9 = (f32[64,1125]{1,0:T(8,128)S(1)}, f32[64,1125]{1,0:T(8,128)S(1)}, u32[]{:S(2)}, u32[]{:S(2)}) collective-permute-start(f32[64,1125]{1,0:T(8,128)S(1)} %collective-permute-done.2), channel_id=1, source_target_pairs={{0,2},{1,15},{2,4},{3,1},{4,6},{5,3},{6,8},{7,5},{8,10},{9,7},{10,... | collective-permute-start | bytes 864008 | tf_op jit(solution)/shard_map/ppermute | solution.py:26
  40.9 16.8 %collective-permute-start.6 = (f32[5,2,2,16,480]{4,3,0,1,2:T(8,128)S(1)}, f32[5,2,2,16,480]{4,3,0,1,2:T(8,128)S(1)}, u32[]{:S(2)}, u32[]{:S(2)}) collective-permute-start(f32[5,2,2,16,480]{4,3,0,1,2:T(8,128)S(1)} %slice.93), channel_id=1, source_target_pairs={{0,16},{1,49},{2,18},{3,51},{4,20},{5,53},{6,22},{7,55},{8,24},{9,... | collective-permute-start | bytes 1843208 | tf_op jit(solution)/shard_map/ppermute | solution.py:26
  48.1 12.6 %collective-permute-start.10 = (f32[3,2,16,480]{3,2,1,0:T(8,128)S(1)}, f32[3,2,16,480]{3,2,1,0:T(8,128)S(1)}, u32[]{:S(2)}, u32[]{:S(2)}) collective-permute-start(f32[3,2,16,480]{3,2,1,0:T(8,128)S(1)} %bitcast.119), channel_id=1, source_target_pairs={{0,16},{1,49},{2,18},{3,51},{4,20},{5,53},{6,22},{7,55},{8,24},{9,... | collective-permute-start | bytes 552968 | tf_op jit(solution)/shard_map/ppermute | solution.py:26
  51.7 9.0 %collective-permute-start.11 = (f32[3,2,16,480]{3,2,1,0:T(8,128)S(1)}, f32[3,2,16,480]{3,2,1,0:T(8,128)S(1)}, u32[]{:S(2)}, u32[]{:S(2)}) collective-permute-start(f32[3,2,16,480]{3,2,1,0:T(8,128)S(1)} %bitcast.120), channel_id=1, source_target_pairs={{0,48},{1,17},{2,50},{3,19},{4,52},{5,21},{6,54},{7,23},{8,56},{9,... | collective-permute-start | bytes 552968 | tf_op jit(solution)/shard_map/ppermute | solution.py:26
  53.7 11.5 %collective-permute-start.12 = (f32[3,2,16,480]{3,2,1,0:T(8,128)S(1)}, f32[3,2,16,480]{3,2,1,0:T(8,128)S(1)}, u32[]{:S(2)}, u32[]{:S(2)}) collective-permute-start(f32[3,2,16,480]{3,2,1,0:T(8,128)S(1)} %bitcast.121), channel_id=1, source_target_pairs={{0,32},{1,33},{2,34},{3,35},{4,36},{5,37},{6,38},{7,39},{8,40},{9,... | collective-permute-start | bytes 552968 | tf_op jit(solution)/shard_map/ppermute | solution.py:26
  57.8 0.8 copy-start.1
  58.7 8.9 %collective-permute-start.7 = (f32[5,2,16,480]{3,2,0,1:T(8,128)S(1)}, f32[5,2,16,480]{3,2,0,1:T(8,128)S(1)}, u32[]{:S(2)}, u32[]{:S(2)}) collective-permute-start(f32[5,2,16,480]{3,2,0,1:T(8,128)S(1)} %fusion.1), channel_id=1, source_target_pairs={{0,48},{1,17},{2,50},{3,19},{4,52},{5,21},{6,54},{7,23},{8,56},{9,... | collective-permute-start | bytes 921608 | tf_op jit(solution)/shard_map/ppermute | solution.py:26
  68.7 47.1 %copy-start.2 = (f32[60]{0:T(128)S(1)}, f32[60]{0:T(128)}, u32[]{:S(2)}) copy-start(f32[60]{0:T(128)} %param.7) | copy-start | bytes 724
  68.7 47.1 %copy-start.3 = (f32[128]{0:T(128)S(1)}, f32[128]{0:T(128)}, u32[]{:S(2)}) copy-start(f32[128]{0:T(128)} %param.9) | copy-start | bytes 1540
  68.7 47.3 %copy-start.4 = (f32[16]{0:T(128)S(1)}, f32[16]{0:T(128)}, u32[]{:S(2)}) copy-start(f32[16]{0:T(128)} %param.8) | copy-start | bytes 196
  68.9 29.8 %collective-permute-start.13 = (f32[4,16,480]{2,1,0:T(8,128)S(1)}, f32[4,16,480]{2,1,0:T(8,128)S(1)}, u32[]{:S(2)}, u32[]{:S(2)}) collective-permute-start(f32[4,16,480]{2,1,0:T(8,128)S(1)} %get-tuple-element.23), channel_id=1, source_target_pairs={{0,1},{1,64},{2,3},{3,66},{4,5},{5,68},{6,7},{7,70},{8,9},{9,72},{... | collective-permute-start | bytes 368648 | tf_op jit(solution)/shard_map/ppermute | solution.py:26
  78.8 19.9 %collective-permute-start.14 = (f32[4,16,480]{2,1,0:T(8,128)S(1)}, f32[4,16,480]{2,1,0:T(8,128)S(1)}, u32[]{:S(2)}, u32[]{:S(2)}) collective-permute-start(f32[4,16,480]{2,1,0:T(8,128)S(1)} %get-tuple-element.21), channel_id=1, source_target_pairs={{0,0},{1,65},{2,2},{3,67},{4,4},{5,69},{6,6},{7,71},{8,8},{9,73},{... | collective-permute-start | bytes 368648 | tf_op jit(solution)/shard_map/ppermute | solution.py:26
  80.8 19.3 %collective-permute-start.15 = (f32[4,16,480]{2,1,0:T(8,128)S(1)}, f32[4,16,480]{2,1,0:T(8,128)S(1)}, u32[]{:S(2)}, u32[]{:S(2)}) collective-permute-start(f32[4,16,480]{2,1,0:T(8,128)S(1)} %get-tuple-element.22), channel_id=1, source_target_pairs={{0,897},{1,960},{2,899},{3,962},{4,901},{5,964},{6,903},{7,966},{8... | collective-permute-start | bytes 368648 | tf_op jit(solution)/shard_map/ppermute | solution.py:26
  96.6 7.7 %collective-permute-start.16 = (f32[4,16,480]{2,1,0:T(8,128)S(1)}, f32[4,16,480]{2,1,0:T(8,128)S(1)}, u32[]{:S(2)}, u32[]{:S(2)}) collective-permute-start(f32[4,16,480]{2,1,0:T(8,128)S(1)} %get-tuple-element.24), channel_id=1, source_target_pairs={{0,896},{1,961},{2,898},{3,963},{4,900},{5,965},{6,902},{7,967},{8... | collective-permute-start | bytes 368648 | tf_op jit(solution)/shard_map/ppermute | solution.py:26
  105.0 19.0 %all-to-all-start = ((f32[4,16,480]{2,1,0:T(8,128)}), f32[4,16,480]{2,1,0:T(8,128)S(1)}, u32[]{:S(2)}, u32[]{:S(2)}) async-start(f32[4,16,480]{2,1,0:T(8,128)} %add_add_fusion), calls=%async_computation | async-start | bytes 262144 | tf_op jit(solution)/shard_map/all_to_all | solution.py:126

commit v7 on v6

--- a/solution.py
+++ b/solution.py
@@ -86,29 +86,28 @@
     f2 = send(f1, along_y(1))
     h2 = send(h1, along_y(-1))
 
-    def partial_sums(blocks):
+    def product(blocks, part):
         tall = jnp.concatenate(blocks, 0)
-        halves = [
-            jnp.dot(tall, part, precision=lax.Precision.HIGH, preferred_element_type=jnp.float32)
-            for part in (integrals, others)
-        ]
-        return jnp.stack([half.reshape(len(blocks), X, 16, cols) for half in halves], 1)
-
-    def halving_sum(parts):
-        arrived = send(parts[:, :, 1:3], along_x(1))
-        passed_on = parts[:, :, 3] + arrived[:, :, 1]
-        return parts[:, :, 0] + arrived[:, :, 0] + send(passed_on, along_x(-1))
-
-    def direct_sum(parts):
-        return parts[:, :, 0] + send(parts[:, :, 1], along_x(1)) + send(parts[:, :, 3], along_x(-1)) + send(parts[:, :, 2], along_x(2))
+        out = jnp.dot(tall, part, precision=lax.Precision.HIGH, preferred_element_type=jnp.float32)
+        return out.reshape(len(blocks), X, 16, cols)
 
     f3 = send(f2, along_y(1))
     h3 = send(h2, along_y(-1))
-    early = partial_sums((block, f1, h1, f2, h2))
-    f3_after, early = lax.optimization_barrier((f3, early))
+    near_blocks = (block, f1, h1, f2, h2)
+    own = product(near_blocks, integrals)
+    f3_after, own = lax.optimization_barrier((f3, own))
     f4 = send(f3_after, along_y(1))
-    first = halving_sum(early)
-    second = direct_sum(partial_sums((f3, h3, f4)))
+    early = jnp.stack([own, product(near_blocks, others)], 1)
+    h3_after, early = lax.optimization_barrier((h3, early))
+    arrived = send(early[:, :, 1:3], along_x(1))
+    passed_on = early[:, :, 3] + arrived[:, :, 1]
+    far_blocks = (f3, h3_after, f4)
+    late = jnp.stack([product(far_blocks, integrals), product(far_blocks, others)], 1)
+    late_first = send(late[:, :, 1], along_x(1))
+    late_last, late_far = late[:, :, 3], late[:, :, 2]
+    first = early[:, :, 0] + arrived[:, :, 0] + send(passed_on, along_x(-1))
+    second, first = lax.optimization_barrier((late[:, :, 0] + late_first, first))
+    second = second + send(late_last, along_x(-1)) + send(late_far, along_x(2))
     pieces = jnp.stack(
         [first[0], first[3], second[2], first[4], first[1], first[2], second[0], second[1]], 1
     )

time: 126 us -> 130 us (1.032)
  the two profiles are of different devices: /device:TPU:25 before, /device:TPU:30 now
where the time goes in v7:
time: 130 us; the launch traced here: 129 us
  starting transfers between devices  78.1 us (60%)
  waiting for transfers between devices  39.6 us (30%)
  matrix products  5.42 us (4%)
  local copies, waits for them, and re-layouts  2.76 us (2%)
  other arithmetic  2.69 us (2%)
    ppermute x17, starting transfers between devices, send(): return lax.ppermute(array, AXES, table(move))  69.6 us
    ppermute x17, waiting for transfers between devices, send(): return lax.ppermute(array, AXES, table(move))  30.9 us
    all_to_all x1, waiting for transfers between devices, per_device(): lax.all_to_all(total, AXES, 0, 0, tiled=True, axis_index_groups=classes())  8.67 us
    all_to_all x1, starting transfers between devices, per_device(): lax.all_to_all(total, AXES, 0, 0, tiled=True, axis_index_groups=classes())  8.51 us
    dot_general x4, matrix products, product(): jnp.dot(tall, part, precision=lax.Precision.HIGH, preferred_element_type=...  5.42 us
  transfers between devices with their start and end apart: 18, of which 10 were waited for; matrix products, arithmetic and copies ran while one was open for 7% of the time, Pallas kernels for 0%

profile of v7, /device:TPU:30, one launch (start us, length us, event | category | flops | bytes accessed | tf_op | source)
XLA Modules:
  0.0 129.4 jit_solution(12530782613470386567)
XLA Ops:
  0.0 1.9 %collective-permute-start.6 = (f32[1125,480]{0,1:T(8,128)}, f32[1125,480]{0,1:T(8,128)S(1)}, u32[]{:S(2)}, u32[]{:S(2)}) collective-permute-start(f32[1125,480]{0,1:T(8,128)} %param.6), channel_id=1, source_target_pairs={{0,1},{1,0},{2,3},{3,2},{4,5},{5,4},{6,7},{7,6},{8,9},{9,8},{10,11... | collective-permute-start | bytes 6480008 | tf_op jit(solution)/shard_map/ppermute | solution.py:26
  2.0 1.0 reshape.40
  3.2 0.0 copy-start
  3.2 4.8 %collective-permute-start = (f32[64,1125]{1,0:T(8,128)S(1)}, f32[64,1125]{1,0:T(8,128)S(1)}, u32[]{:S(2)}, u32[]{:S(2)}) collective-permute-start(f32[64,1125]{1,0:T(8,128)S(1)} %pad_maximum_fusion.1), channel_id=1, source_target_pairs={{0,2},{1,15},{2,4},{3,1},{4,6},{5,3},{6,8},{7,5},{8,10},{9,7},{10,... | collective-permute-start | bytes 864008 | tf_op jit(solution)/shard_map/ppermute | solution.py:26
  8.0 1.9 %collective-permute-start.3 = (f32[64,1125]{1,0:T(8,128)S(1)}, f32[64,1125]{1,0:T(8,128)S(1)}, u32[]{:S(2)}, u32[]{:S(2)}) collective-permute-start(f32[64,1125]{1,0:T(8,128)S(1)} %pad_maximum_fusion.1), channel_id=1, source_target_pairs={{0,14},{1,3},{2,0},{3,5},{4,2},{5,7},{6,4},{7,9},{8,6},{9,11},{10,... | collective-permute-start | bytes 864008 | tf_op jit(solution)/shard_map/ppermute | solution.py:26
  10.0 3.8 %collective-permute-done = f32[64,1125]{1,0:T(8,128)S(1)} collective-permute-done((f32[64,1125]{1,0:T(8,128)S(1)}, f32[64,1125]{1,0:T(8,128)S(1)}, u32[]{:S(2)}, u32[]{:S(2)}) %collective-permute-start) | collective-permute-done | bytes 288032 | tf_op jit(solution)/shard_map/ppermute | solution.py:26
  13.7 5.6 %collective-permute-start.1 = (f32[64,1125]{1,0:T(8,128)S(1)}, f32[64,1125]{1,0:T(8,128)S(1)}, u32[]{:S(2)}, u32[]{:S(2)}) collective-permute-start(f32[64,1125]{1,0:T(8,128)S(1)} %collective-permute-done), channel_id=1, source_target_pairs={{0,2},{1,15},{2,4},{3,1},{4,6},{5,3},{6,8},{7,5},{8,10},{9,7},{10,... | collective-permute-start | bytes 864008 | tf_op jit(solution)/shard_map/ppermute | solution.py:26
  19.3 0.0 collective-permute-done.3
  19.4 1.9 %collective-permute-start.4 = (f32[64,1125]{1,0:T(8,128)S(1)}, f32[64,1125]{1,0:T(8,128)S(1)}, u32[]{:S(2)}, u32[]{:S(2)}) collective-permute-start(f32[64,1125]{1,0:T(8,128)S(1)} %collective-permute-done.3), channel_id=1, source_target_pairs={{0,14},{1,3},{2,0},{3,5},{4,2},{5,7},{6,4},{7,9},{8,6},{9,11},{10,... | collective-permute-start | bytes 864008 | tf_op jit(solution)/shard_map/ppermute | solution.py:26
  21.3 4.9 %collective-permute-done.1 = f32[64,1125]{1,0:T(8,128)S(1)} collective-permute-done((f32[64,1125]{1,0:T(8,128)S(1)}, f32[64,1125]{1,0:T(8,128)S(1)}, u32[]{:S(2)}, u32[]{:S(2)}) %collective-permute-start.1) | collective-permute-done | bytes 288032 | tf_op jit(solution)/shard_map/ppermute | solution.py:26
  26.2 5.6 %collective-permute-start.2 = (f32[64,1125]{1,0:T(8,128)S(1)}, f32[64,1125]{1,0:T(8,128)S(1)}, u32[]{:S(2)}, u32[]{:S(2)}) collective-permute-start(f32[64,1125]{1,0:T(8,128)S(1)} %collective-permute-done.1), channel_id=1, source_target_pairs={{0,2},{1,15},{2,4},{3,1},{4,6},{5,3},{6,8},{7,5},{8,10},{9,7},{10,... | collective-permute-start | bytes 864008 | tf_op jit(solution)/shard_map/ppermute | solution.py:26
  31.8 0.0 collective-permute-done.4
  31.9 1.9 %collective-permute-start.5 = (f32[64,1125]{1,0:T(8,128)S(1)}, f32[64,1125]{1,0:T(8,128)S(1)}, u32[]{:S(2)}, u32[]{:S(2)}) collective-permute-start(f32[64,1125]{1,0:T(8,128)S(1)} %collective-permute-done.4), channel_id=1, source_target_pairs={{0,14},{1,3},{2,0},{3,5},{4,2},{5,7},{6,4},{7,9},{8,6},{9,11},{10,... | collective-permute-start | bytes 864008 | tf_op jit(solution)/shard_map/ppermute | solution.py:26
  33.8 0.0 copy-done
  33.9 1.6 %fusion.26 = f32[320,480]{1,0:T(8,128)S(1)} fusion(f32[320,1125]{1,0:T(8,128)S(1)} %constant_dynamic-update-slice_fusion, f32[1125,480]{0,1:T(8,128)S(1)} %copy-done), kind=kOutput, calls=%fused_computation.71 | convolution fusion | flops 1036800000 | bytes 4214400 | tf_op jit(solution)/shard_map/dot_general | solution.py:91
  35.4 3.1 %collective-permute-done.2 = f32[64,1125]{1,0:T(8,128)S(1)} collective-permute-done((f32[64,1125]{1,0:T(8,128)S(1)}, f32[64,1125]{1,0:T(8,128)S(1)}, u32[]{:S(2)}, u32[]{:S(2)}) %collective-permute-start.2) | collective-permute-done | bytes 288032 | tf_op jit(solution)/shard_map/ppermute | solution.py:26
  38.5 5.6 %collective-permute-start.7 = (f32[64,1125]{1,0:T(8,128)S(1)}, f32[64,1125]{1,0:T(8,128)S(1)}, u32[]{:S(2)}, u32[]{:S(2)}) collective-permute-start(f32[64,1125]{1,0:T(8,128)S(1)} %collective-permute-done.2), channel_id=1, source_target_pairs={{0,2},{1,15},{2,4},{3,1},{4,6},{5,3},{6,8},{7,5},{8,10},{9,7},{10,... | collective-permute-start | bytes 864008 | tf_op jit(solution)/shard_map/ppermute | solution.py:26
  44.2 0.0 collective-permute-done.6
  44.2 1.5 %fusion.27 = f32[320,480]{1,0:T(8,128)S(1)} fusion(f32[320,1125]{1,0:T(8,128)S(1)} %constant_dynamic-update-slice_fusion, f32[1125,480]{0,1:T(8,128)S(1)} %collective-permute-done.6), kind=kOutput, calls=%fused_computation.72 | convolution fusion | flops 1036800000 | bytes 4214400 | tf_op jit(solution)/shard_map/dot_general | solution.py:91
  45.7 0.1 pad_maximum_fusion
  45.8 0.0 collective-permute-done.5
  45.9 0.1 copy.21
  46.0 0.1 slice.97
  46.0 2.7 %collective-permute-start.9 = (f32[5,2,2,16,480]{4,3,0,1,2:T(8,128)S(1)}, f32[5,2,2,16,480]{4,3,0,1,2:T(8,128)S(1)}, u32[]{:S(2)}, u32[]{:S(2)}) collective-permute-start(f32[5,2,2,16,480]{4,3,0,1,2:T(8,128)S(1)} %slice.97), channel_id=1, source_target_pairs={{0,16},{1,49},{2,18},{3,51},{4,20},{5,53},{6,22},{7,55},{8,24},{9,... | collective-permute-start | bytes 1843208 | tf_op jit(solution)/shard_map/ppermute | solution.py:26
  48.8 0.0 collective-permute-done.7
  48.8 1.2 fusion.28
  50.1 1.2 fusion.29
  51.2 0.1 fusion.4
  51.3 3.1 %collective-permute-start.8 = (f32[3,2,16,480]{3,2,1,0:T(8,128)S(1)}, f32[3,2,16,480]{3,2,1,0:T(8,128)S(1)}, u32[]{:S(2)}, u32[]{:S(2)}) collective-permute-start(f32[3,2,16,480]{3,2,1,0:T(8,128)S(1)} %bitcast.106), channel_id=1, source_target_pairs={{0,16},{1,49},{2,18},{3,51},{4,20},{5,53},{6,22},{7,55},{8,24},{9,... | collective-permute-start | bytes 552968 | tf_op jit(solution)/shard_map/ppermute | solution.py:26
  54.4 5.3 %collective-permute-done.9 = f32[5,2,2,16,480]{4,3,0,1,2:T(8,128)S(1)} collective-permute-done((f32[5,2,2,16,480]{4,3,0,1,2:T(8,128)S(1)}, f32[5,2,2,16,480]{4,3,0,1,2:T(8,128)S(1)}, u32[]{:S(2)}, u32[]{:S(2)}) %collective-permute-start.9) | collective-permute-done | bytes 614432 | tf_op jit(solution)/shard_map/ppermute | solution.py:26
  59.7 0.8 copy-done.1
  60.5 0.8 fusion.1
  61.3 2.0 %collective-permute-start.10 = (f32[5,2,16,480]{3,2,0,1:T(8,128)}, f32[5,2,16,480]{3,2,0,1:T(8,128)S(1)}, u32[]{:S(2)}, u32[]{:S(2)}) collective-permute-start(f32[5,2,16,480]{3,2,0,1:T(8,128)} %fusion.1), channel_id=1, source_target_pairs={{0,48},{1,17},{2,50},{3,19},{4,52},{5,21},{6,54},{7,23},{8,56},{9,... | collective-permute-start | bytes 921608 | tf_op jit(solution)/shard_map/ppermute | solution.py:26
  63.5 5.1 %collective-permute-start.11 = (f32[3,2,16,480]{3,2,1,0:T(8,128)S(1)}, f32[3,2,16,480]{3,2,1,0:T(8,128)S(1)}, u32[]{:S(2)}, u32[]{:S(2)}) collective-permute-start(f32[3,2,16,480]{3,2,1,0:T(8,128)S(1)} %bitcast.107), channel_id=1, source_target_pairs={{0,48},{1,17},{2,50},{3,19},{4,52},{5,21},{6,54},{7,23},{8,56},{9,... | collective-permute-start | bytes 552968 | tf_op jit(solution)/shard_map/ppermute | solution.py:26
  68.7 2.1 %collective-permute-start.12 = (f32[3,2,16,480]{3,2,1,0:T(8,128)S(1)}, f32[3,2,16,480]{3,2,1,0:T(8,128)S(1)}, u32[]{:S(2)}, u32[]{:S(2)}) collective-permute-start(f32[3,2,16,480]{3,2,1,0:T(8,128)S(1)} %bitcast.108), channel_id=1, source_target_pairs={{0,32},{1,33},{2,34},{3,35},{4,36},{5,37},{6,38},{7,39},{8,40},{9,... | collective-permute-start | bytes 552968 | tf_op jit(solution)/shard_map/ppermute | solution.py:26
  70.8 0.0 collective-permute-done.8
  70.8 2.1 %collective-permute-done.10 = f32[5,2,16,480]{3,2,0,1:T(8,128)S(1)} collective-permute-done((f32[5,2,16,480]{3,2,0,1:T(8,128)}, f32[5,2,16,480]{3,2,0,1:T(8,128)S(1)}, u32[]{:S(2)}, u32[]{:S(2)}) %collective-permute-start.10) | collective-permute-done | bytes 307232 | tf_op jit(solution)/shard_map/ppermute | solution.py:26
  73.0 0.1 fusion.3
  73.1 2.0 %collective-permute-done.11 = f32[3,2,16,480]{3,2,1,0:T(8,128)S(1)} collective-permute-done((f32[3,2,16,480]{3,2,1,0:T(8,128)S(1)}, f32[3,2,16,480]{3,2,1,0:T(8,128)S(1)}, u32[]{:S(2)}, u32[]{:S(2)}) %collective-permute-start.11) | collective-permute-done | bytes 184352 | tf_op jit(solution)/shard_map/ppermute | solution.py:26
  75.1 2.7 %collective-permute-done.12 = f32[3,2,16,480]{3,2,1,0:T(8,128)S(1)} collective-permute-done((f32[3,2,16,480]{3,2,1,0:T(8,128)S(1)}, f32[3,2,16,480]{3,2,1,0:T(8,128)S(1)}, u32[]{:S(2)}, u32[]{:S(2)}) %collective-permute-start.12) | collective-permute-done | bytes 184352 | tf_op jit(solution)/shard_map/ppermute | solution.py:26
  77.8 0.0 copy-start.3
  77.8 0.0 copy-start.4
  77.8 0.0 copy-start.5
  77.9 0.1 dynamic-slice_bitcast_fusion.2
  78.0 1.9 %collective-permute-start.13 = (f32[4,16,480]{2,1,0:T(8,128)S(1)}, f32[4,16,480]{2,1,0:T(8,128)S(1)}, u32[]{:S(2)}, u32[]{:S(2)}) collective-permute-start(f32[4,16,480]{2,1,0:T(8,128)S(1)} %get-tuple-element.31), channel_id=1, source_target_pairs={{0,1},{1,64},{2,3},{3,66},{4,5},{5,68},{6,7},{7,70},{8,9},{9,72},{... | collective-permute-start | bytes 368648 | tf_op jit(solution)/shard_map/ppermute | solution.py:26
  79.9 0.7 collective-permute-start.14
  80.6 20.7 %collective-permute-start.15 = (f32[4,16,480]{2,1,0:T(8,128)S(1)}, f32[4,16,480]{2,1,0:T(8,128)S(1)}, u32[]{:S(2)}, u32[]{:S(2)}) collective-permute-start(f32[4,16,480]{2,1,0:T(8,128)S(1)} %get-tuple-element.30), channel_id=1, source_target_pairs={{0,897},{1,960},{2,899},{3,962},{4,901},{5,964},{6,903},{7,966},{8... | collective-permute-start | bytes 368648 | tf_op jit(solution)/shard_map/ppermute | solution.py:26
  101.3 1.9 %collective-permute-start.16 = (f32[4,16,480]{2,1,0:T(8,128)S(1)}, f32[4,16,480]{2,1,0:T(8,128)S(1)}, u32[]{:S(2)}, u32[]{:S(2)}) collective-permute-start(f32[4,16,480]{2,1,0:T(8,128)S(1)} %get-tuple-element.32), channel_id=1, source_target_pairs={{0,896},{1,961},{2,898},{3,963},{4,900},{5,965},{6,902},{7,967},{8... | collective-permute-start | bytes 368648 | tf_op jit(solution)/shard_map/ppermute | solution.py:26
  103.2 0.0 collective-permute-done.13
  103.3 0.0 collective-permute-done.14
  103.3 4.1 %collective-permute-done.15 = f32[4,16,480]{2,1,0:T(8,128)S(1)} collective-permute-done((f32[4,16,480]{2,1,0:T(8,128)S(1)}, f32[4,16,480]{2,1,0:T(8,128)S(1)}, u32[]{:S(2)}, u32[]{:S(2)}) %collective-permute-start.15) | collective-permute-done | bytes 122912 | tf_op jit(solution)/shard_map/ppermute | solution.py:26
  107.4 2.9 %collective-permute-done.16 = f32[4,16,480]{2,1,0:T(8,128)S(1)} collective-permute-done((f32[4,16,480]{2,1,0:T(8,128)S(1)}, f32[4,16,480]{2,1,0:T(8,128)S(1)}, u32[]{:S(2)}, u32[]{:S(2)}) %collective-permute-start.16) | collective-permute-done | bytes 122912 | tf_op jit(solution)/shard_map/ppermute | solution.py:26
  110.3 0.7 add_add_fusion.1
  111.0 8.5 %all-to-all-start = ((f32[4,16,480]{2,1,0:T(8,128)}), f32[4,16,480]{2,1,0:T(8,128)S(1)}, u32[]{:S(2)}, u32[]{:S(2)}) async-start(f32[4,16,480]{2,1,0:T(8,128)} %add_add_fusion.1), calls=%async_computation | async-start | bytes 262144 | tf_op jit(solution)/shard_map/all_to_all | solution.py:125
  119.5 0.0 copy-done.3
  119.5 0.1 broadcast_subtract_fusion
  119.6 0.1 sub.54
  119.7 0.0 copy-done.5
  119.7 0.1 broadcast_subtract_fusion.1
  119.8 0.1 sub.50
  119.8 0.1 dynamic_slice.40
  119.9 0.1 dynamic_slice.39
  120.0 8.7 %all-to-all-done = f32[4,16,480]{2,1,0:T(8,128)S(1)} async-done(((f32[4,16,480]{2,1,0:T(8,128)}), f32[4,16,480]{2,1,0:T(8,128)S(1)}, u32[]{:S(2)}, u32[]{:S(2)}) %all-to-all-start) | async-done | bytes 122912 | tf_op jit(solution)/shard_map/all_to_all | solution.py:125
  128.7 0.7 fusion.20
  (30 shorter events, 0.4 us)
Async XLA Ops:
  0.0 44.2 %collective-permute-start.6 = (f32[1125,480]{0,1:T(8,128)}, f32[1125,480]{0,1:T(8,128)S(1)}, u32[]{:S(2)}, u32[]{:S(2)}) collective-permute-start(f32[1125,480]{0,1:T(8,128)} %param.6), channel_id=1, source_target_pairs={{0,1},{1,0},{2,3},{3,2},{4,5},{5,4},{6,7},{7,6},{8,9},{9,8},{10,11... | collective-permute-start | bytes 6480008 | tf_op jit(solution)/shard_map/ppermute | solution.py:26
  3.2 30.7 %copy-start = (f32[1125,480]{0,1:T(8,128)S(1)}, f32[1125,480]{0,1:T(8,128)}, u32[]{:S(2)}) copy-start(f32[1125,480]{0,1:T(8,128)} %param.6) | copy-start | bytes 6480004
  3.2 10.5 %collective-permute-start = (f32[64,1125]{1,0:T(8,128)S(1)}, f32[64,1125]{1,0:T(8,128)S(1)}, u32[]{:S(2)}, u32[]{:S(2)}) collective-permute-start(f32[64,1125]{1,0:T(8,128)S(1)} %pad_maximum_fusion.1), channel_id=1, source_target_pairs={{0,2},{1,15},{2,4},{3,1},{4,6},{5,3},{6,8},{7,5},{8,10},{9,7},{10,... | collective-permute-start | bytes 864008 | tf_op jit(solution)/shard_map/ppermute | solution.py:26
  8.0 11.3 %collective-permute-start.3 = (f32[64,1125]{1,0:T(8,128)S(1)}, f32[64,1125]{1,0:T(8,128)S(1)}, u32[]{:S(2)}, u32[]{:S(2)}) collective-permute-start(f32[64,1125]{1,0:T(8,128)S(1)} %pad_maximum_fusion.1), channel_id=1, source_target_pairs={{0,14},{1,3},{2,0},{3,5},{4,2},{5,7},{6,4},{7,9},{8,6},{9,11},{10,... | collective-permute-start | bytes 864008 | tf_op jit(solution)/shard_map/ppermute | solution.py:26
  13.7 12.5 %collective-permute-start.1 = (f32[64,1125]{1,0:T(8,128)S(1)}, f32[64,1125]{1,0:T(8,128)S(1)}, u32[]{:S(2)}, u32[]{:S(2)}) collective-permute-start(f32[64,1125]{1,0:T(8,128)S(1)} %collective-permute-done), channel_id=1, source_target_pairs={{0,2},{1,15},{2,4},{3,1},{4,6},{5,3},{6,8},{7,5},{8,10},{9,7},{10,... | collective-permute-start | bytes 864008 | tf_op jit(solution)/shard_map/ppermute | solution.py:26
  19.4 12.5 %collective-permute-start.4 = (f32[64,1125]{1,0:T(8,128)S(1)}, f32[64,1125]{1,0:T(8,128)S(1)}, u32[]{:S(2)}, u32[]{:S(2)}) collective-permute-start(f32[64,1125]{1,0:T(8,128)S(1)} %collective-permute-done.3), channel_id=1, source_target_pairs={{0,14},{1,3},{2,0},{3,5},{4,2},{5,7},{6,4},{7,9},{8,6},{9,11},{10,... | collective-permute-start | bytes 864008 | tf_op jit(solution)/shard_map/ppermute | solution.py:26
  26.2 12.3 %collective-permute-start.2 = (f32[64,1125]{1,0:T(8,128)S(1)}, f32[64,1125]{1,0:T(8,128)S(1)}, u32[]{:S(2)}, u32[]{:S(2)}) collective-permute-start(f32[64,1125]{1,0:T(8,128)S(1)} %collective-permute-done.1), channel_id=1, source_target_pairs={{0,2},{1,15},{2,4},{3,1},{4,6},{5,3},{6,8},{7,5},{8,10},{9,7},{10,... | collective-permute-start | bytes 864008 | tf_op jit(solution)/shard_map/ppermute | solution.py:26
  31.9 14.0 %collective-permute-start.5 = (f32[64,1125]{1,0:T(8,128)S(1)}, f32[64,1125]{1,0:T(8,128)S(1)}, u32[]{:S(2)}, u32[]{:S(2)}) collective-permute-start(f32[64,1125]{1,0:T(8,128)S(1)} %collective-permute-done.4), channel_id=1, source_target_pairs={{0,14},{1,3},{2,0},{3,5},{4,2},{5,7},{6,4},{7,9},{8,6},{9,11},{10,... | collective-permute-start | bytes 864008 | tf_op jit(solution)/shard_map/ppermute | solution.py:26
  38.5 10.3 %collective-permute-start.7 = (f32[64,1125]{1,0:T(8,128)S(1)}, f32[64,1125]{1,0:T(8,128)S(1)}, u32[]{:S(2)}, u32[]{:S(2)}) collective-permute-start(f32[64,1125]{1,0:T(8,128)S(1)} %collective-permute-done.2), channel_id=1, source_target_pairs={{0,2},{1,15},{2,4},{3,1},{4,6},{5,3},{6,8},{7,5},{8,10},{9,7},{10,... | collective-permute-start | bytes 864008 | tf_op jit(solution)/shard_map/ppermute | solution.py:26
  46.0 13.7 %collective-permute-start.9 = (f32[5,2,2,16,480]{4,3,0,1,2:T(8,128)S(1)}, f32[5,2,2,16,480]{4,3,0,1,2:T(8,128)S(1)}, u32[]{:S(2)}, u32[]{:S(2)}) collective-permute-start(f32[5,2,2,16,480]{4,3,0,1,2:T(8,128)S(1)} %slice.97), channel_id=1, source_target_pairs={{0,16},{1,49},{2,18},{3,51},{4,20},{5,53},{6,22},{7,55},{8,24},{9,... | collective-permute-start | bytes 1843208 | tf_op jit(solution)/shard_map/ppermute | solution.py:26
  51.3 19.5 %collective-permute-start.8 = (f32[3,2,16,480]{3,2,1,0:T(8,128)S(1)}, f32[3,2,16,480]{3,2,1,0:T(8,128)S(1)}, u32[]{:S(2)}, u32[]{:S(2)}) collective-permute-start(f32[3,2,16,480]{3,2,1,0:T(8,128)S(1)} %bitcast.106), channel_id=1, source_target_pairs={{0,16},{1,49},{2,18},{3,51},{4,20},{5,53},{6,22},{7,55},{8,24},{9,... | collective-permute-start | bytes 552968 | tf_op jit(solution)/shard_map/ppermute | solution.py:26
  59.7 0.8 copy-start.1
  61.3 11.6 %copy-start.2 = (f32[5,2,2,16,480]{4,3,0,1,2:T(8,128)S(1)}, f32[5,2,2,16,480]{4,3,0,1,2:T(8,128)}, u32[]{:S(2)}) copy-start(f32[5,2,2,16,480]{4,3,0,1,2:T(8,128)} %copy-done.1) | copy-start | bytes 1843204
  61.3 11.6 %collective-permute-start.10 = (f32[5,2,16,480]{3,2,0,1:T(8,128)}, f32[5,2,16,480]{3,2,0,1:T(8,128)S(1)}, u32[]{:S(2)}, u32[]{:S(2)}) collective-permute-start(f32[5,2,16,480]{3,2,0,1:T(8,128)} %fusion.1), channel_id=1, source_target_pairs={{0,48},{1,17},{2,50},{3,19},{4,52},{5,21},{6,54},{7,23},{8,56},{9,... | collective-permute-start | bytes 921608 | tf_op jit(solution)/shard_map/ppermute | solution.py:26
  63.5 11.6 %collective-permute-start.11 = (f32[3,2,16,480]{3,2,1,0:T(8,128)S(1)}, f32[3,2,16,480]{3,2,1,0:T(8,128)S(1)}, u32[]{:S(2)}, u32[]{:S(2)}) collective-permute-start(f32[3,2,16,480]{3,2,1,0:T(8,128)S(1)} %bitcast.107), channel_id=1, source_target_pairs={{0,48},{1,17},{2,50},{3,19},{4,52},{5,21},{6,54},{7,23},{8,56},{9,... | collective-permute-start | bytes 552968 | tf_op jit(solution)/shard_map/ppermute | solution.py:26
  68.7 9.1 %collective-permute-start.12 = (f32[3,2,16,480]{3,2,1,0:T(8,128)S(1)}, f32[3,2,16,480]{3,2,1,0:T(8,128)S(1)}, u32[]{:S(2)}, u32[]{:S(2)}) collective-permute-start(f32[3,2,16,480]{3,2,1,0:T(8,128)S(1)} %bitcast.108), channel_id=1, source_target_pairs={{0,32},{1,33},{2,34},{3,35},{4,36},{5,37},{6,38},{7,39},{8,40},{9,... | collective-permute-start | bytes 552968 | tf_op jit(solution)/shard_map/ppermute | solution.py:26
  77.8 41.7 %copy-start.3 = (f32[60]{0:T(128)S(1)}, f32[60]{0:T(128)}, u32[]{:S(2)}) copy-start(f32[60]{0:T(128)} %param.7) | copy-start | bytes 724
  77.8 41.7 %copy-start.4 = (f32[128]{0:T(128)S(1)}, f32[128]{0:T(128)}, u32[]{:S(2)}) copy-start(f32[128]{0:T(128)} %param.9) | copy-start | bytes 1540
  77.8 41.9 %copy-start.5 = (f32[16]{0:T(128)S(1)}, f32[16]{0:T(128)}, u32[]{:S(2)}) copy-start(f32[16]{0:T(128)} %param.8) | copy-start | bytes 196
  78.0 25.3 %collective-permute-start.13 = (f32[4,16,480]{2,1,0:T(8,128)S(1)}, f32[4,16,480]{2,1,0:T(8,128)S(1)}, u32[]{:S(2)}, u32[]{:S(2)}) collective-permute-start(f32[4,16,480]{2,1,0:T(8,128)S(1)} %get-tuple-element.31), channel_id=1, source_target_pairs={{0,1},{1,64},{2,3},{3,66},{4,5},{5,68},{6,7},{7,70},{8,9},{9,72},{... | collective-permute-start | bytes 368648 | tf_op jit(solution)/shard_map/ppermute | solution.py:26
  79.9 23.3 %collective-permute-start.14 = (f32[4,16,480]{2,1,0:T(8,128)S(1)}, f32[4,16,480]{2,1,0:T(8,128)S(1)}, u32[]{:S(2)}, u32[]{:S(2)}) collective-permute-start(f32[4,16,480]{2,1,0:T(8,128)S(1)} %get-tuple-element.29), channel_id=1, source_target_pairs={{0,0},{1,65},{2,2},{3,67},{4,4},{5,69},{6,6},{7,71},{8,8},{9,73},{... | collective-permute-start | bytes 368648 | tf_op jit(solution)/shard_map/ppermute | solution.py:26
  80.6 26.8 %collective-permute-start.15 = (f32[4,16,480]{2,1,0:T(8,128)S(1)}, f32[4,16,480]{2,1,0:T(8,128)S(1)}, u32[]{:S(2)}, u32[]{:S(2)}) collective-permute-start(f32[4,16,480]{2,1,0:T(8,128)S(1)} %get-tuple-element.30), channel_id=1, source_target_pairs={{0,897},{1,960},{2,899},{3,962},{4,901},{5,964},{6,903},{7,966},{8... | collective-permute-start | bytes 368648 | tf_op jit(solution)/shard_map/ppermute | solution.py:26
  101.3 9.0 %collective-permute-start.16 = (f32[4,16,480]{2,1,0:T(8,128)S(1)}, f32[4,16,480]{2,1,0:T(8,128)S(1)}, u32[]{:S(2)}, u32[]{:S(2)}) collective-permute-start(f32[4,16,480]{2,1,0:T(8,128)S(1)} %get-tuple-element.32), channel_id=1, source_target_pairs={{0,896},{1,961},{2,898},{3,963},{4,900},{5,965},{6,902},{7,967},{8... | collective-permute-start | bytes 368648 | tf_op jit(solution)/shard_map/ppermute | solution.py:26
  111.0 17.7 %all-to-all-start = ((f32[4,16,480]{2,1,0:T(8,128)}), f32[4,16,480]{2,1,0:T(8,128)S(1)}, u32[]{:S(2)}, u32[]{:S(2)}) async-start(f32[4,16,480]{2,1,0:T(8,128)} %add_add_fusion.1), calls=%async_computation | async-start | bytes 262144 | tf_op jit(solution)/shard_map/all_to_all | solution.py:125

commit v8 on v7

--- a/solution.py
+++ b/solution.py
@@ -55,6 +55,10 @@
     return move
 
 
+def lines_x():
+    return [[device(z, x, y, c) for x in range(X)] for z in range(Z) for y in range(Y) for c in range(CORES)]
+
+
 def classes():
     groups = []
     for r in range(4):
@@ -77,9 +81,7 @@
 
     side = jnp.where((x % 2 == 0) == (c == 0), 1, -1)
     block = jnp.pad(amplitudes.reshape(X, share, depth), ((0, 0), (0, 16 - share), (0, 0)))
-    block = jnp.concatenate(
-        [lax.dynamic_index_in_dim(block, (x + side * k) % X, 0, keepdims=False) for k in range(X)], 0
-    )
+    block = block.reshape(X * 16, depth)
     f1 = send(block, along_y(1))
     h1 = send(block, along_y(-1))
     others = send(integrals, other_core)
@@ -99,15 +101,18 @@
     f4 = send(f3_after, along_y(1))
     early = jnp.stack([own, product(near_blocks, others)], 1)
     h3_after, early = lax.optimization_barrier((h3, early))
-    arrived = send(early[:, :, 1:3], along_x(1))
-    passed_on = early[:, :, 3] + arrived[:, :, 1]
+
+    def place(k):
+        return lax.dynamic_index_in_dim(early, (x + side * k) % X, 2, keepdims=False)
+
+    arrived = send(jnp.stack([place(1), place(2)], 0), along_x(1))
+    passed_on = place(3) + arrived[1]
     far_blocks = (f3, h3_after, f4)
     late = jnp.stack([product(far_blocks, integrals), product(far_blocks, others)], 1)
-    late_first = send(late[:, :, 1], along_x(1))
-    late_last, late_far = late[:, :, 3], late[:, :, 2]
-    first = early[:, :, 0] + arrived[:, :, 0] + send(passed_on, along_x(-1))
-    second, first = lax.optimization_barrier((late[:, :, 0] + late_first, first))
-    second = second + send(late_last, along_x(-1)) + send(late_far, along_x(2))
+    late = late.transpose(2, 0, 1, 3, 4)
+    first = place(0) + arrived[0] + send(passed_on, along_x(-1))
+    second = lax.all_to_all(late, AXES, 0, 0, tiled=True, axis_index_groups=lines_x())
+    second = second[0] + second[1] + second[2] + second[3]
     pieces = jnp.stack(
         [first[0], first[3], second[2], first[4], first[1], first[2], second[0], second[1]], 1
     )

time: 130 us -> 128 us (0.985)
  the two profiles are of different devices: /device:TPU:30 before, /device:TPU:1 now
where the time goes in v8:
time: 128 us; the launch traced here: 127 us
  starting transfers between devices  68.6 us (54%)
  waiting for transfers between devices  44.9 us (35%)
  other arithmetic  5.66 us (4%)
  matrix products  5.41 us (4%)
  local copies, waits for them, and re-layouts  1.79 us (1%)
    ppermute x14, starting transfers between devices, send(): return lax.ppermute(array, AXES, table(move))  61.8 us
    ppermute x14, waiting for transfers between devices, send(): return lax.ppermute(array, AXES, table(move))  27.9 us
    all_to_all x1, waiting for transfers between devices, per_device(): lax.all_to_all(total, AXES, 0, 0, tiled=True, axis_index_groups=classes())  14 us
    dot_general x4, matrix products, product(): jnp.dot(tall, part, precision=lax.Precision.HIGH, preferred_element_type=...  5.41 us
    all_to_all x1, starting transfers between devices, per_device(): lax.all_to_all(late, AXES, 0, 0, tiled=True, axis_index_groups=lines_x())  3.49 us
    all_to_all x1, starting transfers between devices, per_device(): lax.all_to_all(total, AXES, 0, 0, tiled=True, axis_index_groups=classes())  3.32 us
    all_to_all x1, waiting for transfers between devices, per_device(): lax.all_to_all(late, AXES, 0, 0, tiled=True, axis_index_groups=lines_x())  2.98 us
  transfers between devices with their start and end apart: 16, of which 11 were waited for; matrix products, arithmetic and copies ran while one was open for 8% of the time, Pallas kernels for 0%

profile of v8, /device:TPU:1, one launch (start us, length us, event | category | flops | bytes accessed | tf_op | source)
XLA Modules:
  0.0 127.1 jit_solution(52635374544445253)
XLA Ops:
  0.0 16.1 %collective-permute-start.6 = (f32[1125,480]{0,1:T(8,128)}, f32[1125,480]{0,1:T(8,128)S(1)}, u32[]{:S(2)}, u32[]{:S(2)}) collective-permute-start(f32[1125,480]{0,1:T(8,128)} %param.6), channel_id=1, source_target_pairs={{0,1},{1,0},{2,3},{3,2},{4,5},{5,4},{6,7},{7,6},{8,9},{9,8},{10,11... | collective-permute-start | bytes 6480008 | tf_op jit(solution)/shard_map/ppermute | solution.py:26
  16.1 1.0 reshape.52
  17.1 1.9 %collective-permute-start = (f32[64,1125]{1,0:T(8,128)S(1)}, f32[64,1125]{1,0:T(8,128)S(1)}, u32[]{:S(2)}, u32[]{:S(2)}) collective-permute-start(f32[64,1125]{1,0:T(8,128)S(1)} %bitcast.86), channel_id=1, source_target_pairs={{0,14},{1,3},{2,0},{3,5},{4,2},{5,7},{6,4},{7,9},{8,6},{9,11},{10,... | collective-permute-start | bytes 864008 | tf_op jit(solution)/shard_map/ppermute | solution.py:26
  19.0 4.6 %collective-permute-start.3 = (f32[64,1125]{1,0:T(8,128)S(1)}, f32[64,1125]{1,0:T(8,128)S(1)}, u32[]{:S(2)}, u32[]{:S(2)}) collective-permute-start(f32[64,1125]{1,0:T(8,128)S(1)} %bitcast.87), channel_id=1, source_target_pairs={{0,2},{1,15},{2,4},{3,1},{4,6},{5,3},{6,8},{7,5},{8,10},{9,7},{10,... | collective-permute-start | bytes 864008 | tf_op jit(solution)/shard_map/ppermute | solution.py:26
  23.7 0.0 copy-start
  23.7 3.0 %collective-permute-done = f32[64,1125]{1,0:T(8,128)S(1)} collective-permute-done((f32[64,1125]{1,0:T(8,128)S(1)}, f32[64,1125]{1,0:T(8,128)S(1)}, u32[]{:S(2)}, u32[]{:S(2)}) %collective-permute-start) | collective-permute-done | bytes 288032 | tf_op jit(solution)/shard_map/ppermute | solution.py:26
  26.8 1.9 %collective-permute-start.1 = (f32[64,1125]{1,0:T(8,128)S(1)}, f32[64,1125]{1,0:T(8,128)S(1)}, u32[]{:S(2)}, u32[]{:S(2)}) collective-permute-start(f32[64,1125]{1,0:T(8,128)S(1)} %collective-permute-done), channel_id=1, source_target_pairs={{0,14},{1,3},{2,0},{3,5},{4,2},{5,7},{6,4},{7,9},{8,6},{9,11},{10,... | collective-permute-start | bytes 864008 | tf_op jit(solution)/shard_map/ppermute | solution.py:26
  28.7 0.0 collective-permute-done.3
  28.7 4.6 %collective-permute-start.4 = (f32[64,1125]{1,0:T(8,128)S(1)}, f32[64,1125]{1,0:T(8,128)S(1)}, u32[]{:S(2)}, u32[]{:S(2)}) collective-permute-start(f32[64,1125]{1,0:T(8,128)S(1)} %collective-permute-done.3), channel_id=1, source_target_pairs={{0,2},{1,15},{2,4},{3,1},{4,6},{5,3},{6,8},{7,5},{8,10},{9,7},{10,... | collective-permute-start | bytes 864008 | tf_op jit(solution)/shard_map/ppermute | solution.py:26
  33.3 2.1 %collective-permute-done.1 = f32[64,1125]{1,0:T(8,128)S(1)} collective-permute-done((f32[64,1125]{1,0:T(8,128)S(1)}, f32[64,1125]{1,0:T(8,128)S(1)}, u32[]{:S(2)}, u32[]{:S(2)}) %collective-permute-start.1) | collective-permute-done | bytes 288032 | tf_op jit(solution)/shard_map/ppermute | solution.py:26
  35.4 1.9 %collective-permute-start.2 = (f32[64,1125]{1,0:T(8,128)S(1)}, f32[64,1125]{1,0:T(8,128)S(1)}, u32[]{:S(2)}, u32[]{:S(2)}) collective-permute-start(f32[64,1125]{1,0:T(8,128)S(1)} %collective-permute-done.1), channel_id=1, source_target_pairs={{0,14},{1,3},{2,0},{3,5},{4,2},{5,7},{6,4},{7,9},{8,6},{9,11},{10,... | collective-permute-start | bytes 864008 | tf_op jit(solution)/shard_map/ppermute | solution.py:26
  37.3 1.4 %collective-permute-done.4 = f32[64,1125]{1,0:T(8,128)S(1)} collective-permute-done((f32[64,1125]{1,0:T(8,128)S(1)}, f32[64,1125]{1,0:T(8,128)S(1)}, u32[]{:S(2)}, u32[]{:S(2)}) %collective-permute-start.4) | collective-permute-done | bytes 288032 | tf_op jit(solution)/shard_map/ppermute | solution.py:26
  38.7 3.2 %collective-permute-start.5 = (f32[64,1125]{1,0:T(8,128)S(1)}, f32[64,1125]{1,0:T(8,128)S(1)}, u32[]{:S(2)}, u32[]{:S(2)}) collective-permute-start(f32[64,1125]{1,0:T(8,128)S(1)} %collective-permute-done.4), channel_id=1, source_target_pairs={{0,2},{1,15},{2,4},{3,1},{4,6},{5,3},{6,8},{7,5},{8,10},{9,7},{10,... | collective-permute-start | bytes 864008 | tf_op jit(solution)/shard_map/ppermute | solution.py:26
  42.0 0.0 copy-done
  42.0 1.6 %fusion.14 = f32[320,480]{1,0:T(8,128)S(1)} fusion(f32[320,1125]{1,0:T(8,128)S(1)} %constant_dynamic-update-slice_fusion, f32[1125,480]{0,1:T(8,128)S(1)} %copy-done), kind=kOutput, calls=%fused_computation.52 | convolution fusion | flops 1036800000 | bytes 4214400 | tf_op jit(solution)/shard_map/dot_general | solution.py:93
  43.6 6.1 %collective-permute-done.5 = f32[64,1125]{1,0:T(8,128)S(1)} collective-permute-done((f32[64,1125]{1,0:T(8,128)S(1)}, f32[64,1125]{1,0:T(8,128)S(1)}, u32[]{:S(2)}, u32[]{:S(2)}) %collective-permute-start.5) | collective-permute-done | bytes 288032 | tf_op jit(solution)/shard_map/ppermute | solution.py:26
  49.6 0.1 copy.21
  49.7 2.6 %collective-permute-start.9 = (f32[64,1125]{1,0:T(8,128)S(1)}, f32[64,1125]{1,0:T(8,128)S(1)}, u32[]{:S(2)}, u32[]{:S(2)}) collective-permute-start(f32[64,1125]{1,0:T(8,128)S(1)} %collective-permute-done.5), channel_id=1, source_target_pairs={{0,2},{1,15},{2,4},{3,1},{4,6},{5,3},{6,8},{7,5},{8,10},{9,7},{10,... | collective-permute-start | bytes 864008 | tf_op jit(solution)/shard_map/ppermute | solution.py:26
  52.3 0.0 collective-permute-done.6
  52.3 1.5 %fusion.15 = f32[320,480]{1,0:T(8,128)S(1)} fusion(f32[320,1125]{1,0:T(8,128)S(1)} %constant_dynamic-update-slice_fusion, f32[1125,480]{0,1:T(8,128)S(1)} %collective-permute-done.6), kind=kOutput, calls=%fused_computation.53 | convolution fusion | flops 1036800000 | bytes 4214400 | tf_op jit(solution)/shard_map/dot_general | solution.py:93
  53.8 0.1 pad_maximum_fusion
  54.0 0.0 collective-permute-done.2
  54.0 0.1 dynamic-slice_bitcast_fusion.1
  54.0 0.9 pad_maximum_fusion.2
  54.9 1.9 %collective-permute-start.7 = (f32[2,5,2,16,480]{4,3,2,1,0:T(8,128)}, f32[2,5,2,16,480]{4,3,2,1,0:T(8,128)}, u32[]{:S(2)}, u32[]{:S(2)}) collective-permute-start(f32[2,5,2,16,480]{4,3,2,1,0:T(8,128)} %pad_maximum_fusion.2), channel_id=1, source_target_pairs={{0,16},{1,49},{2,18},{3,51},{4,20},{5,53},{6,22},{7,55},{8,24},{9,... | collective-permute-start | bytes 1843208 | tf_op jit(solution)/shard_map/ppermute | solution.py:26
  56.9 0.6 collective-permute-done.9
  57.5 1.2 fusion.16
  58.7 1.2 fusion.17
  59.9 1.0 copy_bitcast_fusion
  60.8 3.5 %all-to-all-start = ((f32[4,3,2,16,480]{4,3,2,1,0:T(8,128)}), f32[4,3,2,16,480]{4,3,2,1,0:T(8,128)S(1)}, u32[]{:S(2)}, u32[]{:S(2)}) async-start(f32[4,3,2,16,480]{4,3,2,1,0:T(8,128)} %copy_bitcast_fusion), calls=%async_computation | async-start | bytes 1572864 | tf_op jit(solution)/shard_map/all_to_all | solution.py:114
  64.4 3.4 %collective-permute-done.7 = f32[2,5,2,16,480]{4,3,2,1,0:T(8,128)} collective-permute-done((f32[2,5,2,16,480]{4,3,2,1,0:T(8,128)}, f32[2,5,2,16,480]{4,3,2,1,0:T(8,128)}, u32[]{:S(2)}, u32[]{:S(2)}) %collective-permute-start.7) | collective-permute-done | bytes 614432 | tf_op jit(solution)/shard_map/ppermute | solution.py:26
  67.8 1.0 fusion
  68.8 1.9 %collective-permute-start.8 = (f32[5,2,16,480]{3,2,1,0:T(8,128)S(1)}, f32[5,2,16,480]{3,2,1,0:T(8,128)S(1)}, u32[]{:S(2)}, u32[]{:S(2)}) collective-permute-start(f32[5,2,16,480]{3,2,1,0:T(8,128)S(1)} %fusion), channel_id=1, source_target_pairs={{0,48},{1,17},{2,50},{3,19},{4,52},{5,21},{6,54},{7,23},{8,56},{9,... | collective-permute-start | bytes 921608 | tf_op jit(solution)/shard_map/ppermute | solution.py:26
  70.9 3.0 %all-to-all-done = f32[4,3,2,16,480]{4,3,2,1,0:T(8,128)S(1)} async-done(((f32[4,3,2,16,480]{4,3,2,1,0:T(8,128)}), f32[4,3,2,16,480]{4,3,2,1,0:T(8,128)S(1)}, u32[]{:S(2)}, u32[]{:S(2)}) %all-to-all-start) | async-done | bytes 737312 | tf_op jit(solution)/shard_map/all_to_all | solution.py:114
  73.9 0.1 slice_add_fusion
  73.9 5.8 %collective-permute-done.8 = f32[5,2,16,480]{3,2,1,0:T(8,128)S(1)} collective-permute-done((f32[5,2,16,480]{3,2,1,0:T(8,128)S(1)}, f32[5,2,16,480]{3,2,1,0:T(8,128)S(1)}, u32[]{:S(2)}, u32[]{:S(2)}) %collective-permute-start.8) | collective-permute-done | bytes 307232 | tf_op jit(solution)/shard_map/ppermute | solution.py:26
  79.7 1.0 fusion.2
  80.8 0.0 copy-start.1
  80.8 0.0 copy-start.2
  80.8 0.0 copy-start.3
  80.9 0.1 dynamic-slice_bitcast_fusion.4
  81.0 11.7 %collective-permute-start.13 = (f32[4,16,480]{2,1,0:T(8,128)S(1)}, f32[4,16,480]{2,1,0:T(8,128)S(1)}, u32[]{:S(2)}, u32[]{:S(2)}) collective-permute-start(f32[4,16,480]{2,1,0:T(8,128)S(1)} %get-tuple-element.16), channel_id=1, source_target_pairs={{0,896},{1,961},{2,898},{3,963},{4,900},{5,965},{6,902},{7,967},{8... | collective-permute-start | bytes 368648 | tf_op jit(solution)/shard_map/ppermute | solution.py:26
  92.7 3.7 %collective-permute-start.12 = (f32[4,16,480]{2,1,0:T(8,128)S(1)}, f32[4,16,480]{2,1,0:T(8,128)S(1)}, u32[]{:S(2)}, u32[]{:S(2)}) collective-permute-start(f32[4,16,480]{2,1,0:T(8,128)S(1)} %get-tuple-element.17), channel_id=1, source_target_pairs={{0,897},{1,960},{2,899},{3,962},{4,901},{5,964},{6,903},{7,966},{8... | collective-permute-start | bytes 368648 | tf_op jit(solution)/shard_map/ppermute | solution.py:26
  96.4 3.9 %collective-permute-start.10 = (f32[4,16,480]{2,1,0:T(8,128)S(1)}, f32[4,16,480]{2,1,0:T(8,128)S(1)}, u32[]{:S(2)}, u32[]{:S(2)}) collective-permute-start(f32[4,16,480]{2,1,0:T(8,128)S(1)} %get-tuple-element.18), channel_id=1, source_target_pairs={{0,1},{1,64},{2,3},{3,66},{4,5},{5,68},{6,7},{7,70},{8,9},{9,72},{... | collective-permute-start | bytes 368648 | tf_op jit(solution)/shard_map/ppermute | solution.py:26
  100.3 1.9 %collective-permute-start.11 = (f32[4,16,480]{2,1,0:T(8,128)S(1)}, f32[4,16,480]{2,1,0:T(8,128)S(1)}, u32[]{:S(2)}, u32[]{:S(2)}) collective-permute-start(f32[4,16,480]{2,1,0:T(8,128)S(1)} %get-tuple-element.15), channel_id=1, source_target_pairs={{0,0},{1,65},{2,2},{3,67},{4,4},{5,69},{6,6},{7,71},{8,8},{9,73},{... | collective-permute-start | bytes 368648 | tf_op jit(solution)/shard_map/ppermute | solution.py:26
  102.2 0.0 collective-permute-done.13
  102.3 0.0 collective-permute-done.12
  102.3 0.9 collective-permute-done.10
  103.2 4.6 %collective-permute-done.11 = f32[4,16,480]{2,1,0:T(8,128)S(1)} collective-permute-done((f32[4,16,480]{2,1,0:T(8,128)S(1)}, f32[4,16,480]{2,1,0:T(8,128)S(1)}, u32[]{:S(2)}, u32[]{:S(2)}) %collective-permute-start.11) | collective-permute-done | bytes 122912 | tf_op jit(solution)/shard_map/ppermute | solution.py:26
  107.8 0.7 add_add_fusion
  108.5 3.3 %all-to-all-start.1 = ((f32[4,16,480]{2,1,0:T(8,128)}), f32[4,16,480]{2,1,0:T(8,128)S(1)}, u32[]{:S(2)}, u32[]{:S(2)}) async-start(f32[4,16,480]{2,1,0:T(8,128)} %add_add_fusion), calls=%async_computation.1 | async-start | bytes 262144 | tf_op jit(solution)/shard_map/all_to_all | solution.py:130
  111.8 0.0 copy-done.1
  111.8 0.0 copy-done.2
  111.8 0.1 broadcast_subtract_fusion
  111.9 0.1 sub.54
  112.0 0.0 copy-done.3
  112.0 0.1 broadcast_subtract_fusion.1
  112.1 0.1 sub.50
  112.2 0.1 dynamic_slice.40
  112.3 0.1 dynamic_slice.39
  112.4 14.0 %all-to-all-done.1 = f32[4,16,480]{2,1,0:T(8,128)S(1)} async-done(((f32[4,16,480]{2,1,0:T(8,128)}), f32[4,16,480]{2,1,0:T(8,128)S(1)}, u32[]{:S(2)}, u32[]{:S(2)}) %all-to-all-start.1) | async-done | bytes 122912 | tf_op jit(solution)/shard_map/all_to_all | solution.py:130
  126.4 0.7 fusion.12
  (18 shorter events, 0.3 us)
Async XLA Ops:
  0.0 52.3 %collective-permute-start.6 = (f32[1125,480]{0,1:T(8,128)}, f32[1125,480]{0,1:T(8,128)S(1)}, u32[]{:S(2)}, u32[]{:S(2)}) collective-permute-start(f32[1125,480]{0,1:T(8,128)} %param.6), channel_id=1, source_target_pairs={{0,1},{1,0},{2,3},{3,2},{4,5},{5,4},{6,7},{7,6},{8,9},{9,8},{10,11... | collective-permute-start | bytes 6480008 | tf_op jit(solution)/shard_map/ppermute | solution.py:26
  17.1 9.7 %collective-permute-start = (f32[64,1125]{1,0:T(8,128)S(1)}, f32[64,1125]{1,0:T(8,128)S(1)}, u32[]{:S(2)}, u32[]{:S(2)}) collective-permute-start(f32[64,1125]{1,0:T(8,128)S(1)} %bitcast.86), channel_id=1, source_target_pairs={{0,14},{1,3},{2,0},{3,5},{4,2},{5,7},{6,4},{7,9},{8,6},{9,11},{10,... | collective-permute-start | bytes 864008 | tf_op jit(solution)/shard_map/ppermute | solution.py:26
  19.0 9.7 %collective-permute-start.3 = (f32[64,1125]{1,0:T(8,128)S(1)}, f32[64,1125]{1,0:T(8,128)S(1)}, u32[]{:S(2)}, u32[]{:S(2)}) collective-permute-start(f32[64,1125]{1,0:T(8,128)S(1)} %bitcast.87), channel_id=1, source_target_pairs={{0,2},{1,15},{2,4},{3,1},{4,6},{5,3},{6,8},{7,5},{8,10},{9,7},{10,... | collective-permute-start | bytes 864008 | tf_op jit(solution)/shard_map/ppermute | solution.py:26
  23.7 18.3 %copy-start = (f32[1125,480]{0,1:T(8,128)S(1)}, f32[1125,480]{0,1:T(8,128)}, u32[]{:S(2)}) copy-start(f32[1125,480]{0,1:T(8,128)} %param.6) | copy-start | bytes 6480004
  26.8 8.7 %collective-permute-start.1 = (f32[64,1125]{1,0:T(8,128)S(1)}, f32[64,1125]{1,0:T(8,128)S(1)}, u32[]{:S(2)}, u32[]{:S(2)}) collective-permute-start(f32[64,1125]{1,0:T(8,128)S(1)} %collective-permute-done), channel_id=1, source_target_pairs={{0,14},{1,3},{2,0},{3,5},{4,2},{5,7},{6,4},{7,9},{8,6},{9,11},{10,... | collective-permute-start | bytes 864008 | tf_op jit(solution)/shard_map/ppermute | solution.py:26
  28.7 10.0 %collective-permute-start.4 = (f32[64,1125]{1,0:T(8,128)S(1)}, f32[64,1125]{1,0:T(8,128)S(1)}, u32[]{:S(2)}, u32[]{:S(2)}) collective-permute-start(f32[64,1125]{1,0:T(8,128)S(1)} %collective-permute-done.3), channel_id=1, source_target_pairs={{0,2},{1,15},{2,4},{3,1},{4,6},{5,3},{6,8},{7,5},{8,10},{9,7},{10,... | collective-permute-start | bytes 864008 | tf_op jit(solution)/shard_map/ppermute | solution.py:26
  35.4 18.5 %collective-permute-start.2 = (f32[64,1125]{1,0:T(8,128)S(1)}, f32[64,1125]{1,0:T(8,128)S(1)}, u32[]{:S(2)}, u32[]{:S(2)}) collective-permute-start(f32[64,1125]{1,0:T(8,128)S(1)} %collective-permute-done.1), channel_id=1, source_target_pairs={{0,14},{1,3},{2,0},{3,5},{4,2},{5,7},{6,4},{7,9},{8,6},{9,11},{10,... | collective-permute-start | bytes 864008 | tf_op jit(solution)/shard_map/ppermute | solution.py:26
  38.7 10.9 %collective-permute-start.5 = (f32[64,1125]{1,0:T(8,128)S(1)}, f32[64,1125]{1,0:T(8,128)S(1)}, u32[]{:S(2)}, u32[]{:S(2)}) collective-permute-start(f32[64,1125]{1,0:T(8,128)S(1)} %collective-permute-done.4), channel_id=1, source_target_pairs={{0,2},{1,15},{2,4},{3,1},{4,6},{5,3},{6,8},{7,5},{8,10},{9,7},{10,... | collective-permute-start | bytes 864008 | tf_op jit(solution)/shard_map/ppermute | solution.py:26
  49.7 7.8 %collective-permute-start.9 = (f32[64,1125]{1,0:T(8,128)S(1)}, f32[64,1125]{1,0:T(8,128)S(1)}, u32[]{:S(2)}, u32[]{:S(2)}) collective-permute-start(f32[64,1125]{1,0:T(8,128)S(1)} %collective-permute-done.5), channel_id=1, source_target_pairs={{0,2},{1,15},{2,4},{3,1},{4,6},{5,3},{6,8},{7,5},{8,10},{9,7},{10,... | collective-permute-start | bytes 864008 | tf_op jit(solution)/shard_map/ppermute | solution.py:26
  54.9 12.8 %collective-permute-start.7 = (f32[2,5,2,16,480]{4,3,2,1,0:T(8,128)}, f32[2,5,2,16,480]{4,3,2,1,0:T(8,128)}, u32[]{:S(2)}, u32[]{:S(2)}) collective-permute-start(f32[2,5,2,16,480]{4,3,2,1,0:T(8,128)} %pad_maximum_fusion.2), channel_id=1, source_target_pairs={{0,16},{1,49},{2,18},{3,51},{4,20},{5,53},{6,22},{7,55},{8,24},{9,... | collective-permute-start | bytes 1843208 | tf_op jit(solution)/shard_map/ppermute | solution.py:26
  60.8 13.0 %all-to-all-start = ((f32[4,3,2,16,480]{4,3,2,1,0:T(8,128)}), f32[4,3,2,16,480]{4,3,2,1,0:T(8,128)S(1)}, u32[]{:S(2)}, u32[]{:S(2)}) async-start(f32[4,3,2,16,480]{4,3,2,1,0:T(8,128)} %copy_bitcast_fusion), calls=%async_computation | async-start | bytes 1572864 | tf_op jit(solution)/shard_map/all_to_all | solution.py:114
  68.8 10.9 %collective-permute-start.8 = (f32[5,2,16,480]{3,2,1,0:T(8,128)S(1)}, f32[5,2,16,480]{3,2,1,0:T(8,128)S(1)}, u32[]{:S(2)}, u32[]{:S(2)}) collective-permute-start(f32[5,2,16,480]{3,2,1,0:T(8,128)S(1)} %fusion), channel_id=1, source_target_pairs={{0,48},{1,17},{2,50},{3,19},{4,52},{5,21},{6,54},{7,23},{8,56},{9,... | collective-permute-start | bytes 921608 | tf_op jit(solution)/shard_map/ppermute | solution.py:26
  80.8 31.1 %copy-start.1 = (f32[60]{0:T(128)S(1)}, f32[60]{0:T(128)}, u32[]{:S(2)}) copy-start(f32[60]{0:T(128)} %param.7) | copy-start | bytes 724
  80.8 31.1 %copy-start.2 = (f32[128]{0:T(128)S(1)}, f32[128]{0:T(128)}, u32[]{:S(2)}) copy-start(f32[128]{0:T(128)} %param.9) | copy-start | bytes 1540
  80.8 31.2 %copy-start.3 = (f32[16]{0:T(128)S(1)}, f32[16]{0:T(128)}, u32[]{:S(2)}) copy-start(f32[16]{0:T(128)} %param.8) | copy-start | bytes 196
  81.0 21.3 %collective-permute-start.13 = (f32[4,16,480]{2,1,0:T(8,128)S(1)}, f32[4,16,480]{2,1,0:T(8,128)S(1)}, u32[]{:S(2)}, u32[]{:S(2)}) collective-permute-start(f32[4,16,480]{2,1,0:T(8,128)S(1)} %get-tuple-element.16), channel_id=1, source_target_pairs={{0,896},{1,961},{2,898},{3,963},{4,900},{5,965},{6,902},{7,967},{8... | collective-permute-start | bytes 368648 | tf_op jit(solution)/shard_map/ppermute | solution.py:26
  92.7 9.5 %collective-permute-start.12 = (f32[4,16,480]{2,1,0:T(8,128)S(1)}, f32[4,16,480]{2,1,0:T(8,128)S(1)}, u32[]{:S(2)}, u32[]{:S(2)}) collective-permute-start(f32[4,16,480]{2,1,0:T(8,128)S(1)} %get-tuple-element.17), channel_id=1, source_target_pairs={{0,897},{1,960},{2,899},{3,962},{4,901},{5,964},{6,903},{7,966},{8... | collective-permute-start | bytes 368648 | tf_op jit(solution)/shard_map/ppermute | solution.py:26
  96.4 6.8 %collective-permute-start.10 = (f32[4,16,480]{2,1,0:T(8,128)S(1)}, f32[4,16,480]{2,1,0:T(8,128)S(1)}, u32[]{:S(2)}, u32[]{:S(2)}) collective-permute-start(f32[4,16,480]{2,1,0:T(8,128)S(1)} %get-tuple-element.18), channel_id=1, source_target_pairs={{0,1},{1,64},{2,3},{3,66},{4,5},{5,68},{6,7},{7,70},{8,9},{9,72},{... | collective-permute-start | bytes 368648 | tf_op jit(solution)/shard_map/ppermute | solution.py:26
  100.3 7.5 %collective-permute-start.11 = (f32[4,16,480]{2,1,0:T(8,128)S(1)}, f32[4,16,480]{2,1,0:T(8,128)S(1)}, u32[]{:S(2)}, u32[]{:S(2)}) collective-permute-start(f32[4,16,480]{2,1,0:T(8,128)S(1)} %get-tuple-element.15), channel_id=1, source_target_pairs={{0,0},{1,65},{2,2},{3,67},{4,4},{5,69},{6,6},{7,71},{8,8},{9,73},{... | collective-permute-start | bytes 368648 | tf_op jit(solution)/shard_map/ppermute | solution.py:26
  108.5 17.9 %all-to-all-start.1 = ((f32[4,16,480]{2,1,0:T(8,128)}), f32[4,16,480]{2,1,0:T(8,128)S(1)}, u32[]{:S(2)}, u32[]{:S(2)}) async-start(f32[4,16,480]{2,1,0:T(8,128)} %add_add_fusion), calls=%async_computation.1 | async-start | bytes 262144 | tf_op jit(solution)/shard_map/all_to_all | solution.py:130

commit v9 on v8

--- a/solution.py
+++ b/solution.py
@@ -97,17 +97,16 @@
     h3 = send(h2, along_y(-1))
     near_blocks = (block, f1, h1, f2, h2)
     own = product(near_blocks, integrals)
-    f3_after, own = lax.optimization_barrier((f3, own))
+    early = jnp.stack([own, product(near_blocks, others)], 1)
+    f3_after, early = lax.optimization_barrier((f3, early))
     f4 = send(f3_after, along_y(1))
-    early = jnp.stack([own, product(near_blocks, others)], 1)
-    h3_after, early = lax.optimization_barrier((h3, early))
 
     def place(k):
         return lax.dynamic_index_in_dim(early, (x + side * k) % X, 2, keepdims=False)
 
     arrived = send(jnp.stack([place(1), place(2)], 0), along_x(1))
     passed_on = place(3) + arrived[1]
-    far_blocks = (f3, h3_after, f4)
+    far_blocks = (f3, h3, f4)
     late = jnp.stack([product(far_blocks, integrals), product(far_blocks, others)], 1)
     late = late.transpose(2, 0, 1, 3, 4)
     first = place(0) + arrived[0] + send(passed_on, along_x(-1))

time: 128 us -> 128 us (level)
  the two profiles are of different devices: /device:TPU:1 before, /device:TPU:25 now
where the time goes in v9:
time: 128 us; the launch traced here: 127 us
  starting transfers between devices  81.1 us (63%)
  waiting for transfers between devices  32.5 us (25%)
  other arithmetic  5.63 us (4%)
  matrix products  5.41 us (4%)
  local copies, waits for them, and re-layouts  1.84 us (1%)
    ppermute x14, starting transfers between devices, send(): return lax.ppermute(array, AXES, table(move))  69.8 us
    ppermute x14, waiting for transfers between devices, send(): return lax.ppermute(array, AXES, table(move))  17.7 us
    all_to_all x1, starting transfers between devices, per_device(): lax.all_to_all(total, AXES, 0, 0, tiled=True, axis_index_groups=classes())  7.82 us
    all_to_all x1, waiting for transfers between devices, per_device(): lax.all_to_all(total, AXES, 0, 0, tiled=True, axis_index_groups=classes())  7.48 us
    all_to_all x1, waiting for transfers between devices, per_device(): lax.all_to_all(late, AXES, 0, 0, tiled=True, axis_index_groups=lines_x())  7.4 us
    dot_general x4, matrix products, product(): jnp.dot(tall, part, precision=lax.Precision.HIGH, preferred_element_type=...  5.41 us
    all_to_all x1, starting transfers between devices, per_device(): lax.all_to_all(late, AXES, 0, 0, tiled=True, axis_index_groups=lines_x())  3.49 us
  transfers between devices with their start and end apart: 16, of which 11 were waited for; matrix products, arithmetic and copies ran while one was open for 8% of the time, Pallas kernels for 0%

profile of v9, /device:TPU:25, one launch (start us, length us, event | category | flops | bytes accessed | tf_op | source)
XLA Modules:
  0.0 127.2 jit_solution(11350238011226802644)
XLA Ops:
  0.0 2.6 %collective-permute-start.5 = (f32[1125,480]{0,1:T(8,128)}, f32[1125,480]{0,1:T(8,128)S(1)}, u32[]{:S(2)}, u32[]{:S(2)}) collective-permute-start(f32[1125,480]{0,1:T(8,128)} %param.6), channel_id=1, source_target_pairs={{0,1},{1,0},{2,3},{3,2},{4,5},{5,4},{6,7},{7,6},{8,9},{9,8},{10,11... | collective-permute-start | bytes 6480008 | tf_op jit(solution)/shard_map/ppermute | solution.py:26
  2.6 1.0 reshape.49
  3.6 2.1 %collective-permute-start = (f32[64,1125]{1,0:T(8,128)S(1)}, f32[64,1125]{1,0:T(8,128)S(1)}, u32[]{:S(2)}, u32[]{:S(2)}) collective-permute-start(f32[64,1125]{1,0:T(8,128)S(1)} %bitcast.82), channel_id=1, source_target_pairs={{0,2},{1,15},{2,4},{3,1},{4,6},{5,3},{6,8},{7,5},{8,10},{9,7},{10,... | collective-permute-start | bytes 864008 | tf_op jit(solution)/shard_map/ppermute | solution.py:26
  5.7 4.4 %collective-permute-start.3 = (f32[64,1125]{1,0:T(8,128)S(1)}, f32[64,1125]{1,0:T(8,128)S(1)}, u32[]{:S(2)}, u32[]{:S(2)}) collective-permute-start(f32[64,1125]{1,0:T(8,128)S(1)} %bitcast.83), channel_id=1, source_target_pairs={{0,14},{1,3},{2,0},{3,5},{4,2},{5,7},{6,4},{7,9},{8,6},{9,11},{10,... | collective-permute-start | bytes 864008 | tf_op jit(solution)/shard_map/ppermute | solution.py:26
  10.2 0.0 copy-start
  10.3 2.0 %collective-permute-done = f32[64,1125]{1,0:T(8,128)S(1)} collective-permute-done((f32[64,1125]{1,0:T(8,128)S(1)}, f32[64,1125]{1,0:T(8,128)S(1)}, u32[]{:S(2)}, u32[]{:S(2)}) %collective-permute-start) | collective-permute-done | bytes 288032 | tf_op jit(solution)/shard_map/ppermute | solution.py:26
  12.3 1.9 %collective-permute-start.1 = (f32[64,1125]{1,0:T(8,128)S(1)}, f32[64,1125]{1,0:T(8,128)S(1)}, u32[]{:S(2)}, u32[]{:S(2)}) collective-permute-start(f32[64,1125]{1,0:T(8,128)S(1)} %collective-permute-done), channel_id=1, source_target_pairs={{0,2},{1,15},{2,4},{3,1},{4,6},{5,3},{6,8},{7,5},{8,10},{9,7},{10,... | collective-permute-start | bytes 864008 | tf_op jit(solution)/shard_map/ppermute | solution.py:26
  14.2 1.1 collective-permute-done.3
  15.3 5.0 %collective-permute-start.4 = (f32[64,1125]{1,0:T(8,128)S(1)}, f32[64,1125]{1,0:T(8,128)S(1)}, u32[]{:S(2)}, u32[]{:S(2)}) collective-permute-start(f32[64,1125]{1,0:T(8,128)S(1)} %collective-permute-done.3), channel_id=1, source_target_pairs={{0,14},{1,3},{2,0},{3,5},{4,2},{5,7},{6,4},{7,9},{8,6},{9,11},{10,... | collective-permute-start | bytes 864008 | tf_op jit(solution)/shard_map/ppermute | solution.py:26
  20.4 0.6 collective-permute-done.1
  21.0 9.5 %collective-permute-start.2 = (f32[64,1125]{1,0:T(8,128)S(1)}, f32[64,1125]{1,0:T(8,128)S(1)}, u32[]{:S(2)}, u32[]{:S(2)}) collective-permute-start(f32[64,1125]{1,0:T(8,128)S(1)} %collective-permute-done.1), channel_id=1, source_target_pairs={{0,2},{1,15},{2,4},{3,1},{4,6},{5,3},{6,8},{7,5},{8,10},{9,7},{10,... | collective-permute-start | bytes 864008 | tf_op jit(solution)/shard_map/ppermute | solution.py:26
  30.5 0.8 collective-permute-done.4
  31.3 1.9 %collective-permute-start.8 = (f32[64,1125]{1,0:T(8,128)S(1)}, f32[64,1125]{1,0:T(8,128)S(1)}, u32[]{:S(2)}, u32[]{:S(2)}) collective-permute-start(f32[64,1125]{1,0:T(8,128)S(1)} %collective-permute-done.4), channel_id=1, source_target_pairs={{0,14},{1,3},{2,0},{3,5},{4,2},{5,7},{6,4},{7,9},{8,6},{9,11},{10,... | collective-permute-start | bytes 864008 | tf_op jit(solution)/shard_map/ppermute | solution.py:26
  33.3 0.0 copy-done
  33.3 1.6 %fusion.14 = f32[320,480]{1,0:T(8,128)S(1)} fusion(f32[320,1125]{1,0:T(8,128)S(1)} %constant_dynamic-update-slice_fusion, f32[1125,480]{0,1:T(8,128)S(1)} %copy-done), kind=kOutput, calls=%fused_computation.51 | convolution fusion | flops 1036800000 | bytes 4214400 | tf_op jit(solution)/shard_map/dot_general | solution.py:93
  34.8 0.0 collective-permute-done.2
  34.9 0.0 collective-permute-done.5
  34.9 1.5 %fusion.15 = f32[320,480]{1,0:T(8,128)S(1)} fusion(f32[320,1125]{1,0:T(8,128)S(1)} %constant_dynamic-update-slice_fusion, f32[1125,480]{0,1:T(8,128)S(1)} %collective-permute-done.5), kind=kOutput, calls=%fused_computation.52 | convolution fusion | flops 1036800000 | bytes 4214400 | tf_op jit(solution)/shard_map/dot_general | solution.py:93
  36.4 0.1 pad_maximum_fusion
  36.5 0.1 copy.16
  36.6 3.8 %collective-permute-start.9 = (f32[64,1125]{1,0:T(8,128)S(1)}, f32[64,1125]{1,0:T(8,128)S(1)}, u32[]{:S(2)}, u32[]{:S(2)}) collective-permute-start(f32[64,1125]{1,0:T(8,128)S(1)} %collective-permute-done.2), channel_id=1, source_target_pairs={{0,2},{1,15},{2,4},{3,1},{4,6},{5,3},{6,8},{7,5},{8,10},{9,7},{10,... | collective-permute-start | bytes 864008 | tf_op jit(solution)/shard_map/ppermute | solution.py:26
  40.4 0.0 collective-permute-done.8
  40.5 0.1 dynamic-slice_bitcast_fusion.1
  40.5 0.9 pad_maximum_fusion.2
  41.4 1.9 %collective-permute-start.6 = (f32[2,5,2,16,480]{4,3,2,1,0:T(8,128)}, f32[2,5,2,16,480]{4,3,2,1,0:T(8,128)}, u32[]{:S(2)}, u32[]{:S(2)}) collective-permute-start(f32[2,5,2,16,480]{4,3,2,1,0:T(8,128)} %pad_maximum_fusion.2), channel_id=1, source_target_pairs={{0,16},{1,49},{2,18},{3,51},{4,20},{5,53},{6,22},{7,55},{8,24},{9,... | collective-permute-start | bytes 1843208 | tf_op jit(solution)/shard_map/ppermute | solution.py:26
  43.3 2.0 %collective-permute-done.9 = f32[64,1125]{1,0:T(8,128)S(1)} collective-permute-done((f32[64,1125]{1,0:T(8,128)S(1)}, f32[64,1125]{1,0:T(8,128)S(1)}, u32[]{:S(2)}, u32[]{:S(2)}) %collective-permute-start.9) | collective-permute-done | bytes 288032 | tf_op jit(solution)/shard_map/ppermute | solution.py:26
  45.3 1.2 fusion.16
  46.6 1.2 fusion.17
  47.7 1.0 copy_bitcast_fusion
  48.7 3.5 %all-to-all-start = ((f32[4,3,2,16,480]{4,3,2,1,0:T(8,128)}), f32[4,3,2,16,480]{4,3,2,1,0:T(8,128)S(1)}, u32[]{:S(2)}, u32[]{:S(2)}) async-start(f32[4,3,2,16,480]{4,3,2,1,0:T(8,128)} %copy_bitcast_fusion), calls=%async_computation | async-start | bytes 1572864 | tf_op jit(solution)/shard_map/all_to_all | solution.py:113
  52.2 2.1 %collective-permute-done.6 = f32[2,5,2,16,480]{4,3,2,1,0:T(8,128)} collective-permute-done((f32[2,5,2,16,480]{4,3,2,1,0:T(8,128)}, f32[2,5,2,16,480]{4,3,2,1,0:T(8,128)}, u32[]{:S(2)}, u32[]{:S(2)}) %collective-permute-start.6) | collective-permute-done | bytes 614432 | tf_op jit(solution)/shard_map/ppermute | solution.py:26
  54.3 1.0 fusion
  55.3 1.9 %collective-permute-start.7 = (f32[5,2,16,480]{3,2,1,0:T(8,128)S(1)}, f32[5,2,16,480]{3,2,1,0:T(8,128)S(1)}, u32[]{:S(2)}, u32[]{:S(2)}) collective-permute-start(f32[5,2,16,480]{3,2,1,0:T(8,128)S(1)} %fusion), channel_id=1, source_target_pairs={{0,48},{1,17},{2,50},{3,19},{4,52},{5,21},{6,54},{7,23},{8,56},{9,... | collective-permute-start | bytes 921608 | tf_op jit(solution)/shard_map/ppermute | solution.py:26
  57.4 7.4 %all-to-all-done = f32[4,3,2,16,480]{4,3,2,1,0:T(8,128)S(1)} async-done(((f32[4,3,2,16,480]{4,3,2,1,0:T(8,128)}), f32[4,3,2,16,480]{4,3,2,1,0:T(8,128)S(1)}, u32[]{:S(2)}, u32[]{:S(2)}) %all-to-all-start) | async-done | bytes 737312 | tf_op jit(solution)/shard_map/all_to_all | solution.py:113
  64.8 0.1 slice_add_fusion
  64.8 3.5 %collective-permute-done.7 = f32[5,2,16,480]{3,2,1,0:T(8,128)S(1)} collective-permute-done((f32[5,2,16,480]{3,2,1,0:T(8,128)S(1)}, f32[5,2,16,480]{3,2,1,0:T(8,128)S(1)}, u32[]{:S(2)}, u32[]{:S(2)}) %collective-permute-start.7) | collective-permute-done | bytes 307232 | tf_op jit(solution)/shard_map/ppermute | solution.py:26
  68.4 1.0 fusion.2
  69.4 0.0 copy-start.1
  69.4 0.0 copy-start.2
  69.5 0.0 copy-start.3
  69.6 0.1 dynamic-slice_bitcast_fusion.4
  69.6 19.5 %collective-permute-start.13 = (f32[4,16,480]{2,1,0:T(8,128)S(1)}, f32[4,16,480]{2,1,0:T(8,128)S(1)}, u32[]{:S(2)}, u32[]{:S(2)}) collective-permute-start(f32[4,16,480]{2,1,0:T(8,128)S(1)} %get-tuple-element.12), channel_id=1, source_target_pairs={{0,896},{1,961},{2,898},{3,963},{4,900},{5,965},{6,902},{7,967},{8... | collective-permute-start | bytes 368648 | tf_op jit(solution)/shard_map/ppermute | solution.py:26
  89.2 9.4 %collective-permute-start.12 = (f32[4,16,480]{2,1,0:T(8,128)S(1)}, f32[4,16,480]{2,1,0:T(8,128)S(1)}, u32[]{:S(2)}, u32[]{:S(2)}) collective-permute-start(f32[4,16,480]{2,1,0:T(8,128)S(1)} %get-tuple-element.13), channel_id=1, source_target_pairs={{0,897},{1,960},{2,899},{3,962},{4,901},{5,964},{6,903},{7,966},{8... | collective-permute-start | bytes 368648 | tf_op jit(solution)/shard_map/ppermute | solution.py:26
  98.6 3.9 %collective-permute-start.10 = (f32[4,16,480]{2,1,0:T(8,128)S(1)}, f32[4,16,480]{2,1,0:T(8,128)S(1)}, u32[]{:S(2)}, u32[]{:S(2)}) collective-permute-start(f32[4,16,480]{2,1,0:T(8,128)S(1)} %get-tuple-element.14), channel_id=1, source_target_pairs={{0,1},{1,64},{2,3},{3,66},{4,5},{5,68},{6,7},{7,70},{8,9},{9,72},{... | collective-permute-start | bytes 368648 | tf_op jit(solution)/shard_map/ppermute | solution.py:26
  102.5 1.9 %collective-permute-start.11 = (f32[4,16,480]{2,1,0:T(8,128)S(1)}, f32[4,16,480]{2,1,0:T(8,128)S(1)}, u32[]{:S(2)}, u32[]{:S(2)}) collective-permute-start(f32[4,16,480]{2,1,0:T(8,128)S(1)} %get-tuple-element.11), channel_id=1, source_target_pairs={{0,0},{1,65},{2,2},{3,67},{4,4},{5,69},{6,6},{7,71},{8,8},{9,73},{... | collective-permute-start | bytes 368648 | tf_op jit(solution)/shard_map/ppermute | solution.py:26
  104.4 0.0 collective-permute-done.13
  104.4 0.0 collective-permute-done.12
  104.4 0.7 collective-permute-done.10
  105.2 4.8 %collective-permute-done.11 = f32[4,16,480]{2,1,0:T(8,128)S(1)} collective-permute-done((f32[4,16,480]{2,1,0:T(8,128)S(1)}, f32[4,16,480]{2,1,0:T(8,128)S(1)}, u32[]{:S(2)}, u32[]{:S(2)}) %collective-permute-start.11) | collective-permute-done | bytes 122912 | tf_op jit(solution)/shard_map/ppermute | solution.py:26
  110.0 0.7 add_add_fusion
  110.7 7.8 %all-to-all-start.1 = ((f32[4,16,480]{2,1,0:T(8,128)}), f32[4,16,480]{2,1,0:T(8,128)S(1)}, u32[]{:S(2)}, u32[]{:S(2)}) async-start(f32[4,16,480]{2,1,0:T(8,128)} %add_add_fusion), calls=%async_computation.1 | async-start | bytes 262144 | tf_op jit(solution)/shard_map/all_to_all | solution.py:129
  118.5 0.0 copy-done.1
  118.5 0.0 copy-done.2
  118.5 0.1 broadcast_subtract_fusion
  118.6 0.1 sub.54
  118.7 0.0 copy-done.3
  118.7 0.1 broadcast_subtract_fusion.1
  118.8 0.1 sub.50
  118.9 0.1 dynamic_slice.40
  118.9 0.1 dynamic_slice.39
  119.0 7.5 %all-to-all-done.1 = f32[4,16,480]{2,1,0:T(8,128)S(1)} async-done(((f32[4,16,480]{2,1,0:T(8,128)}), f32[4,16,480]{2,1,0:T(8,128)S(1)}, u32[]{:S(2)}, u32[]{:S(2)}) %all-to-all-start.1) | async-done | bytes 122912 | tf_op jit(solution)/shard_map/all_to_all | solution.py:129
  126.5 0.7 fusion.12
  (18 shorter events, 0.3 us)
Async XLA Ops:
  0.0 34.9 %collective-permute-start.5 = (f32[1125,480]{0,1:T(8,128)}, f32[1125,480]{0,1:T(8,128)S(1)}, u32[]{:S(2)}, u32[]{:S(2)}) collective-permute-start(f32[1125,480]{0,1:T(8,128)} %param.6), channel_id=1, source_target_pairs={{0,1},{1,0},{2,3},{3,2},{4,5},{5,4},{6,7},{7,6},{8,9},{9,8},{10,11... | collective-permute-start | bytes 6480008 | tf_op jit(solution)/shard_map/ppermute | solution.py:26
  3.6 8.7 %collective-permute-start = (f32[64,1125]{1,0:T(8,128)S(1)}, f32[64,1125]{1,0:T(8,128)S(1)}, u32[]{:S(2)}, u32[]{:S(2)}) collective-permute-start(f32[64,1125]{1,0:T(8,128)S(1)} %bitcast.82), channel_id=1, source_target_pairs={{0,2},{1,15},{2,4},{3,1},{4,6},{5,3},{6,8},{7,5},{8,10},{9,7},{10,... | collective-permute-start | bytes 864008 | tf_op jit(solution)/shard_map/ppermute | solution.py:26
  5.7 9.6 %collective-permute-start.3 = (f32[64,1125]{1,0:T(8,128)S(1)}, f32[64,1125]{1,0:T(8,128)S(1)}, u32[]{:S(2)}, u32[]{:S(2)}) collective-permute-start(f32[64,1125]{1,0:T(8,128)S(1)} %bitcast.83), channel_id=1, source_target_pairs={{0,14},{1,3},{2,0},{3,5},{4,2},{5,7},{6,4},{7,9},{8,6},{9,11},{10,... | collective-permute-start | bytes 864008 | tf_op jit(solution)/shard_map/ppermute | solution.py:26
  10.2 23.1 %copy-start = (f32[1125,480]{0,1:T(8,128)S(1)}, f32[1125,480]{0,1:T(8,128)}, u32[]{:S(2)}) copy-start(f32[1125,480]{0,1:T(8,128)} %param.6) | copy-start | bytes 6480004
  12.3 8.7 %collective-permute-start.1 = (f32[64,1125]{1,0:T(8,128)S(1)}, f32[64,1125]{1,0:T(8,128)S(1)}, u32[]{:S(2)}, u32[]{:S(2)}) collective-permute-start(f32[64,1125]{1,0:T(8,128)S(1)} %collective-permute-done), channel_id=1, source_target_pairs={{0,2},{1,15},{2,4},{3,1},{4,6},{5,3},{6,8},{7,5},{8,10},{9,7},{10,... | collective-permute-start | bytes 864008 | tf_op jit(solution)/shard_map/ppermute | solution.py:26
  15.3 16.0 %collective-permute-start.4 = (f32[64,1125]{1,0:T(8,128)S(1)}, f32[64,1125]{1,0:T(8,128)S(1)}, u32[]{:S(2)}, u32[]{:S(2)}) collective-permute-start(f32[64,1125]{1,0:T(8,128)S(1)} %collective-permute-done.3), channel_id=1, source_target_pairs={{0,14},{1,3},{2,0},{3,5},{4,2},{5,7},{6,4},{7,9},{8,6},{9,11},{10,... | collective-permute-start | bytes 864008 | tf_op jit(solution)/shard_map/ppermute | solution.py:26
  21.0 13.9 %collective-permute-start.2 = (f32[64,1125]{1,0:T(8,128)S(1)}, f32[64,1125]{1,0:T(8,128)S(1)}, u32[]{:S(2)}, u32[]{:S(2)}) collective-permute-start(f32[64,1125]{1,0:T(8,128)S(1)} %collective-permute-done.1), channel_id=1, source_target_pairs={{0,2},{1,15},{2,4},{3,1},{4,6},{5,3},{6,8},{7,5},{8,10},{9,7},{10,... | collective-permute-start | bytes 864008 | tf_op jit(solution)/shard_map/ppermute | solution.py:26
  31.3 9.1 %collective-permute-start.8 = (f32[64,1125]{1,0:T(8,128)S(1)}, f32[64,1125]{1,0:T(8,128)S(1)}, u32[]{:S(2)}, u32[]{:S(2)}) collective-permute-start(f32[64,1125]{1,0:T(8,128)S(1)} %collective-permute-done.4), channel_id=1, source_target_pairs={{0,14},{1,3},{2,0},{3,5},{4,2},{5,7},{6,4},{7,9},{8,6},{9,11},{10,... | collective-permute-start | bytes 864008 | tf_op jit(solution)/shard_map/ppermute | solution.py:26
  36.6 8.7 %collective-permute-start.9 = (f32[64,1125]{1,0:T(8,128)S(1)}, f32[64,1125]{1,0:T(8,128)S(1)}, u32[]{:S(2)}, u32[]{:S(2)}) collective-permute-start(f32[64,1125]{1,0:T(8,128)S(1)} %collective-permute-done.2), channel_id=1, source_target_pairs={{0,2},{1,15},{2,4},{3,1},{4,6},{5,3},{6,8},{7,5},{8,10},{9,7},{10,... | collective-permute-start | bytes 864008 | tf_op jit(solution)/shard_map/ppermute | solution.py:26
  41.4 12.8 %collective-permute-start.6 = (f32[2,5,2,16,480]{4,3,2,1,0:T(8,128)}, f32[2,5,2,16,480]{4,3,2,1,0:T(8,128)}, u32[]{:S(2)}, u32[]{:S(2)}) collective-permute-start(f32[2,5,2,16,480]{4,3,2,1,0:T(8,128)} %pad_maximum_fusion.2), channel_id=1, source_target_pairs={{0,16},{1,49},{2,18},{3,51},{4,20},{5,53},{6,22},{7,55},{8,24},{9,... | collective-permute-start | bytes 1843208 | tf_op jit(solution)/shard_map/ppermute | solution.py:26
  48.7 16.1 %all-to-all-start = ((f32[4,3,2,16,480]{4,3,2,1,0:T(8,128)}), f32[4,3,2,16,480]{4,3,2,1,0:T(8,128)S(1)}, u32[]{:S(2)}, u32[]{:S(2)}) async-start(f32[4,3,2,16,480]{4,3,2,1,0:T(8,128)} %copy_bitcast_fusion), calls=%async_computation | async-start | bytes 1572864 | tf_op jit(solution)/shard_map/all_to_all | solution.py:113
  55.3 13.1 %collective-permute-start.7 = (f32[5,2,16,480]{3,2,1,0:T(8,128)S(1)}, f32[5,2,16,480]{3,2,1,0:T(8,128)S(1)}, u32[]{:S(2)}, u32[]{:S(2)}) collective-permute-start(f32[5,2,16,480]{3,2,1,0:T(8,128)S(1)} %fusion), channel_id=1, source_target_pairs={{0,48},{1,17},{2,50},{3,19},{4,52},{5,21},{6,54},{7,23},{8,56},{9,... | collective-permute-start | bytes 921608 | tf_op jit(solution)/shard_map/ppermute | solution.py:26
  69.4 49.1 %copy-start.1 = (f32[60]{0:T(128)S(1)}, f32[60]{0:T(128)}, u32[]{:S(2)}) copy-start(f32[60]{0:T(128)} %param.7) | copy-start | bytes 724
  69.4 49.0 %copy-start.2 = (f32[128]{0:T(128)S(1)}, f32[128]{0:T(128)}, u32[]{:S(2)}) copy-start(f32[128]{0:T(128)} %param.9) | copy-start | bytes 1540
  69.5 49.2 %copy-start.3 = (f32[16]{0:T(128)S(1)}, f32[16]{0:T(128)}, u32[]{:S(2)}) copy-start(f32[16]{0:T(128)} %param.8) | copy-start | bytes 196
  69.6 34.8 %collective-permute-start.13 = (f32[4,16,480]{2,1,0:T(8,128)S(1)}, f32[4,16,480]{2,1,0:T(8,128)S(1)}, u32[]{:S(2)}, u32[]{:S(2)}) collective-permute-start(f32[4,16,480]{2,1,0:T(8,128)S(1)} %get-tuple-element.12), channel_id=1, source_target_pairs={{0,896},{1,961},{2,898},{3,963},{4,900},{5,965},{6,902},{7,967},{8... | collective-permute-start | bytes 368648 | tf_op jit(solution)/shard_map/ppermute | solution.py:26
  89.2 15.3 %collective-permute-start.12 = (f32[4,16,480]{2,1,0:T(8,128)S(1)}, f32[4,16,480]{2,1,0:T(8,128)S(1)}, u32[]{:S(2)}, u32[]{:S(2)}) collective-permute-start(f32[4,16,480]{2,1,0:T(8,128)S(1)} %get-tuple-element.13), channel_id=1, source_target_pairs={{0,897},{1,960},{2,899},{3,962},{4,901},{5,964},{6,903},{7,966},{8... | collective-permute-start | bytes 368648 | tf_op jit(solution)/shard_map/ppermute | solution.py:26
  98.6 6.6 %collective-permute-start.10 = (f32[4,16,480]{2,1,0:T(8,128)S(1)}, f32[4,16,480]{2,1,0:T(8,128)S(1)}, u32[]{:S(2)}, u32[]{:S(2)}) collective-permute-start(f32[4,16,480]{2,1,0:T(8,128)S(1)} %get-tuple-element.14), channel_id=1, source_target_pairs={{0,1},{1,64},{2,3},{3,66},{4,5},{5,68},{6,7},{7,70},{8,9},{9,72},{... | collective-permute-start | bytes 368648 | tf_op jit(solution)/shard_map/ppermute | solution.py:26
  102.5 7.5 %collective-permute-start.11 = (f32[4,16,480]{2,1,0:T(8,128)S(1)}, f32[4,16,480]{2,1,0:T(8,128)S(1)}, u32[]{:S(2)}, u32[]{:S(2)}) collective-permute-start(f32[4,16,480]{2,1,0:T(8,128)S(1)} %get-tuple-element.11), channel_id=1, source_target_pairs={{0,0},{1,65},{2,2},{3,67},{4,4},{5,69},{6,6},{7,71},{8,8},{9,73},{... | collective-permute-start | bytes 368648 | tf_op jit(solution)/shard_map/ppermute | solution.py:26
  110.7 15.8 %all-to-all-start.1 = ((f32[4,16,480]{2,1,0:T(8,128)}), f32[4,16,480]{2,1,0:T(8,128)S(1)}, u32[]{:S(2)}, u32[]{:S(2)}) async-start(f32[4,16,480]{2,1,0:T(8,128)} %add_add_fusion), calls=%async_computation.1 | async-start | bytes 262144 | tf_op jit(solution)/shard_map/all_to_all | solution.py:129

commit v10 on v7

--- a/solution.py
+++ b/solution.py
@@ -103,13 +103,12 @@
     passed_on = early[:, :, 3] + arrived[:, :, 1]
     far_blocks = (f3, h3_after, f4)
     late = jnp.stack([product(far_blocks, integrals), product(far_blocks, others)], 1)
-    late_first = send(late[:, :, 1], along_x(1))
-    late_last, late_far = late[:, :, 3], late[:, :, 2]
-    first = early[:, :, 0] + arrived[:, :, 0] + send(passed_on, along_x(-1))
-    second, first = lax.optimization_barrier((late[:, :, 0] + late_first, first))
-    second = second + send(late_last, along_x(-1)) + send(late_far, along_x(2))
+    late_arrived = send(late[:, :, 1:3], along_x(1))
+    late_passed_on = late[:, :, 3] + late_arrived[:, :, 1]
+    summed = send(jnp.concatenate([passed_on, late_passed_on], 0), along_x(-1))
+    summed = summed + jnp.concatenate([early[:, :, 0] + arrived[:, :, 0], late[:, :, 0] + late_arrived[:, :, 0]], 0)
     pieces = jnp.stack(
-        [first[0], first[3], second[2], first[4], first[1], first[2], second[0], second[1]], 1
+        [summed[k] for k in (0, 3, 7, 4, 1, 2, 5, 6)], 1
     )
     pieces = pieces.reshape(2, 2, 4, 16, cols)
 

time: 130 us -> 129 us (level)
  the two profiles are of different devices: /device:TPU:30 before, /device:TPU:25 now
where the time goes in v10:
time: 129 us; the launch traced here: 127 us
  starting transfers between devices  79.1 us (61%)
  waiting for transfers between devices  36.2 us (28%)
  matrix products  5.41 us (4%)
  other arithmetic  3 us (2%)
  local copies, waits for them, and re-layouts  2.63 us (2%)
    ppermute x15, starting transfers between devices, send(): return lax.ppermute(array, AXES, table(move))  68.4 us
    ppermute x15, waiting for transfers between devices, send(): return lax.ppermute(array, AXES, table(move))  28.4 us
    all_to_all x1, starting transfers between devices, per_device(): lax.all_to_all(total, AXES, 0, 0, tiled=True, axis_index_groups=classes())  10.7 us
    all_to_all x1, waiting for transfers between devices, per_device(): lax.all_to_all(total, AXES, 0, 0, tiled=True, axis_index_groups=classes())  7.71 us
    dot_general x4, matrix products, product(): jnp.dot(tall, part, precision=lax.Precision.HIGH, preferred_element_type=...  5.41 us
  transfers between devices with their start and end apart: 16, of which 10 were waited for; matrix products, arithmetic and copies ran while one was open for 7% of the time, Pallas kernels for 0%

profile of v10, /device:TPU:25, one launch (start us, length us, event | category | flops | bytes accessed | tf_op | source)
XLA Modules:
  0.0 127.1 jit_solution(8919376127302629899)
XLA Ops:
  0.0 2.6 %collective-permute-start.6 = (f32[1125,480]{0,1:T(8,128)}, f32[1125,480]{0,1:T(8,128)S(1)}, u32[]{:S(2)}, u32[]{:S(2)}) collective-permute-start(f32[1125,480]{0,1:T(8,128)} %param.6), channel_id=1, source_target_pairs={{0,1},{1,0},{2,3},{3,2},{4,5},{5,4},{6,7},{7,6},{8,9},{9,8},{10,11... | collective-permute-start | bytes 6480008 | tf_op jit(solution)/shard_map/ppermute | solution.py:26
  2.7 1.0 reshape.42
  3.8 0.0 copy-start
  3.9 2.2 %collective-permute-start.3 = (f32[64,1125]{1,0:T(8,128)S(1)}, f32[64,1125]{1,0:T(8,128)S(1)}, u32[]{:S(2)}, u32[]{:S(2)}) collective-permute-start(f32[64,1125]{1,0:T(8,128)S(1)} %pad_maximum_fusion.2), channel_id=1, source_target_pairs={{0,2},{1,15},{2,4},{3,1},{4,6},{5,3},{6,8},{7,5},{8,10},{9,7},{10,... | collective-permute-start | bytes 864008 | tf_op jit(solution)/shard_map/ppermute | solution.py:26
  6.1 4.4 %collective-permute-start = (f32[64,1125]{1,0:T(8,128)S(1)}, f32[64,1125]{1,0:T(8,128)S(1)}, u32[]{:S(2)}, u32[]{:S(2)}) collective-permute-start(f32[64,1125]{1,0:T(8,128)S(1)} %pad_maximum_fusion.2), channel_id=1, source_target_pairs={{0,14},{1,3},{2,0},{3,5},{4,2},{5,7},{6,4},{7,9},{8,6},{9,11},{10,... | collective-permute-start | bytes 864008 | tf_op jit(solution)/shard_map/ppermute | solution.py:26
  10.5 2.2 %collective-permute-done.3 = f32[64,1125]{1,0:T(8,128)S(1)} collective-permute-done((f32[64,1125]{1,0:T(8,128)S(1)}, f32[64,1125]{1,0:T(8,128)S(1)}, u32[]{:S(2)}, u32[]{:S(2)}) %collective-permute-start.3) | collective-permute-done | bytes 288032 | tf_op jit(solution)/shard_map/ppermute | solution.py:26
  12.7 1.9 %collective-permute-start.4 = (f32[64,1125]{1,0:T(8,128)S(1)}, f32[64,1125]{1,0:T(8,128)S(1)}, u32[]{:S(2)}, u32[]{:S(2)}) collective-permute-start(f32[64,1125]{1,0:T(8,128)S(1)} %collective-permute-done.3), channel_id=1, source_target_pairs={{0,2},{1,15},{2,4},{3,1},{4,6},{5,3},{6,8},{7,5},{8,10},{9,7},{10,... | collective-permute-start | bytes 864008 | tf_op jit(solution)/shard_map/ppermute | solution.py:26
  14.6 1.1 collective-permute-done
  15.7 5.0 %collective-permute-start.1 = (f32[64,1125]{1,0:T(8,128)S(1)}, f32[64,1125]{1,0:T(8,128)S(1)}, u32[]{:S(2)}, u32[]{:S(2)}) collective-permute-start(f32[64,1125]{1,0:T(8,128)S(1)} %collective-permute-done), channel_id=1, source_target_pairs={{0,14},{1,3},{2,0},{3,5},{4,2},{5,7},{6,4},{7,9},{8,6},{9,11},{10,... | collective-permute-start | bytes 864008 | tf_op jit(solution)/shard_map/ppermute | solution.py:26
  20.8 0.6 collective-permute-done.4
  21.4 9.5 %collective-permute-start.5 = (f32[64,1125]{1,0:T(8,128)S(1)}, f32[64,1125]{1,0:T(8,128)S(1)}, u32[]{:S(2)}, u32[]{:S(2)}) collective-permute-start(f32[64,1125]{1,0:T(8,128)S(1)} %collective-permute-done.4), channel_id=1, source_target_pairs={{0,2},{1,15},{2,4},{3,1},{4,6},{5,3},{6,8},{7,5},{8,10},{9,7},{10,... | collective-permute-start | bytes 864008 | tf_op jit(solution)/shard_map/ppermute | solution.py:26
  30.9 0.8 collective-permute-done.1
  31.7 1.9 %collective-permute-start.2 = (f32[64,1125]{1,0:T(8,128)S(1)}, f32[64,1125]{1,0:T(8,128)S(1)}, u32[]{:S(2)}, u32[]{:S(2)}) collective-permute-start(f32[64,1125]{1,0:T(8,128)S(1)} %collective-permute-done.1), channel_id=1, source_target_pairs={{0,14},{1,3},{2,0},{3,5},{4,2},{5,7},{6,4},{7,9},{8,6},{9,11},{10,... | collective-permute-start | bytes 864008 | tf_op jit(solution)/shard_map/ppermute | solution.py:26
  33.7 0.0 copy-done
  33.7 1.6 %fusion.26 = f32[320,480]{1,0:T(8,128)S(1)} fusion(f32[320,1125]{1,0:T(8,128)S(1)} %constant_dynamic-update-slice_fusion, f32[1125,480]{0,1:T(8,128)S(1)} %copy-done), kind=kOutput, calls=%fused_computation.67 | convolution fusion | flops 1036800000 | bytes 4214400 | tf_op jit(solution)/shard_map/dot_general | solution.py:91
  35.2 0.0 collective-permute-done.5
  35.2 3.8 %collective-permute-start.8 = (f32[64,1125]{1,0:T(8,128)S(1)}, f32[64,1125]{1,0:T(8,128)S(1)}, u32[]{:S(2)}, u32[]{:S(2)}) collective-permute-start(f32[64,1125]{1,0:T(8,128)S(1)} %collective-permute-done.5), channel_id=1, source_target_pairs={{0,2},{1,15},{2,4},{3,1},{4,6},{5,3},{6,8},{7,5},{8,10},{9,7},{10,... | collective-permute-start | bytes 864008 | tf_op jit(solution)/shard_map/ppermute | solution.py:26
  39.1 0.0 collective-permute-done.6
  39.1 1.5 %fusion.27 = f32[320,480]{1,0:T(8,128)S(1)} fusion(f32[320,1125]{1,0:T(8,128)S(1)} %constant_dynamic-update-slice_fusion, f32[1125,480]{0,1:T(8,128)S(1)} %collective-permute-done.6), kind=kOutput, calls=%fused_computation.68 | convolution fusion | flops 1036800000 | bytes 4214400 | tf_op jit(solution)/shard_map/dot_general | solution.py:91
  40.6 0.1 pad_maximum_fusion
  40.7 0.0 collective-permute-done.2
  40.7 0.1 copy.22
  40.9 1.9 %collective-permute-start.7 = (f32[5,2,2,16,480]{4,3,0,1,2:T(8,128)S(1)}, f32[5,2,2,16,480]{4,3,0,1,2:T(8,128)S(1)}, u32[]{:S(2)}, u32[]{:S(2)}) collective-permute-start(f32[5,2,2,16,480]{4,3,0,1,2:T(8,128)S(1)} %slice.97), channel_id=1, source_target_pairs={{0,16},{1,49},{2,18},{3,51},{4,20},{5,53},{6,22},{7,55},{8,24},{9,... | collective-permute-start | bytes 1843208 | tf_op jit(solution)/shard_map/ppermute | solution.py:26
  42.9 2.0 %collective-permute-done.8 = f32[64,1125]{1,0:T(8,128)S(1)} collective-permute-done((f32[64,1125]{1,0:T(8,128)S(1)}, f32[64,1125]{1,0:T(8,128)S(1)}, u32[]{:S(2)}, u32[]{:S(2)}) %collective-permute-start.8) | collective-permute-done | bytes 288032 | tf_op jit(solution)/shard_map/ppermute | solution.py:26
  44.9 1.2 fusion.28
  46.1 1.2 fusion.29
  47.3 4.4 %collective-permute-start.9 = (f32[3,2,2,16,480]{4,3,0,1,2:T(8,128)S(1)}, f32[3,2,2,16,480]{4,3,0,1,2:T(8,128)S(1)}, u32[]{:S(2)}, u32[]{:S(2)}) collective-permute-start(f32[3,2,2,16,480]{4,3,0,1,2:T(8,128)S(1)} %copy.40), channel_id=1, source_target_pairs={{0,16},{1,49},{2,18},{3,51},{4,20},{5,53},{6,22},{7,55},{8,24},{9,... | collective-permute-start | bytes 1105928 | tf_op jit(solution)/shard_map/ppermute | solution.py:26
  51.7 5.9 %collective-permute-done.9 = f32[3,2,2,16,480]{4,3,0,1,2:T(8,128)S(1)} collective-permute-done((f32[3,2,2,16,480]{4,3,0,1,2:T(8,128)S(1)}, f32[3,2,2,16,480]{4,3,0,1,2:T(8,128)S(1)}, u32[]{:S(2)}, u32[]{:S(2)}) %collective-permute-start.9) | collective-permute-done | bytes 368672 | tf_op jit(solution)/shard_map/ppermute | solution.py:26
  57.6 0.1 fusion.4
  57.7 0.0 collective-permute-done.7
  57.7 0.0 copy-start.1
  57.8 0.7 copy-done.1
  58.6 1.9 %collective-permute-start.10 = (f32[8,2,16,480]{3,2,0,1:T(8,128)S(1)}, f32[8,2,16,480]{3,2,0,1:T(8,128)S(1)}, u32[]{:S(2)}, u32[]{:S(2)}) collective-permute-start(f32[8,2,16,480]{3,2,0,1:T(8,128)S(1)} %pad_maximum_fusion.1), channel_id=1, source_target_pairs={{0,48},{1,17},{2,50},{3,19},{4,52},{5,21},{6,54},{7,23},{8,56},{9,... | collective-permute-start | bytes 1474568 | tf_op jit(solution)/shard_map/ppermute | solution.py:26
  60.6 1.0 fusion.2
  61.6 10.2 %collective-permute-done.10 = f32[8,2,16,480]{3,2,0,1:T(8,128)S(1)} collective-permute-done((f32[8,2,16,480]{3,2,0,1:T(8,128)S(1)}, f32[8,2,16,480]{3,2,0,1:T(8,128)S(1)}, u32[]{:S(2)}, u32[]{:S(2)}) %collective-permute-start.10) | collective-permute-done | bytes 491552 | tf_op jit(solution)/shard_map/ppermute | solution.py:26
  71.8 0.1 maximum_add_fusion
  71.9 0.0 copy-start.2
  71.9 0.0 copy-start.3
  71.9 0.0 copy-start.4
  72.0 0.1 dynamic-slice_bitcast_fusion.2
  72.1 9.0 %collective-permute-start.11 = (f32[4,16,480]{2,1,0:T(8,128)S(1)}, f32[4,16,480]{2,1,0:T(8,128)S(1)}, u32[]{:S(2)}, u32[]{:S(2)}) collective-permute-start(f32[4,16,480]{2,1,0:T(8,128)S(1)} %get-tuple-element.25), channel_id=1, source_target_pairs={{0,1},{1,64},{2,3},{3,66},{4,5},{5,68},{6,7},{7,70},{8,9},{9,72},{... | collective-permute-start | bytes 368648 | tf_op jit(solution)/shard_map/ppermute | solution.py:26
  81.1 1.9 %collective-permute-start.12 = (f32[4,16,480]{2,1,0:T(8,128)S(1)}, f32[4,16,480]{2,1,0:T(8,128)S(1)}, u32[]{:S(2)}, u32[]{:S(2)}) collective-permute-start(f32[4,16,480]{2,1,0:T(8,128)S(1)} %get-tuple-element.23), channel_id=1, source_target_pairs={{0,0},{1,65},{2,2},{3,67},{4,4},{5,69},{6,6},{7,71},{8,8},{9,73},{... | collective-permute-start | bytes 368648 | tf_op jit(solution)/shard_map/ppermute | solution.py:26
  83.1 15.9 %collective-permute-start.13 = (f32[4,16,480]{2,1,0:T(8,128)S(1)}, f32[4,16,480]{2,1,0:T(8,128)S(1)}, u32[]{:S(2)}, u32[]{:S(2)}) collective-permute-start(f32[4,16,480]{2,1,0:T(8,128)S(1)} %get-tuple-element.24), channel_id=1, source_target_pairs={{0,897},{1,960},{2,899},{3,962},{4,901},{5,964},{6,903},{7,966},{8... | collective-permute-start | bytes 368648 | tf_op jit(solution)/shard_map/ppermute | solution.py:26
  98.9 2.0 %collective-permute-start.14 = (f32[4,16,480]{2,1,0:T(8,128)S(1)}, f32[4,16,480]{2,1,0:T(8,128)S(1)}, u32[]{:S(2)}, u32[]{:S(2)}) collective-permute-start(f32[4,16,480]{2,1,0:T(8,128)S(1)} %get-tuple-element.26), channel_id=1, source_target_pairs={{0,896},{1,961},{2,898},{3,963},{4,900},{5,965},{6,902},{7,967},{8... | collective-permute-start | bytes 368648 | tf_op jit(solution)/shard_map/ppermute | solution.py:26
  101.0 0.0 collective-permute-done.11
  101.0 0.0 collective-permute-done.12
  101.0 1.3 %collective-permute-done.13 = f32[4,16,480]{2,1,0:T(8,128)S(1)} collective-permute-done((f32[4,16,480]{2,1,0:T(8,128)S(1)}, f32[4,16,480]{2,1,0:T(8,128)S(1)}, u32[]{:S(2)}, u32[]{:S(2)}) %collective-permute-start.13) | collective-permute-done | bytes 122912 | tf_op jit(solution)/shard_map/ppermute | solution.py:26
  102.3 4.4 %collective-permute-done.14 = f32[4,16,480]{2,1,0:T(8,128)S(1)} collective-permute-done((f32[4,16,480]{2,1,0:T(8,128)S(1)}, f32[4,16,480]{2,1,0:T(8,128)S(1)}, u32[]{:S(2)}, u32[]{:S(2)}) %collective-permute-start.14) | collective-permute-done | bytes 122912 | tf_op jit(solution)/shard_map/ppermute | solution.py:26
  106.7 0.7 add_add_fusion
  107.4 10.7 %all-to-all-start = ((f32[4,16,480]{2,1,0:T(8,128)}), f32[4,16,480]{2,1,0:T(8,128)S(1)}, u32[]{:S(2)}, u32[]{:S(2)}) async-start(f32[4,16,480]{2,1,0:T(8,128)} %add_add_fusion), calls=%async_computation | async-start | bytes 262144 | tf_op jit(solution)/shard_map/all_to_all | solution.py:124
  118.1 0.0 copy-done.2
  118.1 0.0 copy-done.3
  118.1 0.1 broadcast_subtract_fusion
  118.2 0.1 sub.54
  118.3 0.0 copy-done.4
  118.3 0.1 broadcast_subtract_fusion.1
  118.4 0.1 sub.50
  118.5 0.1 dynamic_slice.40
  118.6 0.1 dynamic_slice.39
  118.7 7.7 %all-to-all-done = f32[4,16,480]{2,1,0:T(8,128)S(1)} async-done(((f32[4,16,480]{2,1,0:T(8,128)}), f32[4,16,480]{2,1,0:T(8,128)S(1)}, u32[]{:S(2)}, u32[]{:S(2)}) %all-to-all-start) | async-done | bytes 122912 | tf_op jit(solution)/shard_map/all_to_all | solution.py:124
  126.4 0.7 fusion.20
  (26 shorter events, 0.5 us)
Async XLA Ops:
  0.0 39.1 %collective-permute-start.6 = (f32[1125,480]{0,1:T(8,128)}, f32[1125,480]{0,1:T(8,128)S(1)}, u32[]{:S(2)}, u32[]{:S(2)}) collective-permute-start(f32[1125,480]{0,1:T(8,128)} %param.6), channel_id=1, source_target_pairs={{0,1},{1,0},{2,3},{3,2},{4,5},{5,4},{6,7},{7,6},{8,9},{9,8},{10,11... | collective-permute-start | bytes 6480008 | tf_op jit(solution)/shard_map/ppermute | solution.py:26
  3.8 29.8 %copy-start = (f32[1125,480]{0,1:T(8,128)S(1)}, f32[1125,480]{0,1:T(8,128)}, u32[]{:S(2)}) copy-start(f32[1125,480]{0,1:T(8,128)} %param.6) | copy-start | bytes 6480004
  3.9 8.8 %collective-permute-start.3 = (f32[64,1125]{1,0:T(8,128)S(1)}, f32[64,1125]{1,0:T(8,128)S(1)}, u32[]{:S(2)}, u32[]{:S(2)}) collective-permute-start(f32[64,1125]{1,0:T(8,128)S(1)} %pad_maximum_fusion.2), channel_id=1, source_target_pairs={{0,2},{1,15},{2,4},{3,1},{4,6},{5,3},{6,8},{7,5},{8,10},{9,7},{10,... | collective-permute-start | bytes 864008 | tf_op jit(solution)/shard_map/ppermute | solution.py:26
  6.1 9.6 %collective-permute-start = (f32[64,1125]{1,0:T(8,128)S(1)}, f32[64,1125]{1,0:T(8,128)S(1)}, u32[]{:S(2)}, u32[]{:S(2)}) collective-permute-start(f32[64,1125]{1,0:T(8,128)S(1)} %pad_maximum_fusion.2), channel_id=1, source_target_pairs={{0,14},{1,3},{2,0},{3,5},{4,2},{5,7},{6,4},{7,9},{8,6},{9,11},{10,... | collective-permute-start | bytes 864008 | tf_op jit(solution)/shard_map/ppermute | solution.py:26
  12.7 8.7 %collective-permute-start.4 = (f32[64,1125]{1,0:T(8,128)S(1)}, f32[64,1125]{1,0:T(8,128)S(1)}, u32[]{:S(2)}, u32[]{:S(2)}) collective-permute-start(f32[64,1125]{1,0:T(8,128)S(1)} %collective-permute-done.3), channel_id=1, source_target_pairs={{0,2},{1,15},{2,4},{3,1},{4,6},{5,3},{6,8},{7,5},{8,10},{9,7},{10,... | collective-permute-start | bytes 864008 | tf_op jit(solution)/shard_map/ppermute | solution.py:26
  15.7 16.0 %collective-permute-start.1 = (f32[64,1125]{1,0:T(8,128)S(1)}, f32[64,1125]{1,0:T(8,128)S(1)}, u32[]{:S(2)}, u32[]{:S(2)}) collective-permute-start(f32[64,1125]{1,0:T(8,128)S(1)} %collective-permute-done), channel_id=1, source_target_pairs={{0,14},{1,3},{2,0},{3,5},{4,2},{5,7},{6,4},{7,9},{8,6},{9,11},{10,... | collective-permute-start | bytes 864008 | tf_op jit(solution)/shard_map/ppermute | solution.py:26
  21.4 13.9 %collective-permute-start.5 = (f32[64,1125]{1,0:T(8,128)S(1)}, f32[64,1125]{1,0:T(8,128)S(1)}, u32[]{:S(2)}, u32[]{:S(2)}) collective-permute-start(f32[64,1125]{1,0:T(8,128)S(1)} %collective-permute-done.4), channel_id=1, source_target_pairs={{0,2},{1,15},{2,4},{3,1},{4,6},{5,3},{6,8},{7,5},{8,10},{9,7},{10,... | collective-permute-start | bytes 864008 | tf_op jit(solution)/shard_map/ppermute | solution.py:26
  31.7 9.0 %collective-permute-start.2 = (f32[64,1125]{1,0:T(8,128)S(1)}, f32[64,1125]{1,0:T(8,128)S(1)}, u32[]{:S(2)}, u32[]{:S(2)}) collective-permute-start(f32[64,1125]{1,0:T(8,128)S(1)} %collective-permute-done.1), channel_id=1, source_target_pairs={{0,14},{1,3},{2,0},{3,5},{4,2},{5,7},{6,4},{7,9},{8,6},{9,11},{10,... | collective-permute-start | bytes 864008 | tf_op jit(solution)/shard_map/ppermute | solution.py:26
  35.2 9.6 %collective-permute-start.8 = (f32[64,1125]{1,0:T(8,128)S(1)}, f32[64,1125]{1,0:T(8,128)S(1)}, u32[]{:S(2)}, u32[]{:S(2)}) collective-permute-start(f32[64,1125]{1,0:T(8,128)S(1)} %collective-permute-done.5), channel_id=1, source_target_pairs={{0,2},{1,15},{2,4},{3,1},{4,6},{5,3},{6,8},{7,5},{8,10},{9,7},{10,... | collective-permute-start | bytes 864008 | tf_op jit(solution)/shard_map/ppermute | solution.py:26
  40.9 16.8 %collective-permute-start.7 = (f32[5,2,2,16,480]{4,3,0,1,2:T(8,128)S(1)}, f32[5,2,2,16,480]{4,3,0,1,2:T(8,128)S(1)}, u32[]{:S(2)}, u32[]{:S(2)}) collective-permute-start(f32[5,2,2,16,480]{4,3,0,1,2:T(8,128)S(1)} %slice.97), channel_id=1, source_target_pairs={{0,16},{1,49},{2,18},{3,51},{4,20},{5,53},{6,22},{7,55},{8,24},{9,... | collective-permute-start | bytes 1843208 | tf_op jit(solution)/shard_map/ppermute | solution.py:26
  47.3 10.3 %collective-permute-start.9 = (f32[3,2,2,16,480]{4,3,0,1,2:T(8,128)S(1)}, f32[3,2,2,16,480]{4,3,0,1,2:T(8,128)S(1)}, u32[]{:S(2)}, u32[]{:S(2)}) collective-permute-start(f32[3,2,2,16,480]{4,3,0,1,2:T(8,128)S(1)} %copy.40), channel_id=1, source_target_pairs={{0,16},{1,49},{2,18},{3,51},{4,20},{5,53},{6,22},{7,55},{8,24},{9,... | collective-permute-start | bytes 1105928 | tf_op jit(solution)/shard_map/ppermute | solution.py:26
  57.7 0.8 copy-start.1
  58.6 13.2 %collective-permute-start.10 = (f32[8,2,16,480]{3,2,0,1:T(8,128)S(1)}, f32[8,2,16,480]{3,2,0,1:T(8,128)S(1)}, u32[]{:S(2)}, u32[]{:S(2)}) collective-permute-start(f32[8,2,16,480]{3,2,0,1:T(8,128)S(1)} %pad_maximum_fusion.1), channel_id=1, source_target_pairs={{0,48},{1,17},{2,50},{3,19},{4,52},{5,21},{6,54},{7,23},{8,56},{9,... | collective-permute-start | bytes 1474568 | tf_op jit(solution)/shard_map/ppermute | solution.py:26
  71.9 46.2 %copy-start.2 = (f32[60]{0:T(128)S(1)}, f32[60]{0:T(128)}, u32[]{:S(2)}) copy-start(f32[60]{0:T(128)} %param.7) | copy-start | bytes 724
  71.9 46.2 %copy-start.3 = (f32[128]{0:T(128)S(1)}, f32[128]{0:T(128)}, u32[]{:S(2)}) copy-start(f32[128]{0:T(128)} %param.9) | copy-start | bytes 1540
  71.9 46.4 %copy-start.4 = (f32[16]{0:T(128)S(1)}, f32[16]{0:T(128)}, u32[]{:S(2)}) copy-start(f32[16]{0:T(128)} %param.8) | copy-start | bytes 196
  72.1 28.9 %collective-permute-start.11 = (f32[4,16,480]{2,1,0:T(8,128)S(1)}, f32[4,16,480]{2,1,0:T(8,128)S(1)}, u32[]{:S(2)}, u32[]{:S(2)}) collective-permute-start(f32[4,16,480]{2,1,0:T(8,128)S(1)} %get-tuple-element.25), channel_id=1, source_target_pairs={{0,1},{1,64},{2,3},{3,66},{4,5},{5,68},{6,7},{7,70},{8,9},{9,72},{... | collective-permute-start | bytes 368648 | tf_op jit(solution)/shard_map/ppermute | solution.py:26
  81.1 19.9 %collective-permute-start.12 = (f32[4,16,480]{2,1,0:T(8,128)S(1)}, f32[4,16,480]{2,1,0:T(8,128)S(1)}, u32[]{:S(2)}, u32[]{:S(2)}) collective-permute-start(f32[4,16,480]{2,1,0:T(8,128)S(1)} %get-tuple-element.23), channel_id=1, source_target_pairs={{0,0},{1,65},{2,2},{3,67},{4,4},{5,69},{6,6},{7,71},{8,8},{9,73},{... | collective-permute-start | bytes 368648 | tf_op jit(solution)/shard_map/ppermute | solution.py:26
  83.1 19.3 %collective-permute-start.13 = (f32[4,16,480]{2,1,0:T(8,128)S(1)}, f32[4,16,480]{2,1,0:T(8,128)S(1)}, u32[]{:S(2)}, u32[]{:S(2)}) collective-permute-start(f32[4,16,480]{2,1,0:T(8,128)S(1)} %get-tuple-element.24), channel_id=1, source_target_pairs={{0,897},{1,960},{2,899},{3,962},{4,901},{5,964},{6,903},{7,966},{8... | collective-permute-start | bytes 368648 | tf_op jit(solution)/shard_map/ppermute | solution.py:26
  98.9 7.7 %collective-permute-start.14 = (f32[4,16,480]{2,1,0:T(8,128)S(1)}, f32[4,16,480]{2,1,0:T(8,128)S(1)}, u32[]{:S(2)}, u32[]{:S(2)}) collective-permute-start(f32[4,16,480]{2,1,0:T(8,128)S(1)} %get-tuple-element.26), channel_id=1, source_target_pairs={{0,896},{1,961},{2,898},{3,963},{4,900},{5,965},{6,902},{7,967},{8... | collective-permute-start | bytes 368648 | tf_op jit(solution)/shard_map/ppermute | solution.py:26
  107.4 19.0 %all-to-all-start = ((f32[4,16,480]{2,1,0:T(8,128)}), f32[4,16,480]{2,1,0:T(8,128)S(1)}, u32[]{:S(2)}, u32[]{:S(2)}) async-start(f32[4,16,480]{2,1,0:T(8,128)} %add_add_fusion), calls=%async_computation | async-start | bytes 262144 | tf_op jit(solution)/shard_map/all_to_all | solution.py:124

commit v11 on v7

--- a/solution.py
+++ b/solution.py
@@ -94,14 +94,12 @@
     f3 = send(f2, along_y(1))
     h3 = send(h2, along_y(-1))
     near_blocks = (block, f1, h1, f2, h2)
-    own = product(near_blocks, integrals)
-    f3_after, own = lax.optimization_barrier((f3, own))
+    early = jnp.stack([product(near_blocks, integrals), product(near_blocks, others)], 1)
+    f3_after, early = lax.optimization_barrier((f3, early))
     f4 = send(f3_after, along_y(1))
-    early = jnp.stack([own, product(near_blocks, others)], 1)
-    h3_after, early = lax.optimization_barrier((h3, early))
     arrived = send(early[:, :, 1:3], along_x(1))
     passed_on = early[:, :, 3] + arrived[:, :, 1]
-    far_blocks = (f3, h3_after, f4)
+    far_blocks = (f3, h3, f4)
     late = jnp.stack([product(far_blocks, integrals), product(far_blocks, others)], 1)
     late_first = send(late[:, :, 1], along_x(1))
     late_last, late_far = late[:, :, 3], late[:, :, 2]

time: 130 us -> 128 us (0.985)
  the two profiles are of different devices: /device:TPU:30 before, /device:TPU:25 now
where the time goes in v11:
time: 128 us; the launch traced here: 126 us
  starting transfers between devices  85.6 us (67%)
  waiting for transfers between devices  28.8 us (22%)
  matrix products  5.42 us (4%)
  local copies, waits for them, and re-layouts  2.74 us (2%)
  other arithmetic  2.69 us (2%)
    ppermute x17, starting transfers between devices, send(): return lax.ppermute(array, AXES, table(move))  74.9 us
    ppermute x17, waiting for transfers between devices, send(): return lax.ppermute(array, AXES, table(move))  21.1 us
    all_to_all x1, starting transfers between devices, per_device(): lax.all_to_all(total, AXES, 0, 0, tiled=True, axis_index_groups=classes())  10.7 us
    all_to_all x1, waiting for transfers between devices, per_device(): lax.all_to_all(total, AXES, 0, 0, tiled=True, axis_index_groups=classes())  7.73 us
    dot_general x4, matrix products, product(): jnp.dot(tall, part, precision=lax.Precision.HIGH, preferred_element_type=...  5.42 us
  transfers between devices with their start and end apart: 18, of which 13 were waited for; matrix products, arithmetic and copies ran while one was open for 7% of the time, Pallas kernels for 0%

profile of v11, /device:TPU:25, one launch (start us, length us, event | category | flops | bytes accessed | tf_op | source)
XLA Modules:
  0.0 126.0 jit_solution(13665030631837654430)
XLA Ops:
  0.0 2.6 %collective-permute-start.6 = (f32[1125,480]{0,1:T(8,128)}, f32[1125,480]{0,1:T(8,128)S(1)}, u32[]{:S(2)}, u32[]{:S(2)}) collective-permute-start(f32[1125,480]{0,1:T(8,128)} %param.6), channel_id=1, source_target_pairs={{0,1},{1,0},{2,3},{3,2},{4,5},{5,4},{6,7},{7,6},{8,9},{9,8},{10,11... | collective-permute-start | bytes 6480008 | tf_op jit(solution)/shard_map/ppermute | solution.py:26
  2.7 1.0 reshape.37
  3.8 0.0 copy-start
  3.9 2.2 %collective-permute-start = (f32[64,1125]{1,0:T(8,128)S(1)}, f32[64,1125]{1,0:T(8,128)S(1)}, u32[]{:S(2)}, u32[]{:S(2)}) collective-permute-start(f32[64,1125]{1,0:T(8,128)S(1)} %pad_maximum_fusion.1), channel_id=1, source_target_pairs={{0,2},{1,15},{2,4},{3,1},{4,6},{5,3},{6,8},{7,5},{8,10},{9,7},{10,... | collective-permute-start | bytes 864008 | tf_op jit(solution)/shard_map/ppermute | solution.py:26
  6.1 4.4 %collective-permute-start.3 = (f32[64,1125]{1,0:T(8,128)S(1)}, f32[64,1125]{1,0:T(8,128)S(1)}, u32[]{:S(2)}, u32[]{:S(2)}) collective-permute-start(f32[64,1125]{1,0:T(8,128)S(1)} %pad_maximum_fusion.1), channel_id=1, source_target_pairs={{0,14},{1,3},{2,0},{3,5},{4,2},{5,7},{6,4},{7,9},{8,6},{9,11},{10,... | collective-permute-start | bytes 864008 | tf_op jit(solution)/shard_map/ppermute | solution.py:26
  10.5 2.2 %collective-permute-done = f32[64,1125]{1,0:T(8,128)S(1)} collective-permute-done((f32[64,1125]{1,0:T(8,128)S(1)}, f32[64,1125]{1,0:T(8,128)S(1)}, u32[]{:S(2)}, u32[]{:S(2)}) %collective-permute-start) | collective-permute-done | bytes 288032 | tf_op jit(solution)/shard_map/ppermute | solution.py:26
  12.7 1.9 %collective-permute-start.1 = (f32[64,1125]{1,0:T(8,128)S(1)}, f32[64,1125]{1,0:T(8,128)S(1)}, u32[]{:S(2)}, u32[]{:S(2)}) collective-permute-start(f32[64,1125]{1,0:T(8,128)S(1)} %collective-permute-done), channel_id=1, source_target_pairs={{0,2},{1,15},{2,4},{3,1},{4,6},{5,3},{6,8},{7,5},{8,10},{9,7},{10,... | collective-permute-start | bytes 864008 | tf_op jit(solution)/shard_map/ppermute | solution.py:26
  14.6 1.1 collective-permute-done.3
  15.7 5.0 %collective-permute-start.4 = (f32[64,1125]{1,0:T(8,128)S(1)}, f32[64,1125]{1,0:T(8,128)S(1)}, u32[]{:S(2)}, u32[]{:S(2)}) collective-permute-start(f32[64,1125]{1,0:T(8,128)S(1)} %collective-permute-done.3), channel_id=1, source_target_pairs={{0,14},{1,3},{2,0},{3,5},{4,2},{5,7},{6,4},{7,9},{8,6},{9,11},{10,... | collective-permute-start | bytes 864008 | tf_op jit(solution)/shard_map/ppermute | solution.py:26
  20.8 0.6 collective-permute-done.1
  21.4 9.5 %collective-permute-start.2 = (f32[64,1125]{1,0:T(8,128)S(1)}, f32[64,1125]{1,0:T(8,128)S(1)}, u32[]{:S(2)}, u32[]{:S(2)}) collective-permute-start(f32[64,1125]{1,0:T(8,128)S(1)} %collective-permute-done.1), channel_id=1, source_target_pairs={{0,2},{1,15},{2,4},{3,1},{4,6},{5,3},{6,8},{7,5},{8,10},{9,7},{10,... | collective-permute-start | bytes 864008 | tf_op jit(solution)/shard_map/ppermute | solution.py:26
  30.9 0.8 collective-permute-done.4
  31.7 1.9 %collective-permute-start.5 = (f32[64,1125]{1,0:T(8,128)S(1)}, f32[64,1125]{1,0:T(8,128)S(1)}, u32[]{:S(2)}, u32[]{:S(2)}) collective-permute-start(f32[64,1125]{1,0:T(8,128)S(1)} %collective-permute-done.4), channel_id=1, source_target_pairs={{0,14},{1,3},{2,0},{3,5},{4,2},{5,7},{6,4},{7,9},{8,6},{9,11},{10,... | collective-permute-start | bytes 864008 | tf_op jit(solution)/shard_map/ppermute | solution.py:26
  33.7 0.0 copy-done
  33.7 1.6 %fusion.26 = f32[320,480]{1,0:T(8,128)S(1)} fusion(f32[320,1125]{1,0:T(8,128)S(1)} %constant_dynamic-update-slice_fusion, f32[1125,480]{0,1:T(8,128)S(1)} %copy-done), kind=kOutput, calls=%fused_computation.71 | convolution fusion | flops 1036800000 | bytes 4214400 | tf_op jit(solution)/shard_map/dot_general | solution.py:91
  35.2 0.0 collective-permute-done.6
  35.2 1.5 %fusion.27 = f32[320,480]{1,0:T(8,128)S(1)} fusion(f32[320,1125]{1,0:T(8,128)S(1)} %constant_dynamic-update-slice_fusion, f32[1125,480]{0,1:T(8,128)S(1)} %collective-permute-done.6), kind=kOutput, calls=%fused_computation.72 | convolution fusion | flops 1036800000 | bytes 4214400 | tf_op jit(solution)/shard_map/dot_general | solution.py:91
  36.8 0.1 pad_maximum_fusion
  36.9 0.0 collective-permute-done.2
  36.9 3.8 %collective-permute-start.7 = (f32[64,1125]{1,0:T(8,128)S(1)}, f32[64,1125]{1,0:T(8,128)S(1)}, u32[]{:S(2)}, u32[]{:S(2)}) collective-permute-start(f32[64,1125]{1,0:T(8,128)S(1)} %collective-permute-done.2), channel_id=1, source_target_pairs={{0,2},{1,15},{2,4},{3,1},{4,6},{5,3},{6,8},{7,5},{8,10},{9,7},{10,... | collective-permute-start | bytes 864008 | tf_op jit(solution)/shard_map/ppermute | solution.py:26
  40.7 0.0 collective-permute-done.5
  40.8 0.1 copy.21
  40.9 1.9 %collective-permute-start.9 = (f32[5,2,2,16,480]{4,3,0,1,2:T(8,128)S(1)}, f32[5,2,2,16,480]{4,3,0,1,2:T(8,128)S(1)}, u32[]{:S(2)}, u32[]{:S(2)}) collective-permute-start(f32[5,2,2,16,480]{4,3,0,1,2:T(8,128)S(1)} %slice.97), channel_id=1, source_target_pairs={{0,16},{1,49},{2,18},{3,51},{4,20},{5,53},{6,22},{7,55},{8,24},{9,... | collective-permute-start | bytes 1843208 | tf_op jit(solution)/shard_map/ppermute | solution.py:26
  42.9 2.7 %collective-permute-done.7 = f32[64,1125]{1,0:T(8,128)S(1)} collective-permute-done((f32[64,1125]{1,0:T(8,128)S(1)}, f32[64,1125]{1,0:T(8,128)S(1)}, u32[]{:S(2)}, u32[]{:S(2)}) %collective-permute-start.7) | collective-permute-done | bytes 288032 | tf_op jit(solution)/shard_map/ppermute | solution.py:26
  45.6 1.2 fusion.28
  46.8 1.2 fusion.29
  48.0 0.1 fusion.4
  48.1 3.6 %collective-permute-start.8 = (f32[3,2,16,480]{3,2,1,0:T(8,128)S(1)}, f32[3,2,16,480]{3,2,1,0:T(8,128)S(1)}, u32[]{:S(2)}, u32[]{:S(2)}) collective-permute-start(f32[3,2,16,480]{3,2,1,0:T(8,128)S(1)} %bitcast.105), channel_id=1, source_target_pairs={{0,16},{1,49},{2,18},{3,51},{4,20},{5,53},{6,22},{7,55},{8,24},{9,... | collective-permute-start | bytes 552968 | tf_op jit(solution)/shard_map/ppermute | solution.py:26
  51.7 1.8 %collective-permute-done.9 = f32[5,2,2,16,480]{4,3,0,1,2:T(8,128)S(1)} collective-permute-done((f32[5,2,2,16,480]{4,3,0,1,2:T(8,128)S(1)}, f32[5,2,2,16,480]{4,3,0,1,2:T(8,128)S(1)}, u32[]{:S(2)}, u32[]{:S(2)}) %collective-permute-start.9) | collective-permute-done | bytes 614432 | tf_op jit(solution)/shard_map/ppermute | solution.py:26
  53.5 0.8 copy-done.1
  54.3 0.8 fusion.1
  55.1 2.0 %collective-permute-start.10 = (f32[5,2,16,480]{3,2,0,1:T(8,128)}, f32[5,2,16,480]{3,2,0,1:T(8,128)S(1)}, u32[]{:S(2)}, u32[]{:S(2)}) collective-permute-start(f32[5,2,16,480]{3,2,0,1:T(8,128)} %fusion.1), channel_id=1, source_target_pairs={{0,48},{1,17},{2,50},{3,19},{4,52},{5,21},{6,54},{7,23},{8,56},{9,... | collective-permute-start | bytes 921608 | tf_op jit(solution)/shard_map/ppermute | solution.py:26
  57.3 3.4 %collective-permute-start.11 = (f32[3,2,16,480]{3,2,1,0:T(8,128)S(1)}, f32[3,2,16,480]{3,2,1,0:T(8,128)S(1)}, u32[]{:S(2)}, u32[]{:S(2)}) collective-permute-start(f32[3,2,16,480]{3,2,1,0:T(8,128)S(1)} %bitcast.106), channel_id=1, source_target_pairs={{0,48},{1,17},{2,50},{3,19},{4,52},{5,21},{6,54},{7,23},{8,56},{9,... | collective-permute-start | bytes 552968 | tf_op jit(solution)/shard_map/ppermute | solution.py:26
  60.7 1.9 %collective-permute-start.12 = (f32[3,2,16,480]{3,2,1,0:T(8,128)S(1)}, f32[3,2,16,480]{3,2,1,0:T(8,128)S(1)}, u32[]{:S(2)}, u32[]{:S(2)}) collective-permute-start(f32[3,2,16,480]{3,2,1,0:T(8,128)S(1)} %bitcast.107), channel_id=1, source_target_pairs={{0,32},{1,33},{2,34},{3,35},{4,36},{5,37},{6,38},{7,39},{8,40},{9,... | collective-permute-start | bytes 552968 | tf_op jit(solution)/shard_map/ppermute | solution.py:26
  62.6 0.0 collective-permute-done.8
  62.6 2.1 %collective-permute-done.10 = f32[5,2,16,480]{3,2,0,1:T(8,128)S(1)} collective-permute-done((f32[5,2,16,480]{3,2,0,1:T(8,128)}, f32[5,2,16,480]{3,2,0,1:T(8,128)S(1)}, u32[]{:S(2)}, u32[]{:S(2)}) %collective-permute-start.10) | collective-permute-done | bytes 307232 | tf_op jit(solution)/shard_map/ppermute | solution.py:26
  64.7 0.0 copy-done.2
  64.7 0.1 fusion.3
  64.8 2.9 %collective-permute-done.11 = f32[3,2,16,480]{3,2,1,0:T(8,128)S(1)} collective-permute-done((f32[3,2,16,480]{3,2,1,0:T(8,128)S(1)}, f32[3,2,16,480]{3,2,1,0:T(8,128)S(1)}, u32[]{:S(2)}, u32[]{:S(2)}) %collective-permute-start.11) | collective-permute-done | bytes 184352 | tf_op jit(solution)/shard_map/ppermute | solution.py:26
  67.8 1.2 collective-permute-done.12
  69.0 0.0 copy-start.3
  69.0 0.0 copy-start.4
  69.1 0.0 copy-start.5
  69.2 0.1 dynamic-slice_bitcast_fusion.2
  69.2 10.9 %collective-permute-start.13 = (f32[4,16,480]{2,1,0:T(8,128)S(1)}, f32[4,16,480]{2,1,0:T(8,128)S(1)}, u32[]{:S(2)}, u32[]{:S(2)}) collective-permute-start(f32[4,16,480]{2,1,0:T(8,128)S(1)} %get-tuple-element.27), channel_id=1, source_target_pairs={{0,1},{1,64},{2,3},{3,66},{4,5},{5,68},{6,7},{7,70},{8,9},{9,72},{... | collective-permute-start | bytes 368648 | tf_op jit(solution)/shard_map/ppermute | solution.py:26
  80.1 1.9 %collective-permute-start.14 = (f32[4,16,480]{2,1,0:T(8,128)S(1)}, f32[4,16,480]{2,1,0:T(8,128)S(1)}, u32[]{:S(2)}, u32[]{:S(2)}) collective-permute-start(f32[4,16,480]{2,1,0:T(8,128)S(1)} %get-tuple-element.25), channel_id=1, source_target_pairs={{0,0},{1,65},{2,2},{3,67},{4,4},{5,69},{6,6},{7,71},{8,8},{9,73},{... | collective-permute-start | bytes 368648 | tf_op jit(solution)/shard_map/ppermute | solution.py:26
  82.0 15.9 %collective-permute-start.15 = (f32[4,16,480]{2,1,0:T(8,128)S(1)}, f32[4,16,480]{2,1,0:T(8,128)S(1)}, u32[]{:S(2)}, u32[]{:S(2)}) collective-permute-start(f32[4,16,480]{2,1,0:T(8,128)S(1)} %get-tuple-element.26), channel_id=1, source_target_pairs={{0,897},{1,960},{2,899},{3,962},{4,901},{5,964},{6,903},{7,966},{8... | collective-permute-start | bytes 368648 | tf_op jit(solution)/shard_map/ppermute | solution.py:26
  97.9 2.0 %collective-permute-start.16 = (f32[4,16,480]{2,1,0:T(8,128)S(1)}, f32[4,16,480]{2,1,0:T(8,128)S(1)}, u32[]{:S(2)}, u32[]{:S(2)}) collective-permute-start(f32[4,16,480]{2,1,0:T(8,128)S(1)} %get-tuple-element.28), channel_id=1, source_target_pairs={{0,896},{1,961},{2,898},{3,963},{4,900},{5,965},{6,902},{7,967},{8... | collective-permute-start | bytes 368648 | tf_op jit(solution)/shard_map/ppermute | solution.py:26
  99.9 0.0 collective-permute-done.13
  100.0 0.1 collective-permute-done.14
  100.1 1.3 collective-permute-done.15
  101.3 4.4 %collective-permute-done.16 = f32[4,16,480]{2,1,0:T(8,128)S(1)} collective-permute-done((f32[4,16,480]{2,1,0:T(8,128)S(1)}, f32[4,16,480]{2,1,0:T(8,128)S(1)}, u32[]{:S(2)}, u32[]{:S(2)}) %collective-permute-start.16) | collective-permute-done | bytes 122912 | tf_op jit(solution)/shard_map/ppermute | solution.py:26
  105.7 0.7 add_add_fusion.1
  106.3 10.7 %all-to-all-start = ((f32[4,16,480]{2,1,0:T(8,128)}), f32[4,16,480]{2,1,0:T(8,128)S(1)}, u32[]{:S(2)}, u32[]{:S(2)}) async-start(f32[4,16,480]{2,1,0:T(8,128)} %add_add_fusion.1), calls=%async_computation | async-start | bytes 262144 | tf_op jit(solution)/shard_map/all_to_all | solution.py:123
  117.1 0.0 copy-done.3
  117.1 0.0 copy-done.4
  117.1 0.1 broadcast_subtract_fusion
  117.2 0.1 sub.54
  117.3 0.1 broadcast_subtract_fusion.1
  117.4 0.1 sub.50
  117.4 0.1 dynamic_slice.40
  117.5 0.1 dynamic_slice.39
  117.6 7.7 %all-to-all-done = f32[4,16,480]{2,1,0:T(8,128)S(1)} async-done(((f32[4,16,480]{2,1,0:T(8,128)}), f32[4,16,480]{2,1,0:T(8,128)S(1)}, u32[]{:S(2)}, u32[]{:S(2)}) %all-to-all-start) | async-done | bytes 122912 | tf_op jit(solution)/shard_map/all_to_all | solution.py:123
  125.3 0.7 fusion.20
  (30 shorter events, 0.5 us)
Async XLA Ops:
  0.0 35.2 %collective-permute-start.6 = (f32[1125,480]{0,1:T(8,128)}, f32[1125,480]{0,1:T(8,128)S(1)}, u32[]{:S(2)}, u32[]{:S(2)}) collective-permute-start(f32[1125,480]{0,1:T(8,128)} %param.6), channel_id=1, source_target_pairs={{0,1},{1,0},{2,3},{3,2},{4,5},{5,4},{6,7},{7,6},{8,9},{9,8},{10,11... | collective-permute-start | bytes 6480008 | tf_op jit(solution)/shard_map/ppermute | solution.py:26
  3.8 29.8 %copy-start = (f32[1125,480]{0,1:T(8,128)S(1)}, f32[1125,480]{0,1:T(8,128)}, u32[]{:S(2)}) copy-start(f32[1125,480]{0,1:T(8,128)} %param.6) | copy-start | bytes 6480004
  3.9 8.8 %collective-permute-start = (f32[64,1125]{1,0:T(8,128)S(1)}, f32[64,1125]{1,0:T(8,128)S(1)}, u32[]{:S(2)}, u32[]{:S(2)}) collective-permute-start(f32[64,1125]{1,0:T(8,128)S(1)} %pad_maximum_fusion.1), channel_id=1, source_target_pairs={{0,2},{1,15},{2,4},{3,1},{4,6},{5,3},{6,8},{7,5},{8,10},{9,7},{10,... | collective-permute-start | bytes 864008 | tf_op jit(solution)/shard_map/ppermute | solution.py:26
  6.1 9.6 %collective-permute-start.3 = (f32[64,1125]{1,0:T(8,128)S(1)}, f32[64,1125]{1,0:T(8,128)S(1)}, u32[]{:S(2)}, u32[]{:S(2)}) collective-permute-start(f32[64,1125]{1,0:T(8,128)S(1)} %pad_maximum_fusion.1), channel_id=1, source_target_pairs={{0,14},{1,3},{2,0},{3,5},{4,2},{5,7},{6,4},{7,9},{8,6},{9,11},{10,... | collective-permute-start | bytes 864008 | tf_op jit(solution)/shard_map/ppermute | solution.py:26
  12.7 8.7 %collective-permute-start.1 = (f32[64,1125]{1,0:T(8,128)S(1)}, f32[64,1125]{1,0:T(8,128)S(1)}, u32[]{:S(2)}, u32[]{:S(2)}) collective-permute-start(f32[64,1125]{1,0:T(8,128)S(1)} %collective-permute-done), channel_id=1, source_target_pairs={{0,2},{1,15},{2,4},{3,1},{4,6},{5,3},{6,8},{7,5},{8,10},{9,7},{10,... | collective-permute-start | bytes 864008 | tf_op jit(solution)/shard_map/ppermute | solution.py:26
  15.7 16.0 %collective-permute-start.4 = (f32[64,1125]{1,0:T(8,128)S(1)}, f32[64,1125]{1,0:T(8,128)S(1)}, u32[]{:S(2)}, u32[]{:S(2)}) collective-permute-start(f32[64,1125]{1,0:T(8,128)S(1)} %collective-permute-done.3), channel_id=1, source_target_pairs={{0,14},{1,3},{2,0},{3,5},{4,2},{5,7},{6,4},{7,9},{8,6},{9,11},{10,... | collective-permute-start | bytes 864008 | tf_op jit(solution)/shard_map/ppermute | solution.py:26
  21.4 15.6 %collective-permute-start.2 = (f32[64,1125]{1,0:T(8,128)S(1)}, f32[64,1125]{1,0:T(8,128)S(1)}, u32[]{:S(2)}, u32[]{:S(2)}) collective-permute-start(f32[64,1125]{1,0:T(8,128)S(1)} %collective-permute-done.1), channel_id=1, source_target_pairs={{0,2},{1,15},{2,4},{3,1},{4,6},{5,3},{6,8},{7,5},{8,10},{9,7},{10,... | collective-permute-start | bytes 864008 | tf_op jit(solution)/shard_map/ppermute | solution.py:26
  31.7 9.0 %collective-permute-start.5 = (f32[64,1125]{1,0:T(8,128)S(1)}, f32[64,1125]{1,0:T(8,128)S(1)}, u32[]{:S(2)}, u32[]{:S(2)}) collective-permute-start(f32[64,1125]{1,0:T(8,128)S(1)} %collective-permute-done.4), channel_id=1, source_target_pairs={{0,14},{1,3},{2,0},{3,5},{4,2},{5,7},{6,4},{7,9},{8,6},{9,11},{10,... | collective-permute-start | bytes 864008 | tf_op jit(solution)/shard_map/ppermute | solution.py:26
  36.9 8.7 %collective-permute-start.7 = (f32[64,1125]{1,0:T(8,128)S(1)}, f32[64,1125]{1,0:T(8,128)S(1)}, u32[]{:S(2)}, u32[]{:S(2)}) collective-permute-start(f32[64,1125]{1,0:T(8,128)S(1)} %collective-permute-done.2), channel_id=1, source_target_pairs={{0,2},{1,15},{2,4},{3,1},{4,6},{5,3},{6,8},{7,5},{8,10},{9,7},{10,... | collective-permute-start | bytes 864008 | tf_op jit(solution)/shard_map/ppermute | solution.py:26
  40.9 12.5 %collective-permute-start.9 = (f32[5,2,2,16,480]{4,3,0,1,2:T(8,128)S(1)}, f32[5,2,2,16,480]{4,3,0,1,2:T(8,128)S(1)}, u32[]{:S(2)}, u32[]{:S(2)}) collective-permute-start(f32[5,2,2,16,480]{4,3,0,1,2:T(8,128)S(1)} %slice.97), channel_id=1, source_target_pairs={{0,16},{1,49},{2,18},{3,51},{4,20},{5,53},{6,22},{7,55},{8,24},{9,... | collective-permute-start | bytes 1843208 | tf_op jit(solution)/shard_map/ppermute | solution.py:26
  48.1 14.5 %collective-permute-start.8 = (f32[3,2,16,480]{3,2,1,0:T(8,128)S(1)}, f32[3,2,16,480]{3,2,1,0:T(8,128)S(1)}, u32[]{:S(2)}, u32[]{:S(2)}) collective-permute-start(f32[3,2,16,480]{3,2,1,0:T(8,128)S(1)} %bitcast.105), channel_id=1, source_target_pairs={{0,16},{1,49},{2,18},{3,51},{4,20},{5,53},{6,22},{7,55},{8,24},{9,... | collective-permute-start | bytes 552968 | tf_op jit(solution)/shard_map/ppermute | solution.py:26
  53.5 0.8 copy-start.1
  55.1 9.6 %copy-start.2 = (f32[5,2,2,16,480]{4,3,0,1,2:T(8,128)S(1)}, f32[5,2,2,16,480]{4,3,0,1,2:T(8,128)}, u32[]{:S(2)}) copy-start(f32[5,2,2,16,480]{4,3,0,1,2:T(8,128)} %copy-done.1) | copy-start | bytes 1843204
  55.1 9.6 %collective-permute-start.10 = (f32[5,2,16,480]{3,2,0,1:T(8,128)}, f32[5,2,16,480]{3,2,0,1:T(8,128)S(1)}, u32[]{:S(2)}, u32[]{:S(2)}) collective-permute-start(f32[5,2,16,480]{3,2,0,1:T(8,128)} %fusion.1), channel_id=1, source_target_pairs={{0,48},{1,17},{2,50},{3,19},{4,52},{5,21},{6,54},{7,23},{8,56},{9,... | collective-permute-start | bytes 921608 | tf_op jit(solution)/shard_map/ppermute | solution.py:26
  57.3 10.5 %collective-permute-start.11 = (f32[3,2,16,480]{3,2,1,0:T(8,128)S(1)}, f32[3,2,16,480]{3,2,1,0:T(8,128)S(1)}, u32[]{:S(2)}, u32[]{:S(2)}) collective-permute-start(f32[3,2,16,480]{3,2,1,0:T(8,128)S(1)} %bitcast.106), channel_id=1, source_target_pairs={{0,48},{1,17},{2,50},{3,19},{4,52},{5,21},{6,54},{7,23},{8,56},{9,... | collective-permute-start | bytes 552968 | tf_op jit(solution)/shard_map/ppermute | solution.py:26
  60.7 8.3 %collective-permute-start.12 = (f32[3,2,16,480]{3,2,1,0:T(8,128)S(1)}, f32[3,2,16,480]{3,2,1,0:T(8,128)S(1)}, u32[]{:S(2)}, u32[]{:S(2)}) collective-permute-start(f32[3,2,16,480]{3,2,1,0:T(8,128)S(1)} %bitcast.107), channel_id=1, source_target_pairs={{0,32},{1,33},{2,34},{3,35},{4,36},{5,37},{6,38},{7,39},{8,40},{9,... | collective-permute-start | bytes 552968 | tf_op jit(solution)/shard_map/ppermute | solution.py:26
  69.0 48.0 %copy-start.3 = (f32[60]{0:T(128)S(1)}, f32[60]{0:T(128)}, u32[]{:S(2)}) copy-start(f32[60]{0:T(128)} %param.7) | copy-start | bytes 724
  69.0 48.0 %copy-start.4 = (f32[128]{0:T(128)S(1)}, f32[128]{0:T(128)}, u32[]{:S(2)}) copy-start(f32[128]{0:T(128)} %param.9) | copy-start | bytes 1540
  69.1 48.2 %copy-start.5 = (f32[16]{0:T(128)S(1)}, f32[16]{0:T(128)}, u32[]{:S(2)}) copy-start(f32[16]{0:T(128)} %param.8) | copy-start | bytes 196
  69.2 30.7 %collective-permute-start.13 = (f32[4,16,480]{2,1,0:T(8,128)S(1)}, f32[4,16,480]{2,1,0:T(8,128)S(1)}, u32[]{:S(2)}, u32[]{:S(2)}) collective-permute-start(f32[4,16,480]{2,1,0:T(8,128)S(1)} %get-tuple-element.27), channel_id=1, source_target_pairs={{0,1},{1,64},{2,3},{3,66},{4,5},{5,68},{6,7},{7,70},{8,9},{9,72},{... | collective-permute-start | bytes 368648 | tf_op jit(solution)/shard_map/ppermute | solution.py:26
  80.1 19.9 %collective-permute-start.14 = (f32[4,16,480]{2,1,0:T(8,128)S(1)}, f32[4,16,480]{2,1,0:T(8,128)S(1)}, u32[]{:S(2)}, u32[]{:S(2)}) collective-permute-start(f32[4,16,480]{2,1,0:T(8,128)S(1)} %get-tuple-element.25), channel_id=1, source_target_pairs={{0,0},{1,65},{2,2},{3,67},{4,4},{5,69},{6,6},{7,71},{8,8},{9,73},{... | collective-permute-start | bytes 368648 | tf_op jit(solution)/shard_map/ppermute | solution.py:26
  82.0 19.3 %collective-permute-start.15 = (f32[4,16,480]{2,1,0:T(8,128)S(1)}, f32[4,16,480]{2,1,0:T(8,128)S(1)}, u32[]{:S(2)}, u32[]{:S(2)}) collective-permute-start(f32[4,16,480]{2,1,0:T(8,128)S(1)} %get-tuple-element.26), channel_id=1, source_target_pairs={{0,897},{1,960},{2,899},{3,962},{4,901},{5,964},{6,903},{7,966},{8... | collective-permute-start | bytes 368648 | tf_op jit(solution)/shard_map/ppermute | solution.py:26
  97.9 7.7 %collective-permute-start.16 = (f32[4,16,480]{2,1,0:T(8,128)S(1)}, f32[4,16,480]{2,1,0:T(8,128)S(1)}, u32[]{:S(2)}, u32[]{:S(2)}) collective-permute-start(f32[4,16,480]{2,1,0:T(8,128)S(1)} %get-tuple-element.28), channel_id=1, source_target_pairs={{0,896},{1,961},{2,898},{3,963},{4,900},{5,965},{6,902},{7,967},{8... | collective-permute-start | bytes 368648 | tf_op jit(solution)/shard_map/ppermute | solution.py:26
  106.3 19.0 %all-to-all-start = ((f32[4,16,480]{2,1,0:T(8,128)}), f32[4,16,480]{2,1,0:T(8,128)S(1)}, u32[]{:S(2)}, u32[]{:S(2)}) async-start(f32[4,16,480]{2,1,0:T(8,128)} %add_add_fusion.1), calls=%async_computation | async-start | bytes 262144 | tf_op jit(solution)/shard_map/all_to_all | solution.py:123
